TPU v7x, 32 devices: a whole 2x2x4 slice. The times are simulated.
32 devices in a mesh: rows: 4 (over z), cols: 8 (over y, x, core).
Axes of the slice: x: 2, y: 2, z: 4, core: 2. Of those that a mesh axis runs over, the one named last changes fastest.
Arguments:
- fields: float32 [5, 64, 256, 512], P(None, None, 'cols', 'rows'), may hold values from -6 to 6
- cotangent: float32 [5, 64, 256, 512], P(None, None, 'cols', 'rows'), may hold values from -6 to 6
- ocean_mask: int32 [256, 512], P('cols', 'rows'), may hold values from 0 to 1
- depth_levels: int32 [256, 512], P('cols', 'rows'), may hold values from 16 to 64
- in_weight: bfloat16 [256, 256], replicated, may hold values from -0.375 to 0.375
- in_bias: float32 [256], replicated, may hold values from -3 to 3
- out_weight: bfloat16 [256, 63], replicated, may hold values from -0.375 to 0.375
Outputs:
- new_fields: float32 [5, 64, 256, 512], P(None, None, 'cols', 'rows')
- pressure: float32 [64, 256, 512], P(None, 'cols', 'rows')
- grad_in_weight: float32 [256, 256], replicated
- grad_in_bias: float32 [256], replicated
- grad_out_weight: float32 [256, 63], replicated
All inputs are finite; a program needn't handle non-finite values.
Results may differ from a plain program's by a relative error of at most 0.0059.
Values sent between devices are 32-bit elements; how exact they have to be, the bound alone decides.
No kernel may reach another device: no remote copies, remote signals or barrier semaphores. Data moves between devices by JAX's collectives and lax.ppermute only.
A program may use at most 192 MiB of HBM per device.

v0:
```python
import functools

import jax
import jax.numpy as jnp
import numpy as np
from jax import lax
from jax.experimental import pallas as pl
from jax.experimental.pallas import tpu as pltpu
from jax.sharding import PartitionSpec as P

TIME_STEP = 0.2
RATE_MAX = 2.0
THERMAL = 0.5
HALINE = 0.5
SPECTRAL_SHIFT = 0.001
WENO_EPS = 1e-06
HALO = 3
FIELDS = 5
SUB = 8


def pack_kernel(dep_ref, fields_ref, xfirst_ref, xlast_ref, yfirst_ref, ylast_ref):
    field = pl.program_id(0)
    north, east = dep_ref.shape
    levels = fields_ref.shape[1] // north
    per = east // north
    blocks = levels // per
    dep = dep_ref[...]
    tiled = jnp.concatenate([dep] * per, 0)
    level_in_block = lax.broadcasted_iota(jnp.int32, (east, east), 0) // north
    for t in range(blocks):
        block = fields_ref[0, t * east : (t + 1) * east, :]
        masked = jnp.where(level_in_block + t * per < tiled, block, 0.0)
        turned = masked.T
        row = field * blocks + t
        for s in range(HALO):
            xfirst_ref[s, pl.ds(row, 1), :] = turned[s : s + 1]
            xlast_ref[s, pl.ds(row, 1), :] = turned[east - HALO + s : east - HALO + s + 1]
    level = lax.broadcasted_iota(jnp.int32, (levels, east), 0)
    for s in range(HALO):
        at = pl.multiple_of((field * HALO + s) * levels, SUB)
        low, high = s, north - HALO + s
        first = fields_ref[0, pl.ds(low, levels, stride=north), :]
        last = fields_ref[0, pl.ds(high, levels, stride=north), :]
        yfirst_ref[pl.ds(at, levels), :] = jnp.where(level < dep[low : low + 1], first, 0.0)
        ylast_ref[pl.ds(at, levels), :] = jnp.where(level < dep[high : high + 1], last, 0.0)

    @pl.when(field == 0)
    def _():
        depths = dep.astype(jnp.float32)
        end = FIELDS * HALO * levels
        yfirst_ref[end:, :] = jnp.broadcast_to(depths[:1], (SUB, east))
        ylast_ref[end:, :] = jnp.broadcast_to(depths[north - 1 :], (SUB, east))
        turned = tiled.astype(jnp.float32).T
        for s in range(HALO):
            high = east - HALO + s
            xfirst_ref[s, FIELDS * blocks :, :] = jnp.broadcast_to(turned[s : s + 1], (SUB, east))
            xlast_ref[s, FIELDS * blocks :, :] = jnp.broadcast_to(
                turned[high : high + 1], (SUB, east)
            )


def pack_edges(fields, dep):
    _, levels, north, east = fields.shape
    rows = FIELDS * levels * north // east + SUB
    x_shape = jax.ShapeDtypeStruct((HALO, rows, east), jnp.float32)
    y_shape = jax.ShapeDtypeStruct((FIELDS * HALO * levels + SUB, east), jnp.float32)
    whole = lambda shape: pl.BlockSpec(shape.shape, lambda f: (0,) * len(shape.shape))
    return pl.pallas_call(
        pack_kernel,
        grid=(FIELDS,),
        in_specs=[
            pl.BlockSpec((north, east), lambda f: (0, 0)),
            pl.BlockSpec((1, levels * north, east), lambda f: (f, 0, 0)),
        ],
        out_specs=[whole(x_shape), whole(x_shape), whole(y_shape), whole(y_shape)],
        out_shape=[x_shape, x_shape, y_shape, y_shape],
        compiler_params=pltpu.CompilerParams(vmem_limit_bytes=32 << 20),
    )(dep, fields.reshape(FIELDS, levels * north, east))


def face_flux(slopes, left, right, speed, share):
    dm2, dm1, d0, dp1, dp2 = slopes
    ahead = speed > 0.0
    e1 = jnp.where(ahead, dm2, dp2)
    e2 = jnp.where(ahead, dm1, dp1)
    e4 = jnp.where(ahead, dp1, dm1)
    near = jnp.where(ahead, left, right)
    bend0, bend1, bend2 = e2 - e1, d0 - e2, e4 - d0
    twice2, twice3 = e2 + e2, d0 + d0
    tilt0, tilt1, tilt2 = bend0 + twice2, e2 + d0, bend2 - twice3
    rough0 = bend0 * bend0 * (13.0 / 3.0) + (tilt0 * tilt0 + 4.0 * WENO_EPS)
    rough1 = bend1 * bend1 * (13.0 / 3.0) + (tilt1 * tilt1 + 4.0 * WENO_EPS)
    rough2 = bend2 * bend2 * (13.0 / 3.0) + (tilt2 * tilt2 + 4.0 * WENO_EPS)
    pair0, pair1, pair2 = rough1 * rough2, rough0 * rough2, rough0 * rough1
    g0, g1, g2 = pair0 * pair0, 6.0 * (pair1 * pair1), 3.0 * (pair2 * pair2)
    total = g0 * (5.0 * e2 - (e1 + e1)) + g1 * (e2 + twice3) + g2 * (4.0 * d0 - e4)
    return speed * near + share * (total * pltpu.reciprocal(g0 + g1 + g2, approx=True))


def advect_kernel(
    dep_ref, fields_ref, xlo_ref, xhi_ref, ylo_ref, yhi_ref,
    adv_ref, spread_ref, wm_ref,
    deep, both, lines, slopes, fluxes, cells, wets, su, su6, sv, sv6, sides,
):
    step = pl.program_id(0)
    north, east = dep_ref.shape
    per = east // north
    blocks = SUB // per
    all_blocks = (xlo_ref.shape[1] - SUB) // FIELDS
    levels = all_blocks * per
    depth_row = FIELDS * all_blocks
    depth_end = FIELDS * HALO * levels
    faces = range(0, east + SUB, SUB)
    first_level = step * SUB

    @pl.when(step == 0)
    def _():
        depths = dep_ref[...].astype(jnp.float32)
        deep[SUB : SUB + east, :] = jnp.concatenate([depths] * per, 0).T
        deep[SUB - 1 : SUB, :] = xlo_ref[HALO - 1, depth_row : depth_row + 1, :]
        deep[SUB + east : SUB + east + 1, :] = xhi_ref[0, depth_row : depth_row + 1, :]
        both[:east, :] = jnp.minimum(deep[SUB - 1 : SUB - 1 + east, :], deep[SUB : SUB + east, :])
        both[east : east + 1, :] = jnp.minimum(
            deep[SUB + east - 1 : SUB + east, :], deep[SUB + east : SUB + east + 1, :]
        )

    level = (lax.broadcasted_iota(jnp.int32, (SUB, east), 0) + first_level).astype(jnp.float32)
    side_level = lax.broadcasted_iota(jnp.int32, (SUB, east), 1) // north + first_level
    depths = dep_ref[...].astype(jnp.float32)
    wets[0] = (level < ylo_ref[depth_end : depth_end + 1, :]).astype(jnp.float32)
    wets[north + 1] = (level < yhi_ref[depth_end : depth_end + 1, :]).astype(jnp.float32)
    for y in range(north):
        wets[y + 1] = (level < depths[y : y + 1]).astype(jnp.float32)

    def stage(f, carry):
        for s in range(HALO):
            at = pl.multiple_of((f * HALO + s) * levels + first_level, SUB)
            cells[f, s] = ylo_ref[pl.ds(at, SUB), :]
            cells[f, north + HALO + s] = yhi_ref[pl.ds(at, SUB), :]
        for y in range(north):
            cells[f, y + HALO] = fields_ref[f, pl.ds(y, SUB, stride=north), :] * wets[y + 1]
        for b in range(blocks):
            row = f * all_blocks + step * blocks + b
            for s in range(HALO):
                lines[f, b, SUB - HALO + s : SUB - HALO + s + 1, :] = xlo_ref[s, pl.ds(row, 1), :]
                lines[f, b, SUB + east + s : SUB + east + s + 1, :] = xhi_ref[s, pl.ds(row, 1), :]
            turned = fields_ref[f, b * east : (b + 1) * east, :].T
            height = (side_level + b * per).astype(jnp.float32)
            for r in range(0, east, SUB):
                wet = height < deep[SUB + r : 2 * SUB + r, :]
                lines[f, b, SUB + r : 2 * SUB + r, :] = jnp.where(wet, turned[r : r + SUB], 0.0)
        return carry

    lax.fori_loop(0, FIELDS, stage, 0)

    for b in range(blocks):
        height = (side_level + b * per).astype(jnp.float32)
        for r in faces:
            speed = (0.5 * TIME_STEP) * (
                lines[0, b, SUB + r - 1 : 2 * SUB + r - 1, :] + lines[0, b, SUB + r : 2 * SUB + r, :]
            )
            speed = jnp.where(height < both[r : r + SUB, :], speed, 0.0)
            su[b, r : r + SUB, :] = speed
            su6[b, r : r + SUB, :] = jnp.abs(speed) * (1.0 / 6.0)
        change = 0.5 * (
            lines[0, b, SUB + 1 : SUB + 1 + east, :] - lines[0, b, SUB - 1 : SUB - 1 + east, :]
        )
        sides[b * east : (b + 1) * east, :] = change.T
    for y in range(north):
        spread_ref[y] = sides[pl.ds(y, SUB, stride=north), :] + 0.5 * (
            cells[1, y + HALO + 1] - cells[1, y + HALO - 1]
        )
        wm_ref[y] = cells[2, y + HALO]
    for y in range(north + 1):
        speed = (0.5 * TIME_STEP) * (cells[1, y + HALO - 1] + cells[1, y + HALO])
        speed = speed * (wets[y] * wets[y + 1])
        sv[y] = speed
        sv6[y] = jnp.abs(speed) * (1.0 / 6.0)

    def advance_field(f, carry):
        for b in range(blocks):
            for r in range(0, east + 2 * SUB, SUB):
                ahead = lines[f, b, r + 1 : r + 1 + SUB, :]
                slopes[b, r : r + SUB, :] = ahead - lines[f, b, r : r + SUB, :]
            for r in faces:
                at = SUB + r
                near = [slopes[b, at + k : at + k + SUB, :] for k in (-3, -2, -1, 0, 1)]
                fluxes[b, r : r + SUB, :] = face_flux(
                    near,
                    lines[f, b, at - 1 : at - 1 + SUB, :],
                    lines[f, b, at : at + SUB, :],
                    su[b, r : r + SUB, :],
                    su6[b, r : r + SUB, :],
                )
            change = fluxes[b, 0:east, :] - fluxes[b, 1 : 1 + east, :]
            sides[b * east : (b + 1) * east, :] = change.T
        line = [cells[f, k] for k in range(5)]
        inclines = [line[k + 1] - line[k] for k in range(4)]
        south = None
        for y in range(north + 1):
            line.append(cells[f, y + 2 * HALO - 1])
            inclines.append(line[-1] - line[-2])
            north_face = face_flux(inclines[-5:], line[-4], line[-3], sv[y], sv6[y])
            if y > 0:
                change = sides[pl.ds(y - 1, SUB, stride=north), :] + (south - north_face)
                adv_ref[f, y - 1] = wets[y] * (line[-4] + change)
            south = north_face
        return carry

    lax.fori_loop(0, FIELDS, advance_field, 0)


def advect(fields, dep, xlo, xhi, ylo, yhi):
    _, levels, north, east = fields.shape
    whole = lambda a: pl.BlockSpec(a.shape, lambda k: (0,) * a.ndim)
    plane = pl.BlockSpec((north, SUB, east), lambda k: (0, k, 0))
    f32 = jnp.float32
    one = jax.ShapeDtypeStruct((north, levels, east), f32)
    blocks = SUB * north // east
    return pl.pallas_call(
        advect_kernel,
        grid=(levels // SUB,),
        in_specs=[
            whole(dep),
            pl.BlockSpec((FIELDS, SUB * north, east), lambda k: (0, k, 0)),
            whole(xlo), whole(xhi), whole(ylo), whole(yhi),
        ],
        out_specs=[
            pl.BlockSpec((FIELDS, north, SUB, east), lambda k: (0, 0, k, 0)), plane, plane,
        ],
        out_shape=[jax.ShapeDtypeStruct((FIELDS, north, levels, east), f32), one, one],
        scratch_shapes=[
            pltpu.VMEM((east + 2 * SUB, east), f32),
            pltpu.VMEM((east + SUB, east), f32),
            pltpu.VMEM((FIELDS, blocks, east + 3 * SUB, east), f32),
            pltpu.VMEM((blocks, east + 3 * SUB, east), f32),
            pltpu.VMEM((blocks, east + SUB, east), f32),
            pltpu.VMEM((FIELDS, north + 2 * HALO, SUB, east), f32),
            pltpu.VMEM((north + 2, SUB, east), f32),
            pltpu.VMEM((blocks, east + SUB, east), f32),
            pltpu.VMEM((blocks, east + SUB, east), f32),
            pltpu.VMEM((north + 1, SUB, east), f32),
            pltpu.VMEM((north + 1, SUB, east), f32),
            pltpu.VMEM((SUB * north, east), f32),
        ],
        compiler_params=pltpu.CompilerParams(vmem_limit_bytes=40 << 20),
        cost_estimate=pl.CostEstimate(
            flops=int(fields.size) * 130, bytes_accessed=2 * 4 * int(fields.size), transcendentals=0
        ),
    )(dep, fields.reshape(FIELDS, levels * north, east), xlo, xhi, ylo, yhi)


def shift_both(block, axis, first, last):
    count = lax.axis_size(axis)
    forward = [(i, i + 1) for i in range(count - 1)]
    backward = [(i + 1, i) for i in range(count - 1)]
    return lax.ppermute(last, axis, forward), lax.ppermute(first, axis, backward)


def advance_block(fields, dep):
    xfirst, xlast, yfirst, ylast = pack_edges(fields, dep)
    ylo, yhi = shift_both(None, "cols", yfirst, ylast)
    xlo, xhi = shift_both(None, "rows", xfirst, xlast)
    return advect(fields, dep, xlo, xhi, ylo, yhi)


AXES = ("rows", "cols")
VMEM_LIMIT = 48 << 20
TRACERS = (0, 1, 3, 4)
PARTS = 4


def dct_table(length):
    freq = np.arange(length)[:, None]
    cells = np.arange(length)[None, :]
    scale = np.where(freq == 0, np.sqrt(1.0 / length), np.sqrt(2.0 / length))
    return scale * np.cos(np.pi * (cells + 0.5) * freq / length)


def eigen_table(length):
    return 2.0 - 2.0 * np.cos(np.pi * np.arange(length) / length)


def halves(table):
    high = table.astype(jnp.bfloat16)
    low = (table - high.astype(np.float64)).astype(jnp.bfloat16)
    return high, low


def right_factor(table):
    high, low = halves(table)
    return np.block([[high, low], [high, np.zeros_like(low)]])


def left_factor(table):
    high, low = halves(table)
    return np.concatenate([high, low], 0)


class Tables:
    def __init__(self, levels, north, east, rows, cols):
        self.levels, self.north, self.east, self.rows, self.cols = levels, north, east, rows, cols
        self.count = rows * cols
        self.share = -(-levels // self.count)
        padded = self.share * self.count
        cz, cy, cx = dct_table(levels), dct_table(north), dct_table(east)
        lz, ly, lx = eigen_table(levels), eigen_table(north), eigen_table(east)
        shift = SPECTRAL_SHIFT + lz
        f32 = np.float32
        eye = np.eye(SUB)
        self.ly = [float(v) for v in ly]
        self.south = [float(v) for v in cy[:, 0]]
        self.north_edge = [float(v) for v in cy[:, -1]]
        self.base = (shift[:, None] + lx[None]).astype(f32)
        self.z_forward, self.z_back = left_factor(cz), left_factor(cz.T)
        self.y_forward = left_factor(np.kron(cy, eye))
        self.y_back = left_factor(np.kron(cy.T, eye))
        self.x_forward, self.x_back = right_factor(cx.T), right_factor(cx)
        take = np.zeros((north, east, 2 * north))
        give = np.zeros((2 * north, north, east))
        for k in range(north):
            take[k, :, k], take[k, :, north + k] = cx[:, 0], cx[:, -1]
            give[k, k], give[north + k, k] = -cx[:, -1], cx[:, 0]
        self.take = np.concatenate(halves(take.reshape(north * east, 2 * north)), 1)
        self.give = np.concatenate(halves(give.reshape(2 * north, north * east)), 0)
        lanes = max(east, 2 * north)
        assert lanes == east and cols % SUB == 0
        grid = 1.0 / (shift[:, None, None] + ly[None, :, None] + lx[None, None, :])
        alpha = np.einsum("k,myk->my", cx[:, -1] ** 2, grid)
        beta = np.einsum("k,myk->my", cx[:, -1] * cx[:, 0], grid)
        inner = rows - 1
        near = np.eye(inner, k=1) + np.eye(inner, k=-1)
        system = (1.0 + 2.0 * alpha)[..., None, None] * np.eye(inner) - beta[
            ..., None, None
        ] * near
        inverse = np.linalg.inv(system).transpose(0, 2, 3, 1).reshape(levels, inner**2, north)
        cross = np.zeros((padded, inner**2 + 1, east), f32)
        cross[:levels, : inner**2, :north] = inverse
        cross[:, inner**2] = 1.0
        cross[:levels, inner**2] = shift[:, None]
        self.cross = cross
        all_east = eigen_table(rows * east)
        grid = 1.0 / (shift[:, None, None] + ly[None, :, None] + all_east[None, None, :])
        alpha = np.einsum("y,myk->mk", cy[:, -1] ** 2, grid)
        beta = np.einsum("y,myk->mk", cy[:, -1] * cy[:, 0], grid)
        waves = np.cos(np.pi * np.arange(1, cols) / cols)
        along = np.zeros((padded, cols, rows * east), f32)
        along[:levels, : cols - 1] = 1.0 / (
            1.0 + 2.0 * alpha[:, None] - 2.0 * beta[:, None] * waves[None, :, None]
        )
        self.along = along
        order = np.arange(1, cols)
        sines = np.zeros((cols, cols))
        sines[: cols - 1, : cols - 1] = np.sqrt(2.0 / cols) * np.sin(
            np.pi * np.outer(order, order) / cols
        )
        self.sines = np.kron(np.eye(self.share), sines).astype(f32)
        wide = dct_table(rows * east).reshape(rows * east, rows, east)
        turn = np.einsum("gax,kx->gak", wide, cx).reshape(rows * east, rows * east)
        self.wide_forward = np.stack(halves(turn.T))
        self.wide_back = np.stack(halves(turn))
        both = (ly[:, None] + lx[None]).astype(f32)
        self.strip = np.stack(
            [both, np.broadcast_to(cy[:, -1:], both.shape), np.broadcast_to(cy[:, :1], both.shape)]
        ).astype(f32)
        back = np.full((east, east), 1.0)
        gain = np.zeros((east, east))
        back[:, :north] = back[:, north : 2 * north] = both.T
        gain[:, :north], gain[:, north : 2 * north] = cx[:, -1:], cx[:, :1]
        self.column = np.stack([back, gain]).astype(f32)
        lines = np.zeros((SUB, east), f32)
        lines[0], lines[1] = cx[:, -1], cx[:, 0]
        lines[2, :north] = lines[2, north : 2 * north] = cy[:, -1]
        lines[3, :north] = lines[3, north : 2 * north] = cy[:, 0]
        self.lines = lines


def parts(value):
    high = value.astype(jnp.bfloat16)
    return high, (value - high.astype(jnp.float32)).astype(jnp.bfloat16)


def mul(a, b):
    return jnp.dot(a, b, preferred_element_type=jnp.float32)


def from_left(factor, value):
    rows = factor.shape[0] // 2
    high, low = parts(value)
    both = mul(factor, high)
    return both[:rows] + (both[rows:] + mul(factor[:rows], low))


def from_right(value, factor):
    columns = factor.shape[1] // 2
    both = mul(jnp.concatenate(parts(value), 1), factor)
    return both[:, :columns] + both[:, columns:]


def times(value, high, low):
    first, second = parts(value)
    return mul(first, high) + (mul(second, high) + mul(first, low))


def vertical_change(value):
    levels = value.shape[0]
    level = lax.broadcasted_iota(jnp.int32, value.shape, 0)
    above = jnp.where(level == levels - 1, 0.0, pltpu.roll(value, levels - 1, 0))
    below = jnp.where(level == 0, 0.0, pltpu.roll(value, 1, 0))
    return 0.5 * (above - below)


def local_solve(tables, spec, base_ref, x_ref, y_ref, take_ref, coef_ref, edge_ref):
    north, east, levels = tables.north, tables.east, tables.levels
    for y in range(0, north, 4):
        tile = spec[y : y + 4].reshape(4 * levels, east)
        spec[y : y + 4] = from_right(tile, x_ref[...]).reshape(4, levels, east)
    for m in range(0, levels, SUB):
        tile = from_left(y_ref[...], spec[:, m : m + SUB, :].reshape(north * SUB, east))
        base = base_ref[m : m + SUB, :]
        even = odd = jnp.zeros((SUB, east), jnp.float32)
        for k in range(north):
            value = tile[k * SUB : (k + 1) * SUB] / (base + tables.ly[k])
            coef_ref[k, m : m + SUB, :] = value
            if k % 2:
                odd = odd + tables.south[k] * value
            else:
                even = even + tables.south[k] * value
        edge_ref[pl.ds(PARTS * m + 1, SUB, stride=PARTS), :] = even + odd
        edge_ref[pl.ds(PARTS * m + 2, SUB, stride=PARTS), :] = even - odd
    total = jnp.zeros((levels, east), jnp.float32)
    rest = total
    for k in range(north):
        high, low = parts(coef_ref[k])
        factor = take_ref[k * east : (k + 1) * east, :]
        total = total + mul(high, factor)
        rest = rest + mul(low, factor)
    lane = lax.broadcasted_iota(jnp.int32, total.shape, 1)
    total = total + pltpu.roll(total, east // 2, 1) + rest
    edge_ref[pl.ds(0, levels, stride=PARTS), :] = jnp.where(lane < 2 * north, total, 0.0)
    edge_ref[pl.ds(PARTS - 1, levels, stride=PARTS), :] = jnp.zeros_like(total)
    if edge_ref.shape[0] > levels * PARTS:
        edge_ref[levels * PARTS :, :] = jnp.zeros_like(edge_ref[levels * PARTS :, :])


def finish_solve(tables, spec, coef_ref, jump_ref, base_ref, y_ref, x_ref, z_ref, give_ref, use):
    north, east, levels = tables.north, tables.east, tables.levels
    side, ahead, behind = (
        jump_ref[pl.ds(part, levels, stride=PARTS), :] for part in range(PARTS - 1)
    )
    both = side + pltpu.roll(side, east // 2, 1)
    side_high, side_low = parts(side)
    both = both.astype(jnp.bfloat16)
    half = 2 * north
    for k in range(north):
        lanes = slice(k * east, (k + 1) * east)
        change = mul(both, give_ref[:, lanes]) + mul(side_low[:, :half], give_ref[:half, lanes])
        change = change + (tables.south[k] * behind - tables.north_edge[k] * ahead)
        spec[k] = coef_ref[k] + change / (base_ref[...] + tables.ly[k])
    for m in range(0, levels, SUB):
        tile = from_left(y_ref[...], spec[:, m : m + SUB, :].reshape(north * SUB, east))
        spec[:, m : m + SUB, :] = tile.reshape(north, SUB, east)
    for y in range(0, north, 4):
        tile = from_right(spec[y : y + 4].reshape(4 * levels, east), x_ref[...])
        tile = jnp.concatenate([tile[k * levels : (k + 1) * levels] for k in range(4)], 1)
        tile = from_left(z_ref[...], tile)
        for k in range(4):
            use(y + k, tile[:, k * east : (k + 1) * east])


def interface_kernel(
    tables, edge_ref, cross_ref, along_ref, sines_ref, forward_ref, back_ref,
    strip_ref, column_ref, lines_ref, jump_ref,
):
    rows, cols, east, north = tables.rows, tables.cols, tables.east, tables.north
    share, inner = tables.share, tables.rows - 1
    f32 = jnp.float32
    east_last, east_first = lines_ref[0:1, :], lines_ref[1:2, :]
    north_last, north_first = lines_ref[2:3, :], lines_ref[3:4, :]
    every = lax.Precision.HIGHEST

    def across(m, changes):
        result = []
        for i in range(inner):
            total = jnp.zeros((cols, east), f32)
            for j in range(inner):
                at = i * inner + j
                total = total + cross_ref[m, at : at + 1, :] * changes[j]
            result.append(total)
        return result

    gaps, steps = [], []
    for m in range(share):
        west, south, top = (
            [
                edge_ref[pl.ds((a * cols * share + m) * PARTS + part, cols, stride=share * PARTS), :]
                for a in range(rows)
            ]
            for part in range(PARTS - 1)
        )
        right = [pltpu.roll(tile, east - north, 1) for tile in west]
        gap = [right[i] - west[i + 1] for i in range(inner)]
        gaps.append(gap)
        jumps = jnp.concatenate(across(m, gap), 0)
        shift = cross_ref[m, inner**2 : inner**2 + 1, :]
        inverse = 1.0 / (strip_ref[0] + shift)
        weights = jnp.concatenate([strip_ref[1] * inverse, strip_ref[2] * inverse], 1)
        weights = jnp.concatenate([weights, jnp.zeros((east - north, 2 * east), f32)], 0)
        moved = times(jumps, *parts(weights))
        for a in range(rows):
            for side, at in ((top, 0), (south, east)):
                if a < inner:
                    side[a] = side[a] - east_last * moved[a * cols : (a + 1) * cols, at : at + east]
                if a > 0:
                    side[a] = side[a] + east_first * moved[
                        (a - 1) * cols : a * cols, at : at + east
                    ]
        steps.append(
            jnp.concatenate([top[a] - pltpu.roll(south[a], cols - 1, 0) for a in range(rows)], 1)
        )
    step = jnp.concatenate(steps, 0)
    waves = times(step, forward_ref[0], forward_ref[1])
    waves = jnp.dot(sines_ref[...], waves, precision=every, preferred_element_type=f32)
    waves = waves * jnp.concatenate([along_ref[m] for m in range(share)], 0)
    waves = jnp.dot(sines_ref[...], waves, precision=every, preferred_element_type=f32)
    step = times(waves, back_ref[0], back_ref[1])
    for m in range(share):
        shift = cross_ref[m, inner**2 : inner**2 + 1, :]
        here = step[m * cols : (m + 1) * cols]
        tall = [here[:, a * east : (a + 1) * east] for a in range(rows)]
        weights = column_ref[1] / (column_ref[0] + shift)
        moved = times(jnp.concatenate(tall, 0), *parts(weights))
        sides = []
        for a in range(rows):
            tile = moved[a * cols : (a + 1) * cols]
            sides.append(north_last * tile - north_first * pltpu.roll(tile, 1, 0))
        gap = [
            gaps[m][i] - (sides[i] - pltpu.roll(sides[i + 1], east - north, 1))
            for i in range(inner)
        ]
        jumps = across(m, gap)
        for a in range(rows):
            tile = jnp.zeros((cols, east), f32)
            if a < inner:
                tile = tile + jumps[a]
            if a > 0:
                tile = tile + pltpu.roll(jumps[a - 1], north, 1)
            out = (tile, tall[a], pltpu.roll(tall[a], 1, 0), jnp.zeros_like(tile))
            for part in range(PARTS):
                at = (a * cols * share + m) * PARTS + part
                jump_ref[pl.ds(at, cols, stride=share * PARTS), :] = out[part]


def whole_spec(array):
    shape = tuple(array.shape)
    return pl.BlockSpec(shape, lambda *_: (0,) * len(shape))


def call_params():
    return pltpu.CompilerParams(vmem_limit_bytes=VMEM_LIMIT)


def exchange(block):
    return lax.all_to_all(block, AXES, split_axis=0, concat_axis=0, tiled=True)


def interface(tables, edges):
    received = exchange(edges)
    device = lax.axis_index("rows") * lax.axis_size("cols") + lax.axis_index("cols")
    cross = lax.dynamic_slice_in_dim(tables.cross, device * tables.share, tables.share, 0)
    along = lax.dynamic_slice_in_dim(tables.along, device * tables.share, tables.share, 0)
    operands = (
        received, cross, along, tables.sines, tables.wide_forward, tables.wide_back,
        tables.strip, tables.column, tables.lines,
    )
    jumps = pl.pallas_call(
        functools.partial(interface_kernel, tables),
        in_specs=[whole_spec(a) for a in operands],
        out_specs=whole_spec(received),
        out_shape=jax.ShapeDtypeStruct(received.shape, jnp.float32),
        grid=(1,),
        compiler_params=call_params(),
    )(*operands)
    return exchange(jumps)


def adjoint_kernel(
    tables, dep_ref, cot_ref, z_ref, base_ref, x_ref, y_ref, take_ref, coef_ref, edge_ref, spec
):
    north, east, levels = tables.north, tables.east, tables.levels
    level = lax.broadcasted_iota(jnp.int32, (levels, east), 0)
    for y in range(0, north, 4):
        tiles = []
        for k in range(y, y + 4):
            value = cot_ref[0, pl.ds(k, levels, stride=north), :]
            value = jnp.where(level < dep_ref[k : k + 1, :], value, 0.0)
            tiles.append(TIME_STEP * vertical_change(value))
        tile = from_left(z_ref[...], jnp.concatenate(tiles, 1))
        for k in range(4):
            spec[y + k] = tile[:, k * east : (k + 1) * east]
    local_solve(tables, spec, base_ref, x_ref, y_ref, take_ref, coef_ref, edge_ref)


def solve_shapes(tables):
    coef = jax.ShapeDtypeStruct((tables.north, tables.levels, tables.east), jnp.float32)
    edge = jax.ShapeDtypeStruct((tables.share * tables.count * PARTS, tables.east), jnp.float32)
    return [coef, edge]


def adjoint_local(tables, cotangent, dep):
    levels, north, east = tables.levels, tables.north, tables.east
    consts = (tables.z_forward, tables.base, tables.x_forward, tables.y_forward, tables.take)
    shapes = solve_shapes(tables)
    return pl.pallas_call(
        functools.partial(adjoint_kernel, tables),
        grid=(1,),
        in_specs=[
            whole_spec(dep),
            pl.BlockSpec((1, levels * north, east), lambda k: (2, 0, 0)),
            *(whole_spec(a) for a in consts),
        ],
        out_specs=[whole_spec(a) for a in shapes],
        out_shape=shapes,
        scratch_shapes=[pltpu.VMEM(shapes[0].shape, jnp.float32)],
        compiler_params=call_params(),
    )(dep, cotangent.reshape(FIELDS, levels * north, east), *consts)


def closure(feats, w_in, bias, w_out):
    activity = jnp.tanh(mul(w_in, feats) + bias)
    hidden = activity.astype(jnp.bfloat16)
    return activity, hidden, RATE_MAX * jax.nn.sigmoid(mul(w_out, hidden))


def column_kernel(
    tables, dep_ref, adv_ref, spread_ref, wm_ref, w_in_ref, bias_ref, w_out_ref,
    z_ref, base_ref, x_ref, y_ref, take_ref,
    new_ref, coef_ref, edge_ref, spec, feats, flat,
):
    step = pl.program_id(0)
    north, east, levels = tables.north, tables.east, tables.levels
    for k in range(SUB):
        for i, f in enumerate(TRACERS):
            feats[i * levels : (i + 1) * levels, k * east : (k + 1) * east] = adv_ref[f, k].astype(
                jnp.bfloat16
            )
    _, _, rates = closure(feats[...], w_in_ref[...], bias_ref[...], w_out_ref[...])
    level = lax.broadcasted_iota(jnp.int32, (levels, east), 0)
    depths = dep_ref[pl.ds(pl.multiple_of(step * SUB, SUB), SUB), :]
    sources = []
    for k in range(SUB):
        depth = depths[k : k + 1]
        wet = level < depth
        bond = jnp.where(level + 1 < depth, TIME_STEP, 0.0)
        flow = bond * rates[:, k * east : (k + 1) * east]
        mixed = []
        for f in (3, 4):
            value = adv_ref[f, k]
            flux = flow * (pltpu.roll(value, levels - 1, 0) - value)
            value = jnp.where(wet, value + (flux - pltpu.roll(flux, 1, 0)), 0.0)
            mixed.append(value)
            flat[f, pl.ds(k, levels, stride=SUB), :] = value
        for f in (0, 1):
            flat[f, pl.ds(k, levels, stride=SUB), :] = adv_ref[f, k]
        density = THERMAL * mixed[0] - HALINE * mixed[1] - wm_ref[k] * (1.0 / TIME_STEP)
        source = vertical_change(density) - spread_ref[k] * (1.0 / TIME_STEP)
        sources.append(jnp.where(wet, source, 0.0))
    tile = from_left(z_ref[...], jnp.concatenate(sources, 1))
    for k in range(SUB):
        spec[step * SUB + k] = tile[:, k * east : (k + 1) * east]
    for f in TRACERS:
        new_ref[f] = flat[f].reshape(levels, SUB, east)

    @pl.when(step == north // SUB - 1)
    def _():
        local_solve(tables, spec, base_ref, x_ref, y_ref, take_ref, coef_ref, edge_ref)


def column(tables, dep, adv, spread, wm, w_in, bias, w_out):
    levels, north, east = tables.levels, tables.north, tables.east
    tall = lambda n: pl.BlockSpec((n, SUB, levels, east), lambda k: (0, k, 0, 0))
    plane = pl.BlockSpec((SUB, levels, east), lambda k: (k, 0, 0))
    consts = (
        w_in, bias, w_out,
        tables.z_forward, tables.base, tables.x_forward, tables.y_forward, tables.take,
    )
    shapes = solve_shapes(tables)
    return pl.pallas_call(
        functools.partial(column_kernel, tables),
        grid=(north // SUB,),
        in_specs=[whole_spec(dep), tall(FIELDS), plane, plane, *(whole_spec(a) for a in consts)],
        out_specs=[
            pl.BlockSpec((FIELDS, levels, SUB, east), lambda k: (0, 0, k, 0)),
            *(whole_spec(a) for a in shapes),
        ],
        out_shape=[jax.ShapeDtypeStruct((FIELDS, levels, north, east), jnp.float32), *shapes],
        scratch_shapes=[
            pltpu.VMEM(shapes[0].shape, jnp.float32),
            pltpu.VMEM((len(TRACERS) * levels, SUB * east), jnp.bfloat16),
            pltpu.VMEM((FIELDS, levels * SUB, east), jnp.float32),
        ],
        compiler_params=call_params(),
    )(dep, adv, spread, wm, *consts)


def back_kernel(
    tables, coef_ref, jump_ref, base_ref, y_ref, x_ref, z_ref, give_ref, back_ref, spec
):
    def use(y, tile):
        back_ref[y] = tile

    finish_solve(
        tables, spec, coef_ref, jump_ref, base_ref, y_ref, x_ref, z_ref, give_ref, use
    )


def solve_consts(tables):
    return (tables.base, tables.y_back, tables.x_back, tables.z_back, tables.give)


def back_finish(tables, coef, jumps):
    operands = (coef, jumps, *solve_consts(tables))
    return pl.pallas_call(
        functools.partial(back_kernel, tables),
        grid=(1,),
        in_specs=[whole_spec(a) for a in operands],
        out_specs=whole_spec(coef),
        out_shape=jax.ShapeDtypeStruct(coef.shape, jnp.float32),
        scratch_shapes=[pltpu.VMEM(coef.shape, jnp.float32)],
        compiler_params=call_params(),
    )(*operands)


def pressure_kernel(
    tables, dep_ref, adv_ref, new_ref, coef_ref, jump_ref, base_ref, y_ref, x_ref, z_ref, give_ref,
    pressure_ref, out_ref, spec,
):
    north, east, levels = tables.north, tables.east, tables.levels
    level = lax.broadcasted_iota(jnp.int32, (levels, east), 0)

    def use(y, tile):
        pressure_ref[pl.ds(y, levels, stride=north), :] = tile
        value = adv_ref[0, y] - TIME_STEP * vertical_change(tile)
        value = jnp.where(level < dep_ref[y : y + 1, :], value, 0.0)
        out_ref[0, pl.ds(y, levels, stride=north), :] = value

    finish_solve(
        tables, spec, coef_ref, jump_ref, base_ref, y_ref, x_ref, z_ref, give_ref, use
    )


def pressure_finish(tables, dep, adv, new, coef, jumps):
    levels, north, east = tables.levels, tables.north, tables.east
    consts = solve_consts(tables)
    flat = jax.ShapeDtypeStruct((levels * north, east), jnp.float32)
    pressure, new = pl.pallas_call(
        functools.partial(pressure_kernel, tables),
        grid=(1,),
        in_specs=[
            whole_spec(dep),
            pl.BlockSpec((1, north, levels, east), lambda k: (2, 0, 0, 0)),
            pl.BlockSpec(memory_space=pl.ANY),
            whole_spec(coef),
            whole_spec(jumps),
            *(whole_spec(a) for a in consts),
        ],
        out_specs=[
            whole_spec(flat),
            pl.BlockSpec((1, levels * north, east), lambda k: (2, 0, 0)),
        ],
        out_shape=[flat, jax.ShapeDtypeStruct((FIELDS, levels * north, east), jnp.float32)],
        input_output_aliases={2: 1},
        scratch_shapes=[pltpu.VMEM(coef.shape, jnp.float32)],
        compiler_params=call_params(),
    )(dep, adv, new.reshape(FIELDS, levels * north, east), coef, jumps, *consts)
    return pressure.reshape(levels, north, east), new.reshape(FIELDS, levels, north, east)


def gradient_kernel(
    tables, dep_ref, adv_ref, back_ref, heat_ref, salt_ref, w_in_ref, bias_ref, w_out_ref, w_ref,
    g_in_ref, g_bias_ref, g_out_ref, feats, grads, flat,
):
    step = pl.program_id(0)
    east, levels = tables.east, tables.levels
    for k in range(SUB):
        for i, f in enumerate(TRACERS):
            feats[i * levels : (i + 1) * levels, k * east : (k + 1) * east] = adv_ref[f, k].astype(
                jnp.bfloat16
            )
    activity, hidden, rates = closure(feats[...], w_in_ref[...], bias_ref[...], w_out_ref[...])
    flat[0] = heat_ref[0].reshape(levels * SUB, east)
    flat[1] = salt_ref[0].reshape(levels * SUB, east)
    level = lax.broadcasted_iota(jnp.int32, (levels, east), 0)
    depths = dep_ref[pl.ds(pl.multiple_of(step * SUB, SUB), SUB), :]
    for k in range(SUB):
        depth = depths[k : k + 1]
        wet = level < depth
        density = -vertical_change(jnp.where(wet, back_ref[k], 0.0))
        total = jnp.zeros((levels, east), jnp.float32)
        for i, f, share in ((0, 3, THERMAL), (1, 4, -HALINE)):
            value = adv_ref[f, k]
            grad = flat[i, pl.ds(k, levels, stride=SUB), :] + share * density
            grad = jnp.where(wet, grad, 0.0)
            total = total + (grad - pltpu.roll(grad, levels - 1, 0)) * (
                pltpu.roll(value, levels - 1, 0) - value
            )
        total = jnp.where(level + 1 < depth, TIME_STEP * total, 0.0)
        rate = rates[:, k * east : (k + 1) * east]
        grads[:, k * east : (k + 1) * east] = (
            total * rate * (1.0 - rate * (1.0 / RATE_MAX))
        ).astype(jnp.bfloat16)
    over = (((1,), (1,)), ((), ()))
    grad = grads[...]
    g_out = lax.dot_general(hidden, grad, over, preferred_element_type=jnp.float32)
    pre = mul(w_ref[...], grad) * (1.0 - activity * activity)
    g_in = lax.dot_general(
        feats[...], pre.astype(jnp.bfloat16), over, preferred_element_type=jnp.float32
    )
    g_bias = pre[:, :east]
    for k in range(1, SUB):
        g_bias = g_bias + pre[:, k * east : (k + 1) * east]

    @pl.when(step == 0)
    def _():
        g_in_ref[...] = g_in
        g_out_ref[...] = g_out
        g_bias_ref[...] = g_bias

    @pl.when(step > 0)
    def _():
        g_in_ref[...] += g_in
        g_out_ref[...] += g_out
        g_bias_ref[...] += g_bias


def gradients(tables, dep, adv, back, cotangent, w_in, bias, w_out, w):
    levels, north, east = tables.levels, tables.north, tables.east
    hidden, inputs = w_in.shape
    f32 = jnp.float32
    shapes = [
        jax.ShapeDtypeStruct((inputs, hidden), f32),
        jax.ShapeDtypeStruct((hidden, east), f32),
        jax.ShapeDtypeStruct((hidden, levels), f32),
    ]
    field = lambda f: pl.BlockSpec((1, levels, SUB, east), lambda k: (f, 0, k, 0))
    consts = (w_in, bias, w_out, w)
    g_in, g_bias, g_out = pl.pallas_call(
        functools.partial(gradient_kernel, tables),
        grid=(north // SUB,),
        in_specs=[
            whole_spec(dep),
            pl.BlockSpec((FIELDS, SUB, levels, east), lambda k: (0, k, 0, 0)),
            pl.BlockSpec((SUB, levels, east), lambda k: (k, 0, 0)),
            field(3),
            field(4),
            *(whole_spec(a) for a in consts),
        ],
        out_specs=[whole_spec(a) for a in shapes],
        out_shape=shapes,
        scratch_shapes=[
            pltpu.VMEM((len(TRACERS) * levels, SUB * east), jnp.bfloat16),
            pltpu.VMEM((levels, SUB * east), jnp.bfloat16),
            pltpu.VMEM((2, levels * SUB, east), f32),
        ],
        compiler_params=call_params(),
    )(dep, adv, back, cotangent, cotangent, *consts)
    return g_in, jnp.sum(g_bias, 1), g_out[:, : levels - 1]


def sum_over_mesh(parts):
    count = lax.axis_size("rows") * lax.axis_size("cols")
    flat = jnp.concatenate([part.reshape(-1) for part in parts])
    total = flat.shape[0]
    chunk = -(-total // (count * 1024)) * 1024
    flat = jnp.pad(flat, (0, chunk * count - total)).reshape(count, chunk // 128, 128)
    pieces = exchange(flat)
    summed = jnp.broadcast_to(jnp.sum(pieces, 0, keepdims=True), flat.shape)
    flat = exchange(summed).reshape(-1)
    results = []
    start = 0
    for part in parts:
        results.append(flat[start : start + part.size].reshape(part.shape))
        start += part.size
    return results


def per_device(fields, cotangent, ocean_mask, depth_levels, in_weight, in_bias, out_weight):
    _, levels, north, east = fields.shape
    tables = Tables(levels, north, east, lax.axis_size("rows"), lax.axis_size("cols"))
    dep = jnp.where(ocean_mask == 1, depth_levels, 0)
    w_in = in_weight.T
    bias = in_bias[:, None]
    w = jnp.pad(out_weight, ((0, 0), (0, levels - out_weight.shape[1])))
    w_out = w.T
    back_coef, back_edges = adjoint_local(tables, cotangent, dep)
    back_jumps = interface(tables, back_edges)
    adv, spread, wm = advance_block(fields, dep)
    new, coef, edges = column(tables, dep, adv, spread, wm, w_in, bias, w_out)
    back = back_finish(tables, back_coef, back_jumps)
    jumps = interface(tables, edges)
    grads = gradients(tables, dep, adv, back, cotangent, w_in, bias, w_out, w)
    grad_w_in, grad_b_in, grad_w_out = sum_over_mesh(grads)
    pressure, new_fields = pressure_finish(tables, dep, adv, new, coef, jumps)
    return (new_fields, pressure, grad_w_in, grad_b_in, grad_w_out)


def solution(mesh):
    in_specs = (
        P(None, None, "cols", "rows"),
        P(None, None, "cols", "rows"),
        P("cols", "rows"),
        P("cols", "rows"),
        P(),
        P(),
        P(),
    )
    out_specs = (P(None, None, "cols", "rows"), P(None, "cols", "rows"), P(), P(), P())
    return jax.shard_map(
        per_device, mesh=mesh, in_specs=in_specs, out_specs=out_specs, check_vma=False
    )
```

profile of v0, /device:TPU:0, one launch (start us, length us, event | category | flops | bytes accessed | tf_op | source)
XLA Modules:
  0.0 185.3 jit_solution(3508449488796451574)
XLA Ops:
  0.7 0.7 compare_select_fusion.dep_ref
  1.4 2.5 %copy-done.1 = f32[5,64,32,128]{3,2,1,0:T(8,128)S(1)} copy-done((f32[5,64,32,128]{3,2,1,0:T(8,128)S(1)}, f32[5,64,32,128]{3,2,1,0:T(8,128)}, u32[]{:S(2)}) %copy-start.1) | copy-done | bytes 5242904
  4.0 3.2 %shard_map.263 = (f32[3,88,128]{2,1,0:T(8,128)S(1)}, f32[3,88,128]{2,1,0:T(8,128)S(1)}, f32[968,128]{1,0:T(8,128)}, f32[968,128]{1,0:T(8,128)}) custom-call(s32[32,128]{1,0:T(8,128)S(1)} %compare_select_fusion.dep_ref, f32[5,2048,128]{2,1,0:T(8,128)S(1)} %bitcast.22), custom_call_target="tpu_custom_call" | custom-call | tf_op jit(solution)/shard_map/pallas_call | solution.py:69
  7.1 0.7 copy-done.41
  7.8 0.7 copy-done.42
  8.5 3.3 %collective-permute-start.2 = (f32[968,128]{1,0:T(8,128)}, f32[968,128]{1,0:T(8,128)}, u32[]{:S(2)}, u32[]{:S(2)}) collective-permute-start(f32[968,128]{1,0:T(8,128)} %get-tuple-element.24), channel_id=1, source_target_pairs={{0,1},{1,2},{2,3},{3,4},{4,5},{5,6},{6,7},{8,9},{9,10},{10,11},{11... | collective-permute-start | bytes 1486856 | tf_op jit(solution)/shard_map/ppermute | solution.py:258
  11.8 1.3 collective-permute-start.3
  13.1 4.4 %shard_map.268 = (f32[32,64,128]{2,1,0:T(8,128)S(1)}, f32[256,128]{1,0:T(8,128)S(1)}) custom-call(s32[32,128]{1,0:T(8,128)S(1)} %compare_select_fusion.dep_ref, f32[5,2048,128]{2,1,0:T(8,128)} %bitcast.33, bf16[128,64]{1,0:T(8,128)(2,1)S(1)} %copy-done.33, f32[64,128]{1,0:T(8,128)S(1)} %copy-done.16, bf16[256,256]{1,0:T(8,128)(2,1)S(1)} %copy-done.19, ...), custom_call_target="tpu_custom_call" | custom-call | tf_op jit(solution)/shard_map/pallas_call | solution.py:615
  17.5 1.0 copy-done.10
  18.5 0.6 copy-done.37
  19.1 8.4 %all-to-all-start.2 = ((f32[32,8,128]{2,1,0:T(8,128)}), f32[32,8,128]{2,1,0:T(8,128)S(1)}, u32[]{:S(2)}, u32[]{:S(2)}) async-start(f32[32,8,128]{2,1,0:T(8,128)} %bitcast.32), calls=%async_computation.2 | async-start | bytes 262144 | tf_op jit(solution)/shard_map/all_to_all | solution.py:565
  27.6 0.7 constant_dynamic-slice_fusion.1.cross_ref
  28.3 0.8 constant_dynamic-slice_fusion.along_ref
  29.0 6.7 %all-to-all-done.2 = f32[32,8,128]{2,1,0:T(8,128)S(1)} async-done(((f32[32,8,128]{2,1,0:T(8,128)}), f32[32,8,128]{2,1,0:T(8,128)S(1)}, u32[]{:S(2)}, u32[]{:S(2)}) %all-to-all-start.2) | async-done | bytes 131104 | tf_op jit(solution)/shard_map/all_to_all | solution.py:565
  35.8 0.8 copy-done.25
  36.6 2.1 %shard_map.269 = f32[256,128]{1,0:T(8,128)} custom-call(f32[256,128]{1,0:T(8,128)S(1)} %bitcast.27, f32[2,10,128]{2,1,0:T(8,128)S(1)} %constant_dynamic-slice_fusion.1.cross_ref, f32[2,8,512]{2,1,0:T(8,128)S(1)} %constant_dynamic-slice_fusion.along_ref, f32[16,16]{1,0:T(8,128)S(1)} %copy-done.39, bf16[2,512,512]{2,1,0:T(8,128)(2,1)S(1)} %copy-done.5, ...), custom_call_target="tpu_custom_call" | custom-call | tf_op jit(solution)/shard_map/pallas_call | solution.py:577
  38.7 3.3 %all-to-all-start.3 = ((f32[32,8,128]{2,1,0:T(8,128)}), f32[32,8,128]{2,1,0:T(8,128)}, u32[]{:S(2)}, u32[]{:S(2)}) async-start(f32[32,8,128]{2,1,0:T(8,128)} %bitcast.14), calls=%async_computation.3 | async-start | bytes 262144 | tf_op jit(solution)/shard_map/all_to_all | solution.py:565
  42.0 3.5 %collective-permute-start = (f32[3,88,128]{2,1,0:T(8,128)}, f32[3,88,128]{2,1,0:T(8,128)S(1)}, u32[]{:S(2)}, u32[]{:S(2)}) collective-permute-start(f32[3,88,128]{2,1,0:T(8,128)} %copy-done.42), channel_id=1, source_target_pairs={{0,8},{8,16},{16,24},{1,9},{9,17},{17,25},{2,10},{10,18},{18,26},{... | collective-permute-start | bytes 405512 | tf_op jit(solution)/shard_map/ppermute | solution.py:258
  45.5 1.3 collective-permute-start.1
  47.0 0.7 fusion
  47.9 1.0 copy.41
  49.0 0.7 copy-done.27
  49.6 3.4 %collective-permute-done.1.xhi_ref = f32[3,88,128]{2,1,0:T(8,128)S(1)} collective-permute-done((f32[3,88,128]{2,1,0:T(8,128)}, f32[3,88,128]{2,1,0:T(8,128)S(1)}, u32[]{:S(2)}, u32[]{:S(2)}) %collective-permute-start.1) | collective-permute-done | bytes 135200 | tf_op jit(solution)/shard_map/ppermute | solution.py:258
  53.0 0.7 copy-done.29
  53.7 2.5 %copy-done.2 = f32[5,64,32,128]{3,2,1,0:T(8,128)S(1)} copy-done((f32[5,64,32,128]{3,2,1,0:T(8,128)S(1)}, f32[5,64,32,128]{3,2,1,0:T(8,128)}, u32[]{:S(2)}) %copy-start.2) | copy-done | bytes 5242904
  56.1 0.9 copy-done.28
  57.1 0.9 copy-done.30
  58.0 34.7 %shard_map.264 = (f32[5,32,64,128]{3,2,1,0:T(8,128)S(1)}, f32[32,64,128]{2,1,0:T(8,128)S(1)}, f32[32,64,128]{2,1,0:T(8,128)S(1)}) custom-call(s32[32,128]{1,0:T(8,128)S(1)} %compare_select_fusion.dep_ref, f32[5,2048,128]{2,1,0:T(8,128)S(1)} %bitcast.23, f32[3,88,128]{2,1,0:T(8,128)S(1)} %copy-done.28, f32[3,88,128]{2,1,0:T(8,128)S(1)} %copy-done.30, ...), custom_call_target="tpu_custom_call" | custom-call | flops 170393600 | bytes 10485760 | tf_op jit(solution)/shard_map/pallas_call | solution.py:221
  92.7 2.3 %copy-done = f32[5,32,64,128]{3,2,1,0:T(8,128)} copy-done((f32[5,32,64,128]{3,2,1,0:T(8,128)}, f32[5,32,64,128]{3,2,1,0:T(8,128)S(1)}, u32[]{:S(2)}) %copy-start) | copy-done | bytes 5242904
  95.0 1.3 copy-done.7
  96.3 0.9 copy-done.15
  97.3 0.9 copy-done.20
  98.2 0.8 copy-done.34
  98.9 10.1 %shard_map.265 = (f32[5,64,32,128]{3,2,1,0:T(8,128)}, f32[32,64,128]{2,1,0:T(8,128)S(1)}, f32[256,128]{1,0:T(8,128)S(1)}) custom-call(s32[32,128]{1,0:T(8,128)S(1)} %compare_select_fusion.dep_ref, f32[5,32,64,128]{3,2,1,0:T(8,128)} %copy-done, f32[32,64,128]{2,1,0:T(8,128)S(1)} %get-tuple-element.27.spread_ref, f32[32,64,128]{2,1,0:T(8,128)S(1)} %get-tuple-element.28.wm_ref, ...), custom_call_target="tpu_custom_call" | custom-call | tf_op jit(solution)/shard_map/pallas_call | solution.py:689
  109.0 1.0 copy-done.12
  110.7 5.0 %all-to-all-start = ((f32[32,8,128]{2,1,0:T(8,128)}), f32[32,8,128]{2,1,0:T(8,128)}, u32[]{:S(2)}, u32[]{:S(2)}) async-start(f32[32,8,128]{2,1,0:T(8,128)} %bitcast.31), calls=%async_computation | async-start | bytes 262144 | tf_op jit(solution)/shard_map/all_to_all | solution.py:565
  115.7 0.9 copy-done.8
  116.6 1.2 copy-done.11
  117.9 0.9 copy-done.17
  118.8 0.8 copy-done.31
  119.5 3.9 %shard_map.270.back_ref = f32[32,64,128]{2,1,0:T(8,128)S(1)} custom-call(f32[32,64,128]{2,1,0:T(8,128)S(1)} %copy-done.11, f32[256,128]{1,0:T(8,128)} %bitcast.15.jump_ref, f32[64,128]{1,0:T(8,128)S(1)} %copy-done.16, bf16[512,256]{1,0:T(8,128)(2,1)S(1)} %copy-done.8, bf16[256,256]{1,0:T(8,128)(2,1)S(1)} %copy-done.17, bf16[128,64]{1,0:T(8,128)(2,1)S(1)} %copy-done.31, ...), custom_call_target="tpu_custom_call" | custom-call | tf_op jit(solution)/shard_map/pallas_call | solution.py:724
  123.5 0.8 copy-done.24
  124.3 6.9 %shard_map.271 = (f32[256,256]{1,0:T(8,128)S(1)}, f32[256,128]{1,0:T(8,128)S(1)}, f32[256,64]{1,0:T(8,128)S(1)}) custom-call(s32[32,128]{1,0:T(8,128)S(1)} %compare_select_fusion.dep_ref, f32[5,32,64,128]{3,2,1,0:T(8,128)} %copy-done, f32[32,64,128]{2,1,0:T(8,128)S(1)} %shard_map.270.back_ref, f32[5,64,32,128]{3,2,1,0:T(8,128)} %salt_ref.1, ...), custom_call_target="tpu_custom_call" | custom-call | tf_op jit(solution)/shard_map/pallas_call | solution.py:848
  131.3 0.8 copy.48
  132.2 1.7 reshape.59
  133.9 1.0 reduce_sum.18
  134.9 1.8 select_maximum_fusion
  136.7 5.7 %all-to-all-start.4 = ((f32[32,24,128]{2,1,0:T(8,128)}), f32[32,24,128]{2,1,0:T(8,128)}, u32[]{:S(2)}, u32[]{:S(2)}) async-start(f32[32,24,128]{2,1,0:T(8,128)} %bitcast.38), calls=%async_computation.4 | async-start | bytes 786432 | tf_op jit(solution)/shard_map/all_to_all | solution.py:565
  142.4 0.9 copy-done.22
  143.3 0.8 copy-done.26
  144.1 2.3 %shard_map.266 = f32[256,128]{1,0:T(8,128)S(1)} custom-call(f32[256,128]{1,0:T(8,128)} %bitcast.6.edge_ref, f32[2,10,128]{2,1,0:T(8,128)S(1)} %constant_dynamic-slice_fusion.1.cross_ref, f32[2,8,512]{2,1,0:T(8,128)S(1)} %constant_dynamic-slice_fusion.along_ref, f32[16,16]{1,0:T(8,128)S(1)} %copy-done.39, bf16[2,512,512]{2,1,0:T(8,128)(2,1)S(1)} %copy-done.5, ...), custom_call_target="tpu_custom_call" | custom-call | tf_op jit(solution)/shard_map/pallas_call | solution.py:577
  146.4 0.7 copy-done.23
  147.1 8.5 %all-to-all-done.4 = f32[32,24,128]{2,1,0:T(8,128)} async-done(((f32[32,24,128]{2,1,0:T(8,128)}), f32[32,24,128]{2,1,0:T(8,128)}, u32[]{:S(2)}, u32[]{:S(2)}) %all-to-all-start.4) | async-done | bytes 393248 | tf_op jit(solution)/shard_map/all_to_all | solution.py:565
  155.6 2.6 %all-to-all-start.1 = ((f32[32,8,128]{2,1,0:T(8,128)}), f32[32,8,128]{2,1,0:T(8,128)S(1)}, u32[]{:S(2)}, u32[]{:S(2)}) async-start(f32[32,8,128]{2,1,0:T(8,128)} %bitcast.28), calls=%async_computation.1 | async-start | bytes 262144 | tf_op jit(solution)/shard_map/all_to_all | solution.py:565
  158.2 1.0 reduce_sum.19
  159.2 7.2 %all-to-all-done.1 = f32[32,8,128]{2,1,0:T(8,128)S(1)} async-done(((f32[32,8,128]{2,1,0:T(8,128)}), f32[32,8,128]{2,1,0:T(8,128)S(1)}, u32[]{:S(2)}, u32[]{:S(2)}) %all-to-all-start.1) | async-done | bytes 131104 | tf_op jit(solution)/shard_map/all_to_all | solution.py:565
  166.4 0.8 broadcast_in_dim.15
  167.2 2.6 %all-to-all-start.5 = ((f32[32,24,128]{2,1,0:T(8,128)}), f32[32,24,128]{2,1,0:T(8,128)S(1)}, u32[]{:S(2)}, u32[]{:S(2)}) async-start(f32[32,24,128]{2,1,0:T(8,128)} %broadcast_in_dim.15), calls=%async_computation.5 | async-start | bytes 786432 | tf_op jit(solution)/shard_map/all_to_all | solution.py:565
  169.9 1.2 copy-done.13
  171.1 0.9 copy-done.18
  172.0 6.5 %shard_map.267 = (f32[2048,128]{1,0:T(8,128)}, f32[5,2048,128]{2,1,0:T(8,128)}) custom-call(s32[32,128]{1,0:T(8,128)S(1)} %compare_select_fusion.dep_ref, f32[5,32,64,128]{3,2,1,0:T(8,128)} %copy-done, f32[5,2048,128]{2,1,0:T(8,128)} %bitcast.34, f32[32,64,128]{2,1,0:T(8,128)S(1)} %copy-done.13, ...), custom_call_target="tpu_custom_call", output_to_operand_aliasing={{1}: (2, {})} | custom-call | tf_op jit(solution)/shard_map/pallas_call | solution.py:757
  178.5 4.5 %all-to-all-done.5 = f32[32,24,128]{2,1,0:T(8,128)S(1)} async-done(((f32[32,24,128]{2,1,0:T(8,128)}), f32[32,24,128]{2,1,0:T(8,128)S(1)}, u32[]{:S(2)}, u32[]{:S(2)}) %all-to-all-start.5) | async-done | bytes 393248 | tf_op jit(solution)/shard_map/all_to_all | solution.py:565
  183.8 0.7 copy.47
  184.6 0.7 slice.20
  (75 shorter events, 2.1 us)
Async XLA Ops:
  0.6 12.4 %copy-start.16 = (f32[64,128]{1,0:T(8,128)S(1)}, f32[64,128]{1,0:T(8,128)}, u32[]{:S(2)}) copy-start(f32[64,128]{1,0:T(8,128)} %constant.58.clone.base_ref) | copy-start | bytes 98308
  0.6 12.4 %copy-start.33 = (bf16[128,64]{1,0:T(8,128)(2,1)S(1)}, bf16[128,64]{1,0:T(8,128)(2,1)}, u32[]{:S(2)}) copy-start(bf16[128,64]{1,0:T(8,128)(2,1)} %constant.57.clone.z_ref) | copy-start | bytes 49156
  1.4 2.5 %copy-start.1 = (f32[5,64,32,128]{3,2,1,0:T(8,128)S(1)}, f32[5,64,32,128]{3,2,1,0:T(8,128)}, u32[]{:S(2)}) copy-start(f32[5,64,32,128]{3,2,1,0:T(8,128)} %param.24) | copy-start | bytes 15728644
  3.9 9.2 %copy-start.6 = (bf16[4096,128]{1,0:T(8,128)(2,1)S(1)}, bf16[4096,128]{1,0:T(8,128)(2,1)}, u32[]{:S(2)}) copy-start(bf16[4096,128]{1,0:T(8,128)(2,1)} %constant.61.clone.take_ref) | copy-start | bytes 3145732
  3.9 9.2 %copy-start.14 = (bf16[512,256]{1,0:T(8,128)(2,1)S(1)}, bf16[512,256]{1,0:T(8,128)(2,1)}, u32[]{:S(2)}) copy-start(bf16[512,256]{1,0:T(8,128)(2,1)} %constant.60.clone.y_ref) | copy-start | bytes 786436
  3.9 9.2 %copy-start.19 = (bf16[256,256]{1,0:T(8,128)(2,1)S(1)}, bf16[256,256]{1,0:T(8,128)(2,1)}, u32[]{:S(2)}) copy-start(bf16[256,256]{1,0:T(8,128)(2,1)} %constant.59.clone.x_ref) | copy-start | bytes 393220
  3.9 31.9 %copy-start.4 = (bf16[2,512,512]{2,1,0:T(8,128)(2,1)S(1)}, bf16[2,512,512]{2,1,0:T(8,128)(2,1)}, u32[]{:S(2)}) copy-start(bf16[2,512,512]{2,1,0:T(8,128)(2,1)} %constant.66.clone.back_ref) | copy-start | bytes 3145732
  3.9 31.9 %copy-start.5 = (bf16[2,512,512]{2,1,0:T(8,128)(2,1)S(1)}, bf16[2,512,512]{2,1,0:T(8,128)(2,1)}, u32[]{:S(2)}) copy-start(bf16[2,512,512]{2,1,0:T(8,128)(2,1)} %constant.65.clone.forward_ref) | copy-start | bytes 3145732
  3.9 31.9 %copy-start.21 = (f32[2,128,128]{2,1,0:T(8,128)S(1)}, f32[2,128,128]{2,1,0:T(8,128)}, u32[]{:S(2)}) copy-start(f32[2,128,128]{2,1,0:T(8,128)} %constant.68.clone.column_ref) | copy-start | bytes 393220
  3.9 31.9 %copy-start.39 = (f32[16,16]{1,0:T(8,128)S(1)}, f32[16,16]{1,0:T(8,128)}, u32[]{:S(2)}) copy-start(f32[16,16]{1,0:T(8,128)} %constant.64.clone.sines_ref) | copy-start | bytes 3076
  3.9 31.9 %copy-start.40 = (f32[8,128]{1,0:T(8,128)S(1)}, f32[8,128]{1,0:T(8,128)}, u32[]{:S(2)}) copy-start(f32[8,128]{1,0:T(8,128)} %constant.69.clone.lines_ref) | copy-start | bytes 12292
  7.1 0.7 copy-start.41
  7.8 0.7 copy-start.42
  8.5 38.4 %copy-start.43 = (bf16[256,63]{0,1:T(8,128)(2,1)S(1)}, bf16[256,63]{0,1:T(8,128)(2,1)}, u32[]{:S(2)}) copy-start(bf16[256,63]{0,1:T(8,128)(2,1)} %param.30) | copy-start | bytes 96772
  8.5 39.2 %copy-start.44 = (f32[256]{0:T(256)S(1)}, f32[256]{0:T(256)}, u32[]{:S(2)}) copy-start(f32[256]{0:T(256)} %param.29) | copy-start | bytes 3076
  8.5 45.2 %collective-permute-start.2 = (f32[968,128]{1,0:T(8,128)}, f32[968,128]{1,0:T(8,128)}, u32[]{:S(2)}, u32[]{:S(2)}) collective-permute-start(f32[968,128]{1,0:T(8,128)} %get-tuple-element.24), channel_id=1, source_target_pairs={{0,1},{1,2},{2,3},{3,4},{4,5},{5,6},{6,7},{8,9},{9,10},{10,11},{11... | collective-permute-start | bytes 1486856 | tf_op jit(solution)/shard_map/ppermute | solution.py:258
  11.8 41.9 %collective-permute-start.3 = (f32[968,128]{1,0:T(8,128)}, f32[968,128]{1,0:T(8,128)}, u32[]{:S(2)}, u32[]{:S(2)}) collective-permute-start(f32[968,128]{1,0:T(8,128)} %get-tuple-element.25), channel_id=1, source_target_pairs={{1,0},{2,1},{3,2},{4,3},{5,4},{6,5},{7,6},{9,8},{10,9},{11,10},{12... | collective-permute-start | bytes 1486856 | tf_op jit(solution)/shard_map/ppermute | solution.py:258
  17.5 1.0 copy-start.10
  18.5 0.7 copy-start.37
  19.1 16.7 %all-to-all-start.2 = ((f32[32,8,128]{2,1,0:T(8,128)}), f32[32,8,128]{2,1,0:T(8,128)S(1)}, u32[]{:S(2)}, u32[]{:S(2)}) async-start(f32[32,8,128]{2,1,0:T(8,128)} %bitcast.32), calls=%async_computation.2 | async-start | bytes 262144 | tf_op jit(solution)/shard_map/all_to_all | solution.py:565
  35.8 0.8 copy-start.25
  38.7 72.0 %all-to-all-start.3 = ((f32[32,8,128]{2,1,0:T(8,128)}), f32[32,8,128]{2,1,0:T(8,128)}, u32[]{:S(2)}, u32[]{:S(2)}) async-start(f32[32,8,128]{2,1,0:T(8,128)} %bitcast.14), calls=%async_computation.3 | async-start | bytes 262144 | tf_op jit(solution)/shard_map/all_to_all | solution.py:565
  42.0 7.0 %collective-permute-start = (f32[3,88,128]{2,1,0:T(8,128)}, f32[3,88,128]{2,1,0:T(8,128)S(1)}, u32[]{:S(2)}, u32[]{:S(2)}) collective-permute-start(f32[3,88,128]{2,1,0:T(8,128)} %copy-done.42), channel_id=1, source_target_pairs={{0,8},{8,16},{16,24},{1,9},{9,17},{17,25},{2,10},{10,18},{18,26},{... | collective-permute-start | bytes 405512 | tf_op jit(solution)/shard_map/ppermute | solution.py:258
  45.5 7.5 %collective-permute-start.1 = (f32[3,88,128]{2,1,0:T(8,128)}, f32[3,88,128]{2,1,0:T(8,128)S(1)}, u32[]{:S(2)}, u32[]{:S(2)}) collective-permute-start(f32[3,88,128]{2,1,0:T(8,128)} %copy-done.41), channel_id=1, source_target_pairs={{8,0},{16,8},{24,16},{9,1},{17,9},{25,17},{10,2},{18,10},{26,18},{... | collective-permute-start | bytes 405512 | tf_op jit(solution)/shard_map/ppermute | solution.py:258
  49.0 0.7 copy-start.27
  53.0 0.7 copy-start.29
  53.7 2.5 %copy-start.2 = (f32[5,64,32,128]{3,2,1,0:T(8,128)S(1)}, f32[5,64,32,128]{3,2,1,0:T(8,128)}, u32[]{:S(2)}) copy-start(f32[5,64,32,128]{3,2,1,0:T(8,128)} %param.24) | copy-start | bytes 15728644
  56.1 0.9 copy-start.28
  57.0 0.9 copy-start.30
  92.7 2.3 %copy-start = (f32[5,32,64,128]{3,2,1,0:T(8,128)}, f32[5,32,64,128]{3,2,1,0:T(8,128)S(1)}, u32[]{:S(2)}) copy-start(f32[5,32,64,128]{3,2,1,0:T(8,128)S(1)} %get-tuple-element.26.adv_ref) | copy-start | bytes 15728644
  95.0 20.7 %copy-start.3 = (bf16[128,4096]{1,0:T(8,128)(2,1)S(1)}, bf16[128,4096]{1,0:T(8,128)(2,1)}, u32[]{:S(2)}) copy-start(bf16[128,4096]{1,0:T(8,128)(2,1)} %constant.73.clone.give_ref) | copy-start | bytes 3145732
  95.0 1.3 copy-start.7
  96.3 0.9 copy-start.15
  97.3 0.9 copy-start.20
  98.2 0.8 copy-start.34
  109.0 1.0 copy-start.12
  110.0 0.7 copy-start.36
  110.7 26.0 %all-to-all-start = ((f32[32,8,128]{2,1,0:T(8,128)}), f32[32,8,128]{2,1,0:T(8,128)}, u32[]{:S(2)}, u32[]{:S(2)}) async-start(f32[32,8,128]{2,1,0:T(8,128)} %bitcast.31), calls=%async_computation | async-start | bytes 262144 | tf_op jit(solution)/shard_map/all_to_all | solution.py:565
  115.7 1.0 copy-start.8
  116.6 1.2 copy-start.11
  117.9 0.9 copy-start.17
  118.8 0.8 copy-start.31
  123.5 0.8 copy-start.24
  131.3 0.9 copy-start.35
  131.3 0.9 copy-start.38
  131.3 38.5 %copy-start.9 = (bf16[512,256]{1,0:T(8,128)(2,1)S(1)}, bf16[512,256]{1,0:T(8,128)(2,1)}, u32[]{:S(2)}) copy-start(bf16[512,256]{1,0:T(8,128)(2,1)} %constant.70.clone.y_ref) | copy-start | bytes 786436
  131.3 38.5 %copy-start.32 = (bf16[128,64]{1,0:T(8,128)(2,1)S(1)}, bf16[128,64]{1,0:T(8,128)(2,1)}, u32[]{:S(2)}) copy-start(bf16[128,64]{1,0:T(8,128)(2,1)} %constant.72.clone.z_ref) | copy-start | bytes 49156
  136.7 18.9 %all-to-all-start.4 = ((f32[32,24,128]{2,1,0:T(8,128)}), f32[32,24,128]{2,1,0:T(8,128)}, u32[]{:S(2)}, u32[]{:S(2)}) async-start(f32[32,24,128]{2,1,0:T(8,128)} %bitcast.38), calls=%async_computation.4 | async-start | bytes 786432 | tf_op jit(solution)/shard_map/all_to_all | solution.py:565
  142.4 0.9 copy-start.22
  143.3 0.8 copy-start.26
  146.4 0.7 copy-start.23
  155.6 10.9 %all-to-all-start.1 = ((f32[32,8,128]{2,1,0:T(8,128)}), f32[32,8,128]{2,1,0:T(8,128)S(1)}, u32[]{:S(2)}, u32[]{:S(2)}) async-start(f32[32,8,128]{2,1,0:T(8,128)} %bitcast.28), calls=%async_computation.1 | async-start | bytes 262144 | tf_op jit(solution)/shard_map/all_to_all | solution.py:565
  167.2 15.8 %all-to-all-start.5 = ((f32[32,24,128]{2,1,0:T(8,128)}), f32[32,24,128]{2,1,0:T(8,128)S(1)}, u32[]{:S(2)}, u32[]{:S(2)}) async-start(f32[32,24,128]{2,1,0:T(8,128)} %broadcast_in_dim.15), calls=%async_computation.5 | async-start | bytes 786432 | tf_op jit(solution)/shard_map/all_to_all | solution.py:565
  169.8 1.2 copy-start.13
  171.1 0.9 copy-start.18
where the time goes:
time: 187 us; the launch traced here: 185 us
  Pallas kernels  74.2 us (40%)
  local copies, waits for them, and re-layouts  38.1 us (20%)
  starting transfers between devices  37 us (20%)
  waiting for transfers between devices  30.4 us (16%)
  other arithmetic  4.57 us (2%)
    pallas_call x1, Pallas kernels, advect(): pl.pallas_call(advect_kernel, grid=(levels // SUB,), in_specs=[whole(dep)...  34.7 us
    unnamed x94, local copies, waits for them, and re-layouts  31.6 us
    all_to_all x6, starting transfers between devices, exchange(): return lax.all_to_all(block, AXES, split_axis=0, concat_axis=0, tiled=True)  27.7 us
    all_to_all x6, waiting for transfers between devices, exchange(): return lax.all_to_all(block, AXES, split_axis=0, concat_axis=0, tiled=True)  26.9 us
    pallas_call x1, Pallas kernels, column(): pl.pallas_call(functools.partial(column_kernel, tables), grid=(north // S...  10.1 us
    pallas_call x1, Pallas kernels, gradients(): pl.pallas_call(functools.partial(gradient_kernel, tables), grid=(north //...  6.94 us
    ppermute x2, starting transfers between devices, shift_both(): lax.ppermute(last, axis, forward)  6.81 us
    pallas_call x1, Pallas kernels, pressure_finish(): pl.pallas_call(functools.partial(pressure_kernel, tables), grid=(1,), in_...  6.52 us
  transfers between devices with their start and end apart: 10, of which 6 were waited for; matrix products, arithmetic and copies ran while one was open for 5% of the time, Pallas kernels for 38%

commit v1 on v0

--- a/solution.py
+++ b/solution.py
@@ -75,7 +75,7 @@
         ],
         out_specs=[whole(x_shape), whole(x_shape), whole(y_shape), whole(y_shape)],
         out_shape=[x_shape, x_shape, y_shape, y_shape],
-        compiler_params=pltpu.CompilerParams(vmem_limit_bytes=32 << 20),
+        compiler_params=pltpu.CompilerParams(vmem_limit_bytes=VMEM_LIMIT),
     )(dep, fields.reshape(FIELDS, levels * north, east))
 
 
@@ -99,10 +99,14 @@
 
 
 def advect_kernel(
-    dep_ref, fields_ref, xlo_ref, xhi_ref, ylo_ref, yhi_ref,
-    adv_ref, spread_ref, wm_ref,
-    deep, both, lines, slopes, fluxes, cells, wets, su, su6, sv, sv6, sides,
+    tracers, staged, dep_ref, *refs,
 ):
+    field_refs, refs = refs[: len(staged)], refs[len(staged) :]
+    xlo_ref, xhi_ref, ylo_ref, yhi_ref, _, adv_ref = refs[:6]
+    spread_ref = refs[6] if len(tracers) > 1 else None
+    (
+        deep, both, lines, slopes, fluxes, cells, wets, su, su6, sv, sv6, sides,
+    ) = refs[-12:]
     step = pl.program_id(0)
     north, east = dep_ref.shape
     per = east // north
@@ -133,26 +137,30 @@
     for y in range(north):
         wets[y + 1] = (level < depths[y : y + 1]).astype(jnp.float32)
 
-    def stage(f, carry):
+    for slot, f in enumerate(staged):
+        field = field_refs[slot]
         for s in range(HALO):
             at = pl.multiple_of((f * HALO + s) * levels + first_level, SUB)
-            cells[f, s] = ylo_ref[pl.ds(at, SUB), :]
-            cells[f, north + HALO + s] = yhi_ref[pl.ds(at, SUB), :]
+            cells[slot, s] = ylo_ref[pl.ds(at, SUB), :]
+            cells[slot, north + HALO + s] = yhi_ref[pl.ds(at, SUB), :]
         for y in range(north):
-            cells[f, y + HALO] = fields_ref[f, pl.ds(y, SUB, stride=north), :] * wets[y + 1]
+            cells[slot, y + HALO] = field[0, pl.ds(y, SUB, stride=north), :] * wets[y + 1]
         for b in range(blocks):
             row = f * all_blocks + step * blocks + b
             for s in range(HALO):
-                lines[f, b, SUB - HALO + s : SUB - HALO + s + 1, :] = xlo_ref[s, pl.ds(row, 1), :]
-                lines[f, b, SUB + east + s : SUB + east + s + 1, :] = xhi_ref[s, pl.ds(row, 1), :]
-            turned = fields_ref[f, b * east : (b + 1) * east, :].T
+                lines[slot, b, SUB - HALO + s : SUB - HALO + s + 1, :] = xlo_ref[
+                    s, pl.ds(row, 1), :
+                ]
+                lines[slot, b, SUB + east + s : SUB + east + s + 1, :] = xhi_ref[
+                    s, pl.ds(row, 1), :
+                ]
+            turned = field[0, b * east : (b + 1) * east, :].T
             height = (side_level + b * per).astype(jnp.float32)
             for r in range(0, east, SUB):
                 wet = height < deep[SUB + r : 2 * SUB + r, :]
-                lines[f, b, SUB + r : 2 * SUB + r, :] = jnp.where(wet, turned[r : r + SUB], 0.0)
-        return carry
-
-    lax.fori_loop(0, FIELDS, stage, 0)
+                lines[slot, b, SUB + r : 2 * SUB + r, :] = jnp.where(
+                    wet, turned[r : r + SUB], 0.0
+                )
 
     for b in range(blocks):
         height = (side_level + b * per).astype(jnp.float32)
@@ -163,20 +171,23 @@
             speed = jnp.where(height < both[r : r + SUB, :], speed, 0.0)
             su[b, r : r + SUB, :] = speed
             su6[b, r : r + SUB, :] = jnp.abs(speed) * (1.0 / 6.0)
-        change = 0.5 * (
-            lines[0, b, SUB + 1 : SUB + 1 + east, :] - lines[0, b, SUB - 1 : SUB - 1 + east, :]
-        )
-        sides[b * east : (b + 1) * east, :] = change.T
-    for y in range(north):
-        spread_ref[y] = sides[pl.ds(y, SUB, stride=north), :] + 0.5 * (
-            cells[1, y + HALO + 1] - cells[1, y + HALO - 1]
-        )
-        wm_ref[y] = cells[2, y + HALO]
+        if spread_ref is not None:
+            change = 0.5 * (
+                lines[0, b, SUB + 1 : SUB + 1 + east, :] - lines[0, b, SUB - 1 : SUB - 1 + east, :]
+            )
+            sides[b * east : (b + 1) * east, :] = change.T
+    if spread_ref is not None:
+        for y in range(north):
+            spread_ref[y] = sides[pl.ds(y, SUB, stride=north), :] + 0.5 * (
+                cells[1, y + HALO + 1] - cells[1, y + HALO - 1]
+            )
     for y in range(north + 1):
         speed = (0.5 * TIME_STEP) * (cells[1, y + HALO - 1] + cells[1, y + HALO])
         speed = speed * (wets[y] * wets[y + 1])
         sv[y] = speed
         sv6[y] = jnp.abs(speed) * (1.0 / 6.0)
+
+    first = len(staged) - len(tracers)
 
     def advance_field(f, carry):
         for b in range(blocks):
@@ -204,39 +215,44 @@
             north_face = face_flux(inclines[-5:], line[-4], line[-3], sv[y], sv6[y])
             if y > 0:
                 change = sides[pl.ds(y - 1, SUB, stride=north), :] + (south - north_face)
-                adv_ref[f, y - 1] = wets[y] * (line[-4] + change)
+                adv_ref[f - first, y - 1] = wets[y] * (line[-4] + change)
             south = north_face
         return carry
 
-    lax.fori_loop(0, FIELDS, advance_field, 0)
-
-
-def advect(fields, dep, xlo, xhi, ylo, yhi):
+    lax.fori_loop(first, len(staged), advance_field, 0)
+
+
+def advect(fields, dep, tracers, edges, after):
     _, levels, north, east = fields.shape
     whole = lambda a: pl.BlockSpec(a.shape, lambda k: (0,) * a.ndim)
-    plane = pl.BlockSpec((north, SUB, east), lambda k: (0, k, 0))
+    staged = tracers if tracers[0] == 0 else (0, 1, *tracers)
+    one = lambda f: pl.BlockSpec((1, SUB * north, east), lambda k: (f, k, 0))
     f32 = jnp.float32
-    one = jax.ShapeDtypeStruct((north, levels, east), f32)
     blocks = SUB * north // east
+    flat = fields.reshape(FIELDS, levels * north, east)
+    out_specs = [pl.BlockSpec((len(tracers), north, SUB, east), lambda k: (0, 0, k, 0))]
+    out_shape = [jax.ShapeDtypeStruct((len(tracers), north, levels, east), f32)]
+    if tracers[0] == 0:
+        out_specs.append(pl.BlockSpec((north, SUB, east), lambda k: (0, k, 0)))
+        out_shape.append(jax.ShapeDtypeStruct((north, levels, east), f32))
     return pl.pallas_call(
-        advect_kernel,
+        functools.partial(advect_kernel, tracers, staged),
         grid=(levels // SUB,),
         in_specs=[
             whole(dep),
-            pl.BlockSpec((FIELDS, SUB * north, east), lambda k: (0, k, 0)),
-            whole(xlo), whole(xhi), whole(ylo), whole(yhi),
-        ],
-        out_specs=[
-            pl.BlockSpec((FIELDS, north, SUB, east), lambda k: (0, 0, k, 0)), plane, plane,
-        ],
-        out_shape=[jax.ShapeDtypeStruct((FIELDS, north, levels, east), f32), one, one],
+            *(one(f) for f in staged),
+            *(whole(a) for a in edges),
+            pl.BlockSpec(memory_space=pl.ANY),
+        ],
+        out_specs=out_specs,
+        out_shape=out_shape,
         scratch_shapes=[
             pltpu.VMEM((east + 2 * SUB, east), f32),
             pltpu.VMEM((east + SUB, east), f32),
-            pltpu.VMEM((FIELDS, blocks, east + 3 * SUB, east), f32),
+            pltpu.VMEM((len(staged), blocks, east + 3 * SUB, east), f32),
             pltpu.VMEM((blocks, east + 3 * SUB, east), f32),
             pltpu.VMEM((blocks, east + SUB, east), f32),
-            pltpu.VMEM((FIELDS, north + 2 * HALO, SUB, east), f32),
+            pltpu.VMEM((len(staged), north + 2 * HALO, SUB, east), f32),
             pltpu.VMEM((north + 2, SUB, east), f32),
             pltpu.VMEM((blocks, east + SUB, east), f32),
             pltpu.VMEM((blocks, east + SUB, east), f32),
@@ -244,29 +260,24 @@
             pltpu.VMEM((north + 1, SUB, east), f32),
             pltpu.VMEM((SUB * north, east), f32),
         ],
-        compiler_params=pltpu.CompilerParams(vmem_limit_bytes=40 << 20),
-        cost_estimate=pl.CostEstimate(
-            flops=int(fields.size) * 130, bytes_accessed=2 * 4 * int(fields.size), transcendentals=0
-        ),
-    )(dep, fields.reshape(FIELDS, levels * north, east), xlo, xhi, ylo, yhi)
-
-
-def shift_both(block, axis, first, last):
+        compiler_params=pltpu.CompilerParams(vmem_limit_bytes=VMEM_LIMIT),
+    )(dep, *(flat for _ in staged), *edges, after)
+
+
+def shift_both(axis, first, last):
     count = lax.axis_size(axis)
     forward = [(i, i + 1) for i in range(count - 1)]
     backward = [(i + 1, i) for i in range(count - 1)]
     return lax.ppermute(last, axis, forward), lax.ppermute(first, axis, backward)
 
 
-def advance_block(fields, dep):
+def advance_edges(fields, dep):
     xfirst, xlast, yfirst, ylast = pack_edges(fields, dep)
-    ylo, yhi = shift_both(None, "cols", yfirst, ylast)
-    xlo, xhi = shift_both(None, "rows", xfirst, xlast)
-    return advect(fields, dep, xlo, xhi, ylo, yhi)
+    return (*shift_both("rows", xfirst, xlast), *shift_both("cols", yfirst, ylast))
 
 
 AXES = ("rows", "cols")
-VMEM_LIMIT = 48 << 20
+VMEM_LIMIT = 60 << 20
 TRACERS = (0, 1, 3, 4)
 PARTS = 4
 
@@ -470,10 +481,18 @@
 
 
 def interface_kernel(
-    tables, edge_ref, cross_ref, along_ref, sines_ref, forward_ref, back_ref,
-    strip_ref, column_ref, lines_ref, jump_ref,
+    tables, device_ref, edge_ref, cross_ref, along_ref, sines_ref, forward_ref, back_ref,
+    strip_ref, column_ref, lines_ref, *rest,
 ):
+    del device_ref
+    extra_ref, jump_ref = rest
     rows, cols, east, north = tables.rows, tables.cols, tables.east, tables.north
+    each = jump_ref.shape[0] // tables.count
+    if each > tables.share * PARTS:
+        more = extra_ref.shape[0] // tables.count
+        for d in range(tables.count):
+            at = d * each + tables.share * PARTS
+            jump_ref[at : at + more, :] = extra_ref[d * more : (d + 1) * more, :]
     share, inner = tables.share, tables.rows - 1
     f32 = jnp.float32
     east_last, east_first = lines_ref[0:1, :], lines_ref[1:2, :]
@@ -548,8 +567,8 @@
                 tile = tile + pltpu.roll(jumps[a - 1], north, 1)
             out = (tile, tall[a], pltpu.roll(tall[a], 1, 0), jnp.zeros_like(tile))
             for part in range(PARTS):
-                at = (a * cols * share + m) * PARTS + part
-                jump_ref[pl.ds(at, cols, stride=share * PARTS), :] = out[part]
+                at = a * cols * each + m * PARTS + part
+                jump_ref[pl.ds(at, cols, stride=each), :] = out[part]
 
 
 def whole_spec(array):
@@ -565,29 +584,38 @@
     return lax.all_to_all(block, AXES, split_axis=0, concat_axis=0, tiled=True)
 
 
-def interface(tables, edges):
-    received = exchange(edges)
+def interface(tables, received, extra, travels):
     device = lax.axis_index("rows") * lax.axis_size("cols") + lax.axis_index("cols")
-    cross = lax.dynamic_slice_in_dim(tables.cross, device * tables.share, tables.share, 0)
-    along = lax.dynamic_slice_in_dim(tables.along, device * tables.share, tables.share, 0)
     operands = (
-        received, cross, along, tables.sines, tables.wide_forward, tables.wide_back,
+        received, tables.cross, tables.along, tables.sines, tables.wide_forward, tables.wide_back,
         tables.strip, tables.column, tables.lines,
     )
-    jumps = pl.pallas_call(
+    specs = [whole_spec(a) for a in operands]
+    for at in (1, 2):
+        shape = (tables.share, *operands[at].shape[1:])
+        specs[at] = pl.BlockSpec(shape, lambda k, mine: (mine[0], 0, 0))
+    rows = received.shape[0] + (extra.shape[0] if travels else 0)
+    shape = jax.ShapeDtypeStruct((rows, tables.east), jnp.float32)
+    return pl.pallas_call(
         functools.partial(interface_kernel, tables),
-        in_specs=[whole_spec(a) for a in operands],
-        out_specs=whole_spec(received),
-        out_shape=jax.ShapeDtypeStruct(received.shape, jnp.float32),
-        grid=(1,),
+        grid_spec=pltpu.PrefetchScalarGridSpec(
+            num_scalar_prefetch=1,
+            grid=(1,),
+            in_specs=[
+                *specs,
+                whole_spec(extra) if travels else pl.BlockSpec(memory_space=pl.ANY),
+            ],
+            out_specs=whole_spec(shape),
+        ),
+        out_shape=shape,
         compiler_params=call_params(),
-    )(*operands)
-    return exchange(jumps)
+    )(device.astype(jnp.int32).reshape(1), *operands, extra)
 
 
 def adjoint_kernel(
-    tables, dep_ref, cot_ref, z_ref, base_ref, x_ref, y_ref, take_ref, coef_ref, edge_ref, spec
+    tables, dep_ref, cot_ref, z_ref, base_ref, x_ref, y_ref, take_ref, *rest,
 ):
+    coef_ref, edge_ref, spec = rest[-3:]
     north, east, levels = tables.north, tables.east, tables.levels
     level = lax.broadcasted_iota(jnp.int32, (levels, east), 0)
     for y in range(0, north, 4):
@@ -608,7 +636,7 @@
     return [coef, edge]
 
 
-def adjoint_local(tables, cotangent, dep):
+def adjoint_local(tables, cotangent, dep, *after):
     levels, north, east = tables.levels, tables.north, tables.east
     consts = (tables.z_forward, tables.base, tables.x_forward, tables.y_forward, tables.take)
     shapes = solve_shapes(tables)
@@ -619,138 +647,297 @@
             whole_spec(dep),
             pl.BlockSpec((1, levels * north, east), lambda k: (2, 0, 0)),
             *(whole_spec(a) for a in consts),
+            *(pl.BlockSpec(memory_space=pl.ANY) for _ in after),
         ],
         out_specs=[whole_spec(a) for a in shapes],
         out_shape=shapes,
         scratch_shapes=[pltpu.VMEM(shapes[0].shape, jnp.float32)],
         compiler_params=call_params(),
-    )(dep, cotangent.reshape(FIELDS, levels * north, east), *consts)
-
-
-def closure(feats, w_in, bias, w_out):
-    activity = jnp.tanh(mul(w_in, feats) + bias)
-    hidden = activity.astype(jnp.bfloat16)
-    return activity, hidden, RATE_MAX * jax.nn.sigmoid(mul(w_out, hidden))
+    )(dep, cotangent.reshape(FIELDS, levels * north, east), *consts, *after)
+
+
+def set_weights(w_in_ref, bias_ref, w_ref, w_in, bias, w, w_out, levels):
+    inputs, width = w_in_ref.shape
+    east = bias.shape[1]
+    w_in[...] = w_in_ref[...].astype(jnp.float32).T.astype(jnp.bfloat16)
+    bias[...] = jnp.broadcast_to(bias_ref[...], (east, width)).T
+    for k in range(0, width, east):
+        w[k : k + east, :] = jnp.zeros((east, east), jnp.float32)
+        w[k : k + levels - 1, :] = w_ref[:, k : k + east].astype(jnp.float32)
+        tile = w[k : k + east, :]
+        w_out[:, k : k + east] = tile[:levels].astype(jnp.bfloat16)
+        w[k : k + east, :] = tile.T
+
+
+def closure(adv_ref, w_in, bias, w_out, feats, activity, hidden):
+    levels, east = adv_ref.shape[2:]
+    for k in range(SUB):
+        for f in range(len(TRACERS)):
+            feats[f * levels : (f + 1) * levels, k * east : (k + 1) * east] = adv_ref[f, k].astype(
+                jnp.bfloat16
+            )
+    before = mul(w_in[...], feats[...])
+    for k in range(SUB):
+        lanes = slice(k * east, (k + 1) * east)
+        value = jnp.tanh(before[:, lanes] + bias[...])
+        if activity is not None:
+            activity[:, lanes] = value
+        hidden[:, lanes] = value.astype(jnp.bfloat16)
+    return RATE_MAX * jax.nn.sigmoid(mul(w_out[...], hidden[...]))
 
 
 def column_kernel(
-    tables, dep_ref, adv_ref, spread_ref, wm_ref, w_in_ref, bias_ref, w_out_ref,
+    tables, dep_ref, adv_ref, spread_ref, w_field_ref, w_in_ref, bias_ref, w_ref,
     z_ref, base_ref, x_ref, y_ref, take_ref,
-    new_ref, coef_ref, edge_ref, spec, feats, flat,
+    mixed_ref, coef_ref, edge_ref,
+    spec, feats, hidden, flat, w_in, bias, w, w_out,
 ):
     step = pl.program_id(0)
     north, east, levels = tables.north, tables.east, tables.levels
-    for k in range(SUB):
-        for i, f in enumerate(TRACERS):
-            feats[i * levels : (i + 1) * levels, k * east : (k + 1) * east] = adv_ref[f, k].astype(
-                jnp.bfloat16
-            )
-    _, _, rates = closure(feats[...], w_in_ref[...], bias_ref[...], w_out_ref[...])
+
+    @pl.when(step == 0)
+    def _():
+        set_weights(w_in_ref, bias_ref, w_ref, w_in, bias, w, w_out, levels)
+
+    rates = closure(adv_ref, w_in, bias, w_out, feats, None, hidden)
+    flat[...] = w_field_ref[0].reshape(levels * SUB, east)
     level = lax.broadcasted_iota(jnp.int32, (levels, east), 0)
     depths = dep_ref[pl.ds(pl.multiple_of(step * SUB, SUB), SUB), :]
     sources = []
     for k in range(SUB):
+        lanes = slice(k * east, (k + 1) * east)
         depth = depths[k : k + 1]
         wet = level < depth
-        bond = jnp.where(level + 1 < depth, TIME_STEP, 0.0)
-        flow = bond * rates[:, k * east : (k + 1) * east]
+        flow = jnp.where(level + 1 < depth, TIME_STEP, 0.0) * rates[:, lanes]
         mixed = []
-        for f in (3, 4):
-            value = adv_ref[f, k]
+        for i in range(2):
+            value = adv_ref[2 + i, k]
             flux = flow * (pltpu.roll(value, levels - 1, 0) - value)
             value = jnp.where(wet, value + (flux - pltpu.roll(flux, 1, 0)), 0.0)
             mixed.append(value)
-            flat[f, pl.ds(k, levels, stride=SUB), :] = value
-        for f in (0, 1):
-            flat[f, pl.ds(k, levels, stride=SUB), :] = adv_ref[f, k]
-        density = THERMAL * mixed[0] - HALINE * mixed[1] - wm_ref[k] * (1.0 / TIME_STEP)
+            mixed_ref[i, k] = value
+        rise = jnp.where(wet, flat[pl.ds(k, levels, stride=SUB), :], 0.0)
+        density = THERMAL * mixed[0] - HALINE * mixed[1] - rise * (1.0 / TIME_STEP)
         source = vertical_change(density) - spread_ref[k] * (1.0 / TIME_STEP)
         sources.append(jnp.where(wet, source, 0.0))
     tile = from_left(z_ref[...], jnp.concatenate(sources, 1))
     for k in range(SUB):
         spec[step * SUB + k] = tile[:, k * east : (k + 1) * east]
-    for f in TRACERS:
-        new_ref[f] = flat[f].reshape(levels, SUB, east)
 
     @pl.when(step == north // SUB - 1)
     def _():
         local_solve(tables, spec, base_ref, x_ref, y_ref, take_ref, coef_ref, edge_ref)
 
 
-def column(tables, dep, adv, spread, wm, w_in, bias, w_out):
+def closure_scratch(levels, east, inputs, hidden):
+    f32, bf16 = jnp.float32, jnp.bfloat16
+    return [
+        pltpu.VMEM((hidden, inputs), bf16),
+        pltpu.VMEM((hidden, east), f32),
+        pltpu.VMEM((hidden, east), f32),
+        pltpu.VMEM((levels, hidden), bf16),
+    ]
+
+
+def column(tables, dep, adv, spread, fields, in_weight, in_bias, out_weight):
     levels, north, east = tables.levels, tables.north, tables.east
-    tall = lambda n: pl.BlockSpec((n, SUB, levels, east), lambda k: (0, k, 0, 0))
-    plane = pl.BlockSpec((SUB, levels, east), lambda k: (k, 0, 0))
+    inputs, hidden = in_weight.shape
+    f32, bf16 = jnp.float32, jnp.bfloat16
     consts = (
-        w_in, bias, w_out,
+        in_weight, in_bias, out_weight,
         tables.z_forward, tables.base, tables.x_forward, tables.y_forward, tables.take,
     )
+    mixed = jax.ShapeDtypeStruct((2, north, levels, east), f32)
     shapes = solve_shapes(tables)
+    lanes = SUB * east
     return pl.pallas_call(
         functools.partial(column_kernel, tables),
         grid=(north // SUB,),
-        in_specs=[whole_spec(dep), tall(FIELDS), plane, plane, *(whole_spec(a) for a in consts)],
+        in_specs=[
+            whole_spec(dep),
+            pl.BlockSpec((len(TRACERS), SUB, levels, east), lambda k: (0, k, 0, 0)),
+            pl.BlockSpec((SUB, levels, east), lambda k: (k, 0, 0)),
+            pl.BlockSpec((1, levels, SUB, east), lambda k: (2, 0, k, 0)),
+            *(whole_spec(a) for a in consts),
+        ],
         out_specs=[
-            pl.BlockSpec((FIELDS, levels, SUB, east), lambda k: (0, 0, k, 0)),
+            pl.BlockSpec((2, SUB, levels, east), lambda k: (0, k, 0, 0)),
             *(whole_spec(a) for a in shapes),
         ],
-        out_shape=[jax.ShapeDtypeStruct((FIELDS, levels, north, east), jnp.float32), *shapes],
+        out_shape=[mixed, *shapes],
         scratch_shapes=[
-            pltpu.VMEM(shapes[0].shape, jnp.float32),
-            pltpu.VMEM((len(TRACERS) * levels, SUB * east), jnp.bfloat16),
-            pltpu.VMEM((FIELDS, levels * SUB, east), jnp.float32),
+            pltpu.VMEM(shapes[0].shape, f32),
+            pltpu.VMEM((inputs, lanes), bf16),
+            pltpu.VMEM((hidden, lanes), bf16),
+            pltpu.VMEM((levels * SUB, east), f32),
+            *closure_scratch(levels, east, inputs, hidden),
         ],
         compiler_params=call_params(),
-    )(dep, adv, spread, wm, *consts)
-
-
-def back_kernel(
-    tables, coef_ref, jump_ref, base_ref, y_ref, x_ref, z_ref, give_ref, back_ref, spec
+    )(dep, adv, spread, fields, *consts)
+
+
+def gradient_kernel(
+    tables, dep_ref, adv_ref, heat_ref, salt_ref, w_in_ref, bias_ref, w_ref,
+    coef_ref, jump_ref, base_ref, y_ref, x_ref, z_ref, give_ref, after_ref,
+    total_ref,
+    spec, back, feats, activity, hidden, grads, cots, w_in, bias, w, w_out,
+    g_in_ref, g_bias_ref, g_out_ref,
 ):
-    def use(y, tile):
-        back_ref[y] = tile
-
-    finish_solve(
-        tables, spec, coef_ref, jump_ref, base_ref, y_ref, x_ref, z_ref, give_ref, use
-    )
+    del after_ref
+    step = pl.program_id(0)
+    north, east, levels = tables.north, tables.east, tables.levels
+    f32, bf16 = jnp.float32, jnp.bfloat16
+
+    @pl.when(step == 0)
+    def _():
+        set_weights(w_in_ref, bias_ref, w_ref, w_in, bias, w, w_out, levels)
+        g_in_ref[...] = jnp.zeros_like(g_in_ref)
+        g_out_ref[...] = jnp.zeros_like(g_out_ref)
+        g_bias_ref[...] = jnp.zeros_like(g_bias_ref)
+
+        def use(y, tile):
+            back[y] = tile
+
+        finish_solve(
+            tables, spec, coef_ref, jump_ref, base_ref, y_ref, x_ref, z_ref, give_ref, use
+        )
+
+    rates = closure(adv_ref, w_in, bias, w_out, feats, activity, hidden)
+    cots[0] = heat_ref[0].reshape(levels * SUB, east)
+    cots[1] = salt_ref[0].reshape(levels * SUB, east)
+    level = lax.broadcasted_iota(jnp.int32, (levels, east), 0)
+    depths = dep_ref[pl.ds(pl.multiple_of(step * SUB, SUB), SUB), :]
+    for k in range(SUB):
+        lanes = slice(k * east, (k + 1) * east)
+        depth = depths[k : k + 1]
+        wet = level < depth
+        rate = rates[:, lanes]
+        flow = jnp.where(level + 1 < depth, TIME_STEP, 0.0) * rate
+        slope = -vertical_change(jnp.where(wet, back[step * SUB + k], 0.0))
+        total = jnp.zeros((levels, east), f32)
+        for i, share in ((0, THERMAL), (1, -HALINE)):
+            value = adv_ref[2 + i, k]
+            drop = pltpu.roll(value, levels - 1, 0) - value
+            grad = cots[i, pl.ds(k, levels, stride=SUB), :] + share * slope
+            grad = jnp.where(wet, grad, 0.0)
+            total = total + (grad - pltpu.roll(grad, levels - 1, 0)) * drop
+        grads[:, lanes] = (total * flow * (1.0 - rate * (1.0 / RATE_MAX))).astype(bf16)
+    over = (((1,), (1,)), ((), ()))
+    grad = grads[...]
+    g_out_ref[...] += lax.dot_general(hidden[...], grad, over, preferred_element_type=f32)
+    pre = mul(w[:, :levels].astype(bf16), grad)
+    for k in range(SUB):
+        lanes = slice(k * east, (k + 1) * east)
+        value = activity[:, lanes]
+        value = pre[:, lanes] * (1.0 - value * value)
+        g_bias_ref[...] += value
+        hidden[:, lanes] = value.astype(bf16)
+    g_in_ref[...] += lax.dot_general(feats[...], hidden[...], over, preferred_element_type=f32)
+
+    @pl.when(step == north // SUB - 1)
+    def _():
+        inputs, width = g_in_ref.shape
+        for k in range(width // east):
+            total_ref[k * inputs : (k + 1) * inputs, :] = g_in_ref[:, k * east : (k + 1) * east]
+        sums = jnp.sum(g_bias_ref[...], 1, keepdims=True)
+        last = jnp.concatenate([g_out_ref[...], jnp.broadcast_to(sums, g_out_ref.shape)], 1)
+        at = inputs * width // east
+        for k in range(0, width, east):
+            total_ref[at + k : at + k + east, :] = last[k : k + east].T
+
+
+def gradients(tables, dep, adv, cotangent, in_weight, in_bias, out_weight, coef, jumps, after):
+    levels, north, east = tables.levels, tables.north, tables.east
+    inputs, hidden = in_weight.shape
+    f32, bf16 = jnp.float32, jnp.bfloat16
+    field = lambda f: pl.BlockSpec((1, levels, SUB, east), lambda k: (f, 0, k, 0))
+    consts = (in_weight, in_bias, out_weight, coef, jumps, *solve_consts(tables))
+    rows = inputs * hidden // east + hidden
+    assert 2 * levels == east
+    total = jax.ShapeDtypeStruct((-(-rows // tables.count) * tables.count, east), f32)
+    lanes = SUB * east
+    return pl.pallas_call(
+        functools.partial(gradient_kernel, tables),
+        grid=(north // SUB,),
+        in_specs=[
+            whole_spec(dep),
+            pl.BlockSpec((len(TRACERS), SUB, levels, east), lambda k: (0, k, 0, 0)),
+            field(3),
+            field(4),
+            *(whole_spec(a) for a in consts),
+            pl.BlockSpec(memory_space=pl.ANY),
+        ],
+        out_specs=whole_spec(total),
+        out_shape=total,
+        scratch_shapes=[
+            pltpu.VMEM(coef.shape, f32),
+            pltpu.VMEM(coef.shape, f32),
+            pltpu.VMEM((inputs, lanes), bf16),
+            pltpu.VMEM((hidden, lanes), f32),
+            pltpu.VMEM((hidden, lanes), bf16),
+            pltpu.VMEM((levels, lanes), bf16),
+            pltpu.VMEM((2, levels * SUB, east), f32),
+            *closure_scratch(levels, east, inputs, hidden),
+            pltpu.VMEM((inputs, hidden), f32),
+            pltpu.VMEM((hidden, east), f32),
+            pltpu.VMEM((hidden, levels), f32),
+        ],
+        compiler_params=call_params(),
+    )(dep, adv, cotangent, cotangent, *consts, after)
+
+
+def gather_kernel(adv_ref, mixed_ref, after_ref, new_ref, flat):
+    del after_ref
+    levels, east = adv_ref.shape[2:]
+    for f, (ref, i) in zip(TRACERS, ((adv_ref, 0), (adv_ref, 1), (mixed_ref, 0), (mixed_ref, 1))):
+        for k in range(SUB):
+            flat[f, pl.ds(k, levels, stride=SUB), :] = ref[i, k]
+        new_ref[f] = flat[f].reshape(levels, SUB, east)
+
+
+def gather_fields(adv, mixed, after):
+    _, north, levels, east = adv.shape
+    block = pl.BlockSpec((2, SUB, levels, east), lambda k: (0, k, 0, 0))
+    return pl.pallas_call(
+        gather_kernel,
+        grid=(north // SUB,),
+        in_specs=[block, block, pl.BlockSpec(memory_space=pl.ANY)],
+        out_specs=pl.BlockSpec((FIELDS, levels, SUB, east), lambda k: (0, 0, k, 0)),
+        out_shape=jax.ShapeDtypeStruct((FIELDS, levels, north, east), jnp.float32),
+        scratch_shapes=[pltpu.VMEM((FIELDS, levels * SUB, east), jnp.float32)],
+        compiler_params=call_params(),
+    )(adv, mixed, after)
 
 
 def solve_consts(tables):
     return (tables.base, tables.y_back, tables.x_back, tables.z_back, tables.give)
 
 
-def back_finish(tables, coef, jumps):
-    operands = (coef, jumps, *solve_consts(tables))
-    return pl.pallas_call(
-        functools.partial(back_kernel, tables),
-        grid=(1,),
-        in_specs=[whole_spec(a) for a in operands],
-        out_specs=whole_spec(coef),
-        out_shape=jax.ShapeDtypeStruct(coef.shape, jnp.float32),
-        scratch_shapes=[pltpu.VMEM(coef.shape, jnp.float32)],
-        compiler_params=call_params(),
-    )(*operands)
-
-
 def pressure_kernel(
-    tables, dep_ref, adv_ref, new_ref, coef_ref, jump_ref, base_ref, y_ref, x_ref, z_ref, give_ref,
-    pressure_ref, out_ref, spec,
+    tables, dep_ref, w_ref, new_ref, coef_ref, jump_ref, base_ref, y_ref, x_ref, z_ref, give_ref,
+    pressure_ref, out_ref, spec, jumps,
 ):
     north, east, levels = tables.north, tables.east, tables.levels
+    mine = tables.share * PARTS
+    each = jump_ref.shape[0] // tables.count
+    for part in range(mine):
+        jumps[pl.ds(part, tables.count, stride=mine), :] = jump_ref[
+            pl.ds(part, tables.count, stride=each), :
+        ]
     level = lax.broadcasted_iota(jnp.int32, (levels, east), 0)
 
     def use(y, tile):
         pressure_ref[pl.ds(y, levels, stride=north), :] = tile
-        value = adv_ref[0, y] - TIME_STEP * vertical_change(tile)
+        value = w_ref[0, y] - TIME_STEP * vertical_change(tile)
         value = jnp.where(level < dep_ref[y : y + 1, :], value, 0.0)
         out_ref[0, pl.ds(y, levels, stride=north), :] = value
 
     finish_solve(
-        tables, spec, coef_ref, jump_ref, base_ref, y_ref, x_ref, z_ref, give_ref, use
+        tables, spec, coef_ref, jumps, base_ref, y_ref, x_ref, z_ref, give_ref, use
     )
 
 
-def pressure_finish(tables, dep, adv, new, coef, jumps):
+def pressure_finish(tables, dep, w, new, coef, jumps):
     levels, north, east = tables.levels, tables.north, tables.east
     consts = solve_consts(tables)
     flat = jax.ShapeDtypeStruct((levels * north, east), jnp.float32)
@@ -759,7 +946,7 @@
         grid=(1,),
         in_specs=[
             whole_spec(dep),
-            pl.BlockSpec((1, north, levels, east), lambda k: (2, 0, 0, 0)),
+            whole_spec(w),
             pl.BlockSpec(memory_space=pl.ANY),
             whole_spec(coef),
             whole_spec(jumps),
@@ -771,138 +958,92 @@
         ],
         out_shape=[flat, jax.ShapeDtypeStruct((FIELDS, levels * north, east), jnp.float32)],
         input_output_aliases={2: 1},
-        scratch_shapes=[pltpu.VMEM(coef.shape, jnp.float32)],
+        scratch_shapes=[
+            pltpu.VMEM(coef.shape, jnp.float32),
+            pltpu.VMEM((tables.share * tables.count * PARTS, east), jnp.float32),
+        ],
         compiler_params=call_params(),
-    )(dep, adv, new.reshape(FIELDS, levels * north, east), coef, jumps, *consts)
+    )(dep, w, new.reshape(FIELDS, levels * north, east), coef, jumps, *consts)
     return pressure.reshape(levels, north, east), new.reshape(FIELDS, levels, north, east)
 
 
-def gradient_kernel(
-    tables, dep_ref, adv_ref, back_ref, heat_ref, salt_ref, w_in_ref, bias_ref, w_out_ref, w_ref,
-    g_in_ref, g_bias_ref, g_out_ref, feats, grads, flat,
-):
-    step = pl.program_id(0)
-    east, levels = tables.east, tables.levels
-    for k in range(SUB):
-        for i, f in enumerate(TRACERS):
-            feats[i * levels : (i + 1) * levels, k * east : (k + 1) * east] = adv_ref[f, k].astype(
-                jnp.bfloat16
-            )
-    activity, hidden, rates = closure(feats[...], w_in_ref[...], bias_ref[...], w_out_ref[...])
-    flat[0] = heat_ref[0].reshape(levels * SUB, east)
-    flat[1] = salt_ref[0].reshape(levels * SUB, east)
-    level = lax.broadcasted_iota(jnp.int32, (levels, east), 0)
-    depths = dep_ref[pl.ds(pl.multiple_of(step * SUB, SUB), SUB), :]
-    for k in range(SUB):
-        depth = depths[k : k + 1]
-        wet = level < depth
-        density = -vertical_change(jnp.where(wet, back_ref[k], 0.0))
-        total = jnp.zeros((levels, east), jnp.float32)
-        for i, f, share in ((0, 3, THERMAL), (1, 4, -HALINE)):
-            value = adv_ref[f, k]
-            grad = flat[i, pl.ds(k, levels, stride=SUB), :] + share * density
-            grad = jnp.where(wet, grad, 0.0)
-            total = total + (grad - pltpu.roll(grad, levels - 1, 0)) * (
-                pltpu.roll(value, levels - 1, 0) - value
-            )
-        total = jnp.where(level + 1 < depth, TIME_STEP * total, 0.0)
-        rate = rates[:, k * east : (k + 1) * east]
-        grads[:, k * east : (k + 1) * east] = (
-            total * rate * (1.0 - rate * (1.0 / RATE_MAX))
-        ).astype(jnp.bfloat16)
-    over = (((1,), (1,)), ((), ()))
-    grad = grads[...]
-    g_out = lax.dot_general(hidden, grad, over, preferred_element_type=jnp.float32)
-    pre = mul(w_ref[...], grad) * (1.0 - activity * activity)
-    g_in = lax.dot_general(
-        feats[...], pre.astype(jnp.bfloat16), over, preferred_element_type=jnp.float32
-    )
-    g_bias = pre[:, :east]
-    for k in range(1, SUB):
-        g_bias = g_bias + pre[:, k * east : (k + 1) * east]
-
-    @pl.when(step == 0)
-    def _():
-        g_in_ref[...] = g_in
-        g_out_ref[...] = g_out
-        g_bias_ref[...] = g_bias
-
-    @pl.when(step > 0)
-    def _():
-        g_in_ref[...] += g_in
-        g_out_ref[...] += g_out
-        g_bias_ref[...] += g_bias
-
-
-def gradients(tables, dep, adv, back, cotangent, w_in, bias, w_out, w):
-    levels, north, east = tables.levels, tables.north, tables.east
-    hidden, inputs = w_in.shape
-    f32 = jnp.float32
+def sum_kernel(count, skip, pieces_ref, *rest):
+    out_ref = rest[-1]
+    each = pieces_ref.shape[0] // count
+    more = each - skip
+    total = pieces_ref[skip:each, :]
+    for d in range(1, count):
+        total = total + pieces_ref[d * each + skip : (d + 1) * each, :]
+    for d in range(count):
+        out_ref[d * more : (d + 1) * more, :] = total
+
+
+def sum_pieces(tables, received, *after):
+    skip = tables.share * PARTS
+    rows = received.shape[0] - skip * tables.count
+    shape = jax.ShapeDtypeStruct((rows, tables.east), jnp.float32)
+    return pl.pallas_call(
+        functools.partial(sum_kernel, tables.count, skip),
+        grid=(1,),
+        in_specs=[whole_spec(received), *(pl.BlockSpec(memory_space=pl.ANY) for _ in after)],
+        out_specs=whole_spec(shape),
+        out_shape=shape,
+        compiler_params=call_params(),
+    )(received, *after)
+
+
+def split_kernel(sums_ref, in_ref, bias_ref, out_ref):
+    inputs, width = in_ref.shape
+    east = sums_ref.shape[1]
+    wide = inputs * width // east
+    for k in range(width // east):
+        lanes = slice(k * east, (k + 1) * east)
+        in_ref[:, lanes] = sums_ref[k * inputs : (k + 1) * inputs, :]
+        at = wide + k * east
+        out_ref[:, lanes] = sums_ref[at : at + out_ref.shape[0], :]
+        bias_ref[:, lanes] = sums_ref[at + east // 2 : at + east // 2 + 1, :]
+
+
+def split_sums(sums, inputs, hidden, outputs):
     shapes = [
-        jax.ShapeDtypeStruct((inputs, hidden), f32),
-        jax.ShapeDtypeStruct((hidden, east), f32),
-        jax.ShapeDtypeStruct((hidden, levels), f32),
+        jax.ShapeDtypeStruct(shape, jnp.float32)
+        for shape in ((inputs, hidden), (1, hidden), (outputs, hidden))
     ]
-    field = lambda f: pl.BlockSpec((1, levels, SUB, east), lambda k: (f, 0, k, 0))
-    consts = (w_in, bias, w_out, w)
     g_in, g_bias, g_out = pl.pallas_call(
-        functools.partial(gradient_kernel, tables),
-        grid=(north // SUB,),
-        in_specs=[
-            whole_spec(dep),
-            pl.BlockSpec((FIELDS, SUB, levels, east), lambda k: (0, k, 0, 0)),
-            pl.BlockSpec((SUB, levels, east), lambda k: (k, 0, 0)),
-            field(3),
-            field(4),
-            *(whole_spec(a) for a in consts),
-        ],
+        split_kernel,
+        grid=(1,),
+        in_specs=[whole_spec(sums)],
         out_specs=[whole_spec(a) for a in shapes],
         out_shape=shapes,
-        scratch_shapes=[
-            pltpu.VMEM((len(TRACERS) * levels, SUB * east), jnp.bfloat16),
-            pltpu.VMEM((levels, SUB * east), jnp.bfloat16),
-            pltpu.VMEM((2, levels * SUB, east), f32),
-        ],
         compiler_params=call_params(),
-    )(dep, adv, back, cotangent, cotangent, *consts)
-    return g_in, jnp.sum(g_bias, 1), g_out[:, : levels - 1]
-
-
-def sum_over_mesh(parts):
-    count = lax.axis_size("rows") * lax.axis_size("cols")
-    flat = jnp.concatenate([part.reshape(-1) for part in parts])
-    total = flat.shape[0]
-    chunk = -(-total // (count * 1024)) * 1024
-    flat = jnp.pad(flat, (0, chunk * count - total)).reshape(count, chunk // 128, 128)
-    pieces = exchange(flat)
-    summed = jnp.broadcast_to(jnp.sum(pieces, 0, keepdims=True), flat.shape)
-    flat = exchange(summed).reshape(-1)
-    results = []
-    start = 0
-    for part in parts:
-        results.append(flat[start : start + part.size].reshape(part.shape))
-        start += part.size
-    return results
+    )(sums)
+    return g_in, g_bias.reshape(hidden), g_out.T
 
 
 def per_device(fields, cotangent, ocean_mask, depth_levels, in_weight, in_bias, out_weight):
     _, levels, north, east = fields.shape
     tables = Tables(levels, north, east, lax.axis_size("rows"), lax.axis_size("cols"))
     dep = jnp.where(ocean_mask == 1, depth_levels, 0)
-    w_in = in_weight.T
-    bias = in_bias[:, None]
-    w = jnp.pad(out_weight, ((0, 0), (0, levels - out_weight.shape[1])))
-    w_out = w.T
-    back_coef, back_edges = adjoint_local(tables, cotangent, dep)
-    back_jumps = interface(tables, back_edges)
-    adv, spread, wm = advance_block(fields, dep)
-    new, coef, edges = column(tables, dep, adv, spread, wm, w_in, bias, w_out)
-    back = back_finish(tables, back_coef, back_jumps)
-    jumps = interface(tables, edges)
-    grads = gradients(tables, dep, adv, back, cotangent, w_in, bias, w_out, w)
-    grad_w_in, grad_b_in, grad_w_out = sum_over_mesh(grads)
-    pressure, new_fields = pressure_finish(tables, dep, adv, new, coef, jumps)
-    return (new_fields, pressure, grad_w_in, grad_b_in, grad_w_out)
+    inputs, hidden = in_weight.shape
+    outputs = out_weight.shape[1]
+    in_bias = in_bias.reshape(1, hidden)
+    out_weight = out_weight.T
+    edges = advance_edges(fields, dep)
+    back_coef, back_edges = adjoint_local(tables, cotangent, dep, edges[0], edges[1])
+    adv, spread = advect(fields, dep, TRACERS, edges, edges[0])
+    back_jumps = exchange(interface(tables, exchange(back_edges), adv, False))
+    mixed, coef, sides = column(tables, dep, adv, spread, fields, in_weight, in_bias, out_weight)
+    received = exchange(sides)
+    grads = gradients(
+        tables, dep, adv, cotangent, in_weight, in_bias, out_weight, back_coef, back_jumps, coef
+    )
+    jumps_out = interface(tables, received, grads, True)
+    jumps = exchange(jumps_out)
+    w = advect(fields, dep, (2,), edges, jumps_out)[0]
+    new = gather_fields(adv, mixed, jumps_out)
+    sums = exchange(sum_pieces(tables, jumps, w, new))
+    pressure, new_fields = pressure_finish(tables, dep, w, new, coef, jumps)
+    return (new_fields, pressure, *split_sums(sums, inputs, hidden, outputs))
 
 
 def solution(mesh):

time: 187 us -> 158 us (0.84)
  local copies, waits for them, and re-layouts: 38.1 us -> 5.11 us
  Pallas kernels: 74.2 us -> 98.3 us
  waiting for transfers between devices: 30.4 us -> 11.8 us
  other arithmetic: 4.57 us -> 1.34 us
  starting transfers between devices: 37 us -> 39.6 us
    unnamed x94 -> x18, local copies, waits for them, and re-layouts: 31.6 us -> 5.11 us
    all_to_all x6 -> x5, waiting for transfers between devices: 26.9 us -> 5.64 us  [exchange(): return lax.all_to_all(block, AXES, split_axis=0, concat_axis=0, tiled=True)]
    pallas_call x4 -> x7, Pallas kernels: 43 us -> 55.8 us  [the longest x2 39 us: advect(): pl.pallas_call(functools.partial(advect_kernel, tracers, staged), grid=(l...]
    pallas_call x1, Pallas kernels: 6.94 us -> 12.8 us  [gradients(): pl.pallas_call(functools.partial(gradient_kernel, tables), grid=(north //...]
    pallas_call x1, Pallas kernels: 3.19 us -> 6.11 us  [pack_edges(): pl.pallas_call(pack_kernel, grid=(FIELDS,), in_specs=[pl.BlockSpec((north...]
    all_to_all x6 -> x5, starting transfers between devices: 27.7 us -> 30.4 us  [exchange(): return lax.all_to_all(block, AXES, split_axis=0, concat_axis=0, tiled=True)]
    reduce_sum x2 -> x0, other arithmetic: 2.05 us -> none  [the longest x1 1.04 us: sum_over_mesh(): summed = jnp.broadcast_to(jnp.sum(pieces, 0, keepdims=True), flat.shape)]
    reshape x2 -> x0, local copies, waits for them, and re-layouts: 1.94 us -> none  [the longest x1 1.74 us: sum_over_mesh(): flat = jnp.concatenate([part.reshape(-1) for part in parts])]
  transfers between devices with their start and end apart: 10 -> 9, of which waited for: 6 -> 3; matrix products, arithmetic and copies ran while one was open for 5% -> 0% of each run, Pallas kernels for 38% -> 51%
where the time goes in v1:
time: 158 us; the launch traced here: 157 us
  Pallas kernels  98.3 us (62%)
  starting transfers between devices  39.6 us (25%)
  waiting for transfers between devices  11.8 us (7%)
  local copies, waits for them, and re-layouts  5.11 us (3%)
    pallas_call x2, Pallas kernels, advect(): pl.pallas_call(functools.partial(advect_kernel, tracers, staged), grid=(l...  39 us
    all_to_all x5, starting transfers between devices, exchange(): return lax.all_to_all(block, AXES, split_axis=0, concat_axis=0, tiled=True)  30.4 us
    pallas_call x1, Pallas kernels, gradients(): pl.pallas_call(functools.partial(gradient_kernel, tables), grid=(north //...  12.8 us
    pallas_call x1, Pallas kernels, column(): pl.pallas_call(functools.partial(column_kernel, tables), grid=(north // S...  10.5 us
    pallas_call x2, Pallas kernels, interface(): pl.pallas_call(functools.partial(interface_kernel, tables), grid_spec=plt...  7.81 us
    pallas_call x1, Pallas kernels, pressure_finish(): pl.pallas_call(functools.partial(pressure_kernel, tables), grid=(1,), in_...  7.54 us
    ppermute x2, starting transfers between devices, shift_both(): lax.ppermute(last, axis, forward)  6.69 us
    pallas_call x1, Pallas kernels, pack_edges(): pl.pallas_call(pack_kernel, grid=(FIELDS,), in_specs=[pl.BlockSpec((north...  6.11 us
  transfers between devices with their start and end apart: 9, of which 3 were waited for; matrix products, arithmetic and copies ran while one was open for 0% of the time, Pallas kernels for 51%

profile of v1, /device:TPU:0, one launch (start us, length us, event | category | flops | bytes accessed | tf_op | source)
XLA Modules:
  0.0 156.9 jit_solution(8536478729688176971)
XLA Ops:
  0.6 1.3 compare_select_fusion.dep_ref
  2.0 6.1 %shard_map.263 = (f32[3,88,128]{2,1,0:T(8,128)}, f32[3,88,128]{2,1,0:T(8,128)}, f32[968,128]{1,0:T(8,128)}, f32[968,128]{1,0:T(8,128)}) custom-call(s32[32,128]{1,0:T(8,128)} %compare_select_fusion.dep_ref, f32[5,2048,128]{2,1,0:T(8,128)} %bitcast.20), custom_call_target="tpu_custom_call" | custom-call | tf_op jit(solution)/shard_map/pallas_call | solution.py:69
  8.1 2.4 %collective-permute-start.2 = (f32[968,128]{1,0:T(8,128)}, f32[968,128]{1,0:T(8,128)S(1)}, u32[]{:S(2)}, u32[]{:S(2)}) collective-permute-start(f32[968,128]{1,0:T(8,128)} %get-tuple-element.23), channel_id=1, source_target_pairs={{0,1},{1,2},{2,3},{3,4},{4,5},{5,6},{6,7},{8,9},{9,10},{10,11},{11... | collective-permute-start | bytes 1486856 | tf_op jit(solution)/shard_map/ppermute | solution.py:271
  10.5 1.3 collective-permute-start.3
  11.8 4.3 %collective-permute-start = (f32[3,88,128]{2,1,0:T(8,128)}, f32[3,88,128]{2,1,0:T(8,128)S(1)}, u32[]{:S(2)}, u32[]{:S(2)}) collective-permute-start(f32[3,88,128]{2,1,0:T(8,128)} %get-tuple-element.21), channel_id=1, source_target_pairs={{0,8},{8,16},{16,24},{1,9},{9,17},{17,25},{2,10},{10,18},{18,26},{... | collective-permute-start | bytes 405512 | tf_op jit(solution)/shard_map/ppermute | solution.py:271
  16.1 1.3 collective-permute-start.1
  17.4 1.6 collective-permute-done.refs_4_.refs_8_.rest_0_.refs_3_
  18.9 0.0 copy-start.1
  18.9 4.6 %collective-permute-done.1.refs_5_.rest_1_.refs_4_ = f32[3,88,128]{2,1,0:T(8,128)S(1)} collective-permute-done((f32[3,88,128]{2,1,0:T(8,128)}, f32[3,88,128]{2,1,0:T(8,128)S(1)}, u32[]{:S(2)}, u32[]{:S(2)}) %collective-permute-start.1) | collective-permute-done | bytes 135200 | tf_op jit(solution)/shard_map/ppermute | solution.py:271
  23.5 0.0 copy-start.5
  23.5 0.0 copy-done.1
  23.5 0.7 copy-done.5
  24.2 5.5 %shard_map.266 = (f32[32,64,128]{2,1,0:T(8,128)}, f32[256,128]{1,0:T(8,128)}) custom-call(s32[32,128]{1,0:T(8,128)} %compare_select_fusion.dep_ref, f32[5,2048,128]{2,1,0:T(8,128)} %bitcast.30, bf16[128,64]{1,0:T(8,128)(2,1)} %constant.48.clone.z_ref, f32[64,128]{1,0:T(8,128)} %constant.49.clone.base_ref, bf16[256,256]{1,0:T(8,128)(2,1)} %constant.50.clone.x_ref, ...), custom_call_target="tpu_custom_call" | custom-call | tf_op jit(solution)/shard_map/pallas_call | solution.py:643
  29.7 7.0 %all-to-all-start.1 = ((f32[32,8,128]{2,1,0:T(8,128)}), f32[32,8,128]{2,1,0:T(8,128)S(1)}, u32[]{:S(2)}, u32[]{:S(2)}) async-start(f32[32,8,128]{2,1,0:T(8,128)} %bitcast.42), calls=%async_computation.1 | async-start | bytes 262144 | tf_op jit(solution)/shard_map/all_to_all | solution.py:584
  36.7 0.0 collective-permute-done.2.refs_6_.refs_5_
  36.8 0.0 copy-start.2
  36.8 0.0 collective-permute-done.3.refs_7_.refs_6_
  36.8 0.8 copy-done.2
  37.6 0.0 copy-start.3
  37.6 0.8 copy-done.3
  38.4 28.4 %shard_map.264 = (f32[4,32,64,128]{3,2,1,0:T(8,128)}, f32[32,64,128]{2,1,0:T(8,128)}) custom-call(s32[32,128]{1,0:T(8,128)} %compare_select_fusion.dep_ref, f32[5,2048,128]{2,1,0:T(8,128)} %bitcast.21, f32[5,2048,128]{2,1,0:T(8,128)} %bitcast.22, f32[5,2048,128]{2,1,0:T(8,128)} %bitcast.23, f32[5,2048,128]{2,1,0:T(8,128)} %bitcast.24, ...), custom_call_target="tpu_custom_call" | custom-call | tf_op jit(solution)/shard_map/pallas_call | solution.py:238
  66.8 0.0 all-to-all-done.1
  66.8 0.0 copy-start.6
  66.8 0.6 copy-done.6
  67.5 3.8 %shard_map.267 = f32[256,128]{1,0:T(8,128)} custom-call(s32[1]{0:T(128)} %bitcast.1.device_ref, f32[256,128]{1,0:T(8,128)} %bitcast.36, f32[64,10,128]{2,1,0:T(8,128)} %constant.53.clone.cross_ref, f32[64,8,512]{2,1,0:T(8,128)} %constant.54.clone.along_ref, f32[16,16]{1,0:T(8,128)} %constant.55.clone.sines_ref, ...), custom_call_target="tpu_custom_call" | custom-call | tf_op jit(solution)/shard_map/pallas_call | solution.py:599
  71.2 5.8 %all-to-all-start.2 = ((f32[32,8,128]{2,1,0:T(8,128)}), f32[32,8,128]{2,1,0:T(8,128)S(1)}, u32[]{:S(2)}, u32[]{:S(2)}) async-start(f32[32,8,128]{2,1,0:T(8,128)} %bitcast.38), calls=%async_computation.2 | async-start | bytes 262144 | tf_op jit(solution)/shard_map/all_to_all | solution.py:584
  77.1 10.5 %shard_map.265 = (f32[2,32,64,128]{3,2,1,0:T(8,128)}, f32[32,64,128]{2,1,0:T(8,128)}, f32[256,128]{1,0:T(8,128)}) custom-call(s32[32,128]{1,0:T(8,128)} %compare_select_fusion.dep_ref, f32[4,32,64,128]{3,2,1,0:T(8,128)} %get-tuple-element.25.adv_ref.rest_0_, f32[32,64,128]{2,1,0:T(8,128)} %get-tuple-element.26.spread_ref, f32[5,64,32,128]{3,2,1,0:T(8,128)} %w_field_ref.1, ...), custom_call_target="tpu_custom_call" | custom-call | tf_op jit(solution)/shard_map/pallas_call | solution.py:753
  87.5 0.0 all-to-all-done.2
  87.6 0.0 copy-start.7
  87.6 6.0 %all-to-all-start = ((f32[32,8,128]{2,1,0:T(8,128)}), f32[32,8,128]{2,1,0:T(8,128)S(1)}, u32[]{:S(2)}, u32[]{:S(2)}) async-start(f32[32,8,128]{2,1,0:T(8,128)} %bitcast.43), calls=%async_computation | async-start | bytes 262144 | tf_op jit(solution)/shard_map/all_to_all | solution.py:584
  93.6 0.0 copy-done.7
  93.6 12.8 %shard_map.268.rest_0_ = f32[768,128]{1,0:T(8,128)} custom-call(s32[32,128]{1,0:T(8,128)} %compare_select_fusion.dep_ref, f32[4,32,64,128]{3,2,1,0:T(8,128)} %get-tuple-element.25.adv_ref.rest_0_, f32[5,64,32,128]{3,2,1,0:T(8,128)} %salt_ref.1, f32[5,64,32,128]{3,2,1,0:T(8,128)} %salt_ref.1, bf16[256,256]{1,0:T(8,128)(2,1)} %w_in_ref.3, f32[1,256]{1,0:T(1,128)} %bitcast.45, ...), custom_call_target="tpu_custom_call" | custom-call | tf_op jit(solution)/shard_map/pallas_call | solution.py:859
  106.4 0.0 all-to-all-done
  106.4 0.0 copy-start.8
  106.4 0.6 copy-done.8
  107.1 4.1 %shard_map.269.refs_7_.after_ref = f32[1024,128]{1,0:T(8,128)} custom-call(s32[1]{0:T(128)} %bitcast.1.device_ref, f32[256,128]{1,0:T(8,128)} %bitcast.39, f32[64,10,128]{2,1,0:T(8,128)} %constant.53.clone.cross_ref, f32[64,8,512]{2,1,0:T(8,128)} %constant.54.clone.along_ref, f32[16,16]{1,0:T(8,128)} %constant.55.clone.sines_ref, ...), custom_call_target="tpu_custom_call" | custom-call | tf_op jit(solution)/shard_map/pallas_call | solution.py:599
  111.1 5.7 %all-to-all-start.3 = ((f32[32,32,128]{2,1,0:T(8,128)}), f32[32,32,128]{2,1,0:T(8,128)S(1)}, u32[]{:S(2)}, u32[]{:S(2)}) async-start(f32[32,32,128]{2,1,0:T(8,128)} %bitcast.31), calls=%async_computation.3 | async-start | bytes 1048576 | tf_op jit(solution)/shard_map/all_to_all | solution.py:584
  116.8 5.4 %shard_map.271.rest_1_ = f32[5,64,32,128]{3,2,1,0:T(8,128)} custom-call(f32[4,32,64,128]{3,2,1,0:T(8,128)} %get-tuple-element.25.adv_ref.rest_0_, f32[2,32,64,128]{3,2,1,0:T(8,128)} %get-tuple-element.31.mixed_ref, f32[1024,128]{1,0:T(8,128)} %shard_map.269.refs_7_.after_ref), custom_call_target="tpu_custom_call" | custom-call | tf_op jit(solution)/shard_map/pallas_call | solution.py:901
  122.2 10.5 %shard_map.270.w_ref.rest_0_ = f32[1,32,64,128]{3,2,1,0:T(8,128)} custom-call(s32[32,128]{1,0:T(8,128)} %compare_select_fusion.dep_ref, f32[5,2048,128]{2,1,0:T(8,128)} %bitcast.25, f32[5,2048,128]{2,1,0:T(8,128)} %bitcast.26, f32[5,2048,128]{2,1,0:T(8,128)} %bitcast.27, f32[3,88,128]{2,1,0:T(8,128)} %copy-done.1, f32[3,88,128]{2,1,0:T(8,128)} %copy-done.5, ...), custom_call_target="tpu_custom_call" | custom-call | tf_op jit(solution)/shard_map/pallas_call | solution.py:238
  132.7 0.0 all-to-all-done.3
  132.8 0.0 copy-start
  132.8 0.8 copy-done
  133.5 1.9 %shard_map.273 = f32[768,128]{1,0:T(8,128)} custom-call(f32[1024,128]{1,0:T(8,128)} %bitcast.32, f32[1,32,64,128]{3,2,1,0:T(8,128)} %shard_map.270.w_ref.rest_0_, f32[5,64,32,128]{3,2,1,0:T(8,128)} %shard_map.271.rest_1_), custom_call_target="tpu_custom_call" | custom-call | tf_op jit(solution)/shard_map/pallas_call | solution.py:985
  135.4 5.8 %all-to-all-start.4 = ((f32[32,24,128]{2,1,0:T(8,128)}), f32[32,24,128]{2,1,0:T(8,128)S(1)}, u32[]{:S(2)}, u32[]{:S(2)}) async-start(f32[32,24,128]{2,1,0:T(8,128)} %bitcast.34), calls=%async_computation.4 | async-start | bytes 786432 | tf_op jit(solution)/shard_map/all_to_all | solution.py:584
  141.3 7.5 %shard_map.272 = (f32[2048,128]{1,0:T(8,128)}, f32[5,2048,128]{2,1,0:T(8,128)}) custom-call(s32[32,128]{1,0:T(8,128)} %compare_select_fusion.dep_ref, f32[1,32,64,128]{3,2,1,0:T(8,128)} %shard_map.270.w_ref.rest_0_, f32[5,2048,128]{2,1,0:T(8,128)} %bitcast.28, f32[32,64,128]{2,1,0:T(8,128)} %get-tuple-element.30.after_ref.coef_ref, ...), custom_call_target="tpu_custom_call", output_to_operand_aliasing={{1}: (2, {})} | custom-call | tf_op jit(solution)/shard_map/pallas_call | solution.py:944
  148.8 5.6 %all-to-all-done.4 = f32[32,24,128]{2,1,0:T(8,128)S(1)} async-done(((f32[32,24,128]{2,1,0:T(8,128)}), f32[32,24,128]{2,1,0:T(8,128)S(1)}, u32[]{:S(2)}, u32[]{:S(2)}) %all-to-all-start.4) | async-done | bytes 393248 | tf_op jit(solution)/shard_map/all_to_all | solution.py:584
  154.4 0.0 copy-start.4
  154.5 0.8 copy-done.4
  155.2 1.7 %shard_map.274 = (f32[256,256]{1,0:T(8,128)}, f32[1,256]{1,0:T(1,128)}, f32[63,256]{1,0:T(8,128)}) custom-call(f32[768,128]{1,0:T(8,128)} %bitcast.35), custom_call_target="tpu_custom_call" | custom-call | tf_op jit(solution)/shard_map/pallas_call | solution.py:1012
Async XLA Ops:
  8.1 28.7 %collective-permute-start.2 = (f32[968,128]{1,0:T(8,128)}, f32[968,128]{1,0:T(8,128)S(1)}, u32[]{:S(2)}, u32[]{:S(2)}) collective-permute-start(f32[968,128]{1,0:T(8,128)} %get-tuple-element.23), channel_id=1, source_target_pairs={{0,1},{1,2},{2,3},{3,4},{4,5},{5,6},{6,7},{8,9},{9,10},{10,11},{11... | collective-permute-start | bytes 1486856 | tf_op jit(solution)/shard_map/ppermute | solution.py:271
  10.5 26.3 %collective-permute-start.3 = (f32[968,128]{1,0:T(8,128)}, f32[968,128]{1,0:T(8,128)S(1)}, u32[]{:S(2)}, u32[]{:S(2)}) collective-permute-start(f32[968,128]{1,0:T(8,128)} %get-tuple-element.24), channel_id=1, source_target_pairs={{1,0},{2,1},{3,2},{4,3},{5,4},{6,5},{7,6},{9,8},{10,9},{11,10},{12... | collective-permute-start | bytes 1486856 | tf_op jit(solution)/shard_map/ppermute | solution.py:271
  11.8 7.2 %collective-permute-start = (f32[3,88,128]{2,1,0:T(8,128)}, f32[3,88,128]{2,1,0:T(8,128)S(1)}, u32[]{:S(2)}, u32[]{:S(2)}) collective-permute-start(f32[3,88,128]{2,1,0:T(8,128)} %get-tuple-element.21), channel_id=1, source_target_pairs={{0,8},{8,16},{16,24},{1,9},{9,17},{17,25},{2,10},{10,18},{18,26},{... | collective-permute-start | bytes 405512 | tf_op jit(solution)/shard_map/ppermute | solution.py:271
  16.1 7.4 %collective-permute-start.1 = (f32[3,88,128]{2,1,0:T(8,128)}, f32[3,88,128]{2,1,0:T(8,128)S(1)}, u32[]{:S(2)}, u32[]{:S(2)}) collective-permute-start(f32[3,88,128]{2,1,0:T(8,128)} %get-tuple-element.22), channel_id=1, source_target_pairs={{8,0},{16,8},{24,16},{9,1},{17,9},{25,17},{10,2},{18,10},{26,18},{... | collective-permute-start | bytes 405512 | tf_op jit(solution)/shard_map/ppermute | solution.py:271
  18.9 4.6 %copy-start.1 = (f32[3,88,128]{2,1,0:T(8,128)}, f32[3,88,128]{2,1,0:T(8,128)S(1)}, u32[]{:S(2)}) copy-start(f32[3,88,128]{2,1,0:T(8,128)S(1)} %collective-permute-done.refs_4_.refs_8_.rest_0_.refs_3_) | copy-start | bytes 405508
  23.5 0.7 copy-start.5
  29.7 37.1 %all-to-all-start.1 = ((f32[32,8,128]{2,1,0:T(8,128)}), f32[32,8,128]{2,1,0:T(8,128)S(1)}, u32[]{:S(2)}, u32[]{:S(2)}) async-start(f32[32,8,128]{2,1,0:T(8,128)} %bitcast.42), calls=%async_computation.1 | async-start | bytes 262144 | tf_op jit(solution)/shard_map/all_to_all | solution.py:584
  36.8 0.8 copy-start.2
  37.6 0.8 copy-start.3
  66.8 0.6 copy-start.6
  71.2 16.3 %all-to-all-start.2 = ((f32[32,8,128]{2,1,0:T(8,128)}), f32[32,8,128]{2,1,0:T(8,128)S(1)}, u32[]{:S(2)}, u32[]{:S(2)}) async-start(f32[32,8,128]{2,1,0:T(8,128)} %bitcast.38), calls=%async_computation.2 | async-start | bytes 262144 | tf_op jit(solution)/shard_map/all_to_all | solution.py:584
  87.6 6.0 %copy-start.7 = (f32[32,8,128]{2,1,0:T(8,128)}, f32[32,8,128]{2,1,0:T(8,128)S(1)}, u32[]{:S(2)}) copy-start(f32[32,8,128]{2,1,0:T(8,128)S(1)} %all-to-all-done.2) | copy-start | bytes 393220
  87.6 18.9 %all-to-all-start = ((f32[32,8,128]{2,1,0:T(8,128)}), f32[32,8,128]{2,1,0:T(8,128)S(1)}, u32[]{:S(2)}, u32[]{:S(2)}) async-start(f32[32,8,128]{2,1,0:T(8,128)} %bitcast.43), calls=%async_computation | async-start | bytes 262144 | tf_op jit(solution)/shard_map/all_to_all | solution.py:584
  106.4 0.7 copy-start.8
  111.1 21.6 %all-to-all-start.3 = ((f32[32,32,128]{2,1,0:T(8,128)}), f32[32,32,128]{2,1,0:T(8,128)S(1)}, u32[]{:S(2)}, u32[]{:S(2)}) async-start(f32[32,32,128]{2,1,0:T(8,128)} %bitcast.31), calls=%async_computation.3 | async-start | bytes 1048576 | tf_op jit(solution)/shard_map/all_to_all | solution.py:584
  132.8 0.8 copy-start
  135.4 19.0 %all-to-all-start.4 = ((f32[32,24,128]{2,1,0:T(8,128)}), f32[32,24,128]{2,1,0:T(8,128)S(1)}, u32[]{:S(2)}, u32[]{:S(2)}) async-start(f32[32,24,128]{2,1,0:T(8,128)} %bitcast.34), calls=%async_computation.4 | async-start | bytes 786432 | tf_op jit(solution)/shard_map/all_to_all | solution.py:584
  154.4 0.8 copy-start.4

commit v2 on v1

--- a/solution.py
+++ b/solution.py
@@ -19,13 +19,14 @@
 SUB = 8
 
 
-def pack_kernel(dep_ref, fields_ref, xfirst_ref, xlast_ref, yfirst_ref, ylast_ref):
+def pack_kernel(mask_ref, depth_ref, fields_ref, dep_ref, xfirst_ref, xlast_ref, yfirst_ref, ylast_ref):
     field = pl.program_id(0)
     north, east = dep_ref.shape
     levels = fields_ref.shape[1] // north
     per = east // north
     blocks = levels // per
-    dep = dep_ref[...]
+    dep = jnp.where(mask_ref[...] == 1, depth_ref[...], 0)
+    dep_ref[...] = dep
     tiled = jnp.concatenate([dep] * per, 0)
     level_in_block = lax.broadcasted_iota(jnp.int32, (east, east), 0) // north
     for t in range(blocks):
@@ -60,7 +61,7 @@
             )
 
 
-def pack_edges(fields, dep):
+def pack_edges(fields, mask, depth):
     _, levels, north, east = fields.shape
     rows = FIELDS * levels * north // east + SUB
     x_shape = jax.ShapeDtypeStruct((HALO, rows, east), jnp.float32)
@@ -70,13 +71,14 @@
         pack_kernel,
         grid=(FIELDS,),
         in_specs=[
-            pl.BlockSpec((north, east), lambda f: (0, 0)),
+            whole(mask),
+            whole(depth),
             pl.BlockSpec((1, levels * north, east), lambda f: (f, 0, 0)),
         ],
-        out_specs=[whole(x_shape), whole(x_shape), whole(y_shape), whole(y_shape)],
-        out_shape=[x_shape, x_shape, y_shape, y_shape],
-        compiler_params=pltpu.CompilerParams(vmem_limit_bytes=VMEM_LIMIT),
-    )(dep, fields.reshape(FIELDS, levels * north, east))
+        out_specs=[whole(mask), whole(x_shape), whole(x_shape), whole(y_shape), whole(y_shape)],
+        out_shape=[jax.ShapeDtypeStruct(mask.shape, jnp.int32), x_shape, x_shape, y_shape, y_shape],
+        compiler_params=pltpu.CompilerParams(vmem_limit_bytes=52 << 20),
+    )(mask, depth, fields.reshape(FIELDS, levels * north, east))
 
 
 def face_flux(slopes, left, right, speed, share):
@@ -87,27 +89,28 @@
     e4 = jnp.where(ahead, dp1, dm1)
     near = jnp.where(ahead, left, right)
     bend0, bend1, bend2 = e2 - e1, d0 - e2, e4 - d0
-    twice2, twice3 = e2 + e2, d0 + d0
-    tilt0, tilt1, tilt2 = bend0 + twice2, e2 + d0, bend2 - twice3
+    tilt0, tilt1, tilt2 = bend0 + (e2 + e2), e2 + d0, bend2 - (d0 + d0)
     rough0 = bend0 * bend0 * (13.0 / 3.0) + (tilt0 * tilt0 + 4.0 * WENO_EPS)
     rough1 = bend1 * bend1 * (13.0 / 3.0) + (tilt1 * tilt1 + 4.0 * WENO_EPS)
     rough2 = bend2 * bend2 * (13.0 / 3.0) + (tilt2 * tilt2 + 4.0 * WENO_EPS)
     pair0, pair1, pair2 = rough1 * rough2, rough0 * rough2, rough0 * rough1
     g0, g1, g2 = pair0 * pair0, 6.0 * (pair1 * pair1), 3.0 * (pair2 * pair2)
-    total = g0 * (5.0 * e2 - (e1 + e1)) + g1 * (e2 + twice3) + g2 * (4.0 * d0 - e4)
+    total = g0 * (tilt0 + (bend0 + e2)) + g1 * (tilt1 + d0) + g2 * (d0 - tilt2)
     return speed * near + share * (total * pltpu.reciprocal(g0 + g1 + g2, approx=True))
 
 
 def advect_kernel(
-    tracers, staged, dep_ref, *refs,
+    tracers, staged, begin, filled, dep_ref, *refs,
 ):
     field_refs, refs = refs[: len(staged)], refs[len(staged) :]
-    xlo_ref, xhi_ref, ylo_ref, yhi_ref, _, adv_ref = refs[:6]
-    spread_ref = refs[6] if len(tracers) > 1 else None
+    xlo_ref, xhi_ref, ylo_ref, yhi_ref = refs[:4]
+    refs = refs[5 + filled :]
+    adv_ref = refs[0]
+    spread_ref = refs[1] if len(tracers) > 1 else None
     (
         deep, both, lines, slopes, fluxes, cells, wets, su, su6, sv, sv6, sides,
     ) = refs[-12:]
-    step = pl.program_id(0)
+    step = pl.program_id(0) + begin
     north, east = dep_ref.shape
     per = east // north
     blocks = SUB // per
@@ -118,7 +121,7 @@
     faces = range(0, east + SUB, SUB)
     first_level = step * SUB
 
-    @pl.when(step == 0)
+    @pl.when(step == begin)
     def _():
         depths = dep_ref[...].astype(jnp.float32)
         deep[SUB : SUB + east, :] = jnp.concatenate([depths] * per, 0).T
@@ -222,30 +225,32 @@
     lax.fori_loop(first, len(staged), advance_field, 0)
 
 
-def advect(fields, dep, tracers, edges, after):
+def advect(fields, dep, tracers, edges, span, after, filled=()):
     _, levels, north, east = fields.shape
     whole = lambda a: pl.BlockSpec(a.shape, lambda k: (0,) * a.ndim)
     staged = tracers if tracers[0] == 0 else (0, 1, *tracers)
-    one = lambda f: pl.BlockSpec((1, SUB * north, east), lambda k: (f, k, 0))
+    one = lambda f: pl.BlockSpec((1, SUB * north, east), lambda k: (f, k + span[0], 0))
     f32 = jnp.float32
     blocks = SUB * north // east
     flat = fields.reshape(FIELDS, levels * north, east)
-    out_specs = [pl.BlockSpec((len(tracers), north, SUB, east), lambda k: (0, 0, k, 0))]
+    out_specs = [pl.BlockSpec((len(tracers), north, SUB, east), lambda k: (0, 0, k + span[0], 0))]
     out_shape = [jax.ShapeDtypeStruct((len(tracers), north, levels, east), f32)]
     if tracers[0] == 0:
-        out_specs.append(pl.BlockSpec((north, SUB, east), lambda k: (0, k, 0)))
+        out_specs.append(pl.BlockSpec((north, SUB, east), lambda k: (0, k + span[0], 0)))
         out_shape.append(jax.ShapeDtypeStruct((north, levels, east), f32))
     return pl.pallas_call(
-        functools.partial(advect_kernel, tracers, staged),
-        grid=(levels // SUB,),
+        functools.partial(advect_kernel, tracers, staged, span[0], len(filled)),
+        grid=(span[1] - span[0],),
         in_specs=[
             whole(dep),
             *(one(f) for f in staged),
             *(whole(a) for a in edges),
             pl.BlockSpec(memory_space=pl.ANY),
+            *(pl.BlockSpec(memory_space=pl.ANY) for _ in filled),
         ],
         out_specs=out_specs,
         out_shape=out_shape,
+        input_output_aliases={len(staged) + 6 + i: i for i in range(len(filled))},
         scratch_shapes=[
             pltpu.VMEM((east + 2 * SUB, east), f32),
             pltpu.VMEM((east + SUB, east), f32),
@@ -261,7 +266,7 @@
             pltpu.VMEM((SUB * north, east), f32),
         ],
         compiler_params=pltpu.CompilerParams(vmem_limit_bytes=VMEM_LIMIT),
-    )(dep, *(flat for _ in staged), *edges, after)
+    )(dep, *(flat for _ in staged), *edges, after, *filled)
 
 
 def shift_both(axis, first, last):
@@ -271,13 +276,14 @@
     return lax.ppermute(last, axis, forward), lax.ppermute(first, axis, backward)
 
 
-def advance_edges(fields, dep):
-    xfirst, xlast, yfirst, ylast = pack_edges(fields, dep)
-    return (*shift_both("rows", xfirst, xlast), *shift_both("cols", yfirst, ylast))
+def advance_edges(fields, mask, depth):
+    dep, xfirst, xlast, yfirst, ylast = pack_edges(fields, mask, depth)
+    south_north = shift_both("cols", yfirst, ylast)
+    return (dep, *shift_both("rows", xfirst, xlast), *south_north)
 
 
 AXES = ("rows", "cols")
-VMEM_LIMIT = 60 << 20
+VMEM_LIMIT = 52 << 20
 TRACERS = (0, 1, 3, 4)
 PARTS = 4
 
@@ -328,13 +334,13 @@
         self.y_forward = left_factor(np.kron(cy, eye))
         self.y_back = left_factor(np.kron(cy.T, eye))
         self.x_forward, self.x_back = right_factor(cx.T), right_factor(cx)
-        take = np.zeros((north, east, 2 * north))
-        give = np.zeros((2 * north, north, east))
-        for k in range(north):
-            take[k, :, k], take[k, :, north + k] = cx[:, 0], cx[:, -1]
-            give[k, k], give[north + k, k] = -cx[:, -1], cx[:, 0]
-        self.take = np.concatenate(halves(take.reshape(north * east, 2 * north)), 1)
-        self.give = np.concatenate(halves(give.reshape(2 * north, north * east)), 0)
+        edges = np.zeros((2 * north, east))
+        edges[:north], edges[north:] = cx[:, 0], cx[:, -1]
+        self.take = np.concatenate(halves(edges.T), 1)
+        edges[:north], edges[north:] = -cx[:, -1], cx[:, 0]
+        give = np.concatenate(halves(edges), 0)
+        self.give = np.concatenate([give, give], 0)
+        assert 4 * north == east
         lanes = max(east, 2 * north)
         assert lanes == east and cols % SUB == 0
         grid = 1.0 / (shift[:, None, None] + ly[None, :, None] + lx[None, None, :])
@@ -422,35 +428,52 @@
     return 0.5 * (above - below)
 
 
-def local_solve(tables, spec, base_ref, x_ref, y_ref, take_ref, coef_ref, edge_ref):
+def pair_of(spec, m, rows):
+    return jnp.concatenate(
+        [spec[:, at : at + SUB, :].reshape(rows, -1) for at in (m, m + SUB)], 1
+    )
+
+
+def block_solve(tables, spec, base_ref, x_ref, y_ref, coef_ref):
     north, east, levels = tables.north, tables.east, tables.levels
     for y in range(0, north, 4):
         tile = spec[y : y + 4].reshape(4 * levels, east)
         spec[y : y + 4] = from_right(tile, x_ref[...]).reshape(4, levels, east)
-    for m in range(0, levels, SUB):
-        tile = from_left(y_ref[...], spec[:, m : m + SUB, :].reshape(north * SUB, east))
-        base = base_ref[m : m + SUB, :]
-        even = odd = jnp.zeros((SUB, east), jnp.float32)
-        for k in range(north):
-            value = tile[k * SUB : (k + 1) * SUB] / (base + tables.ly[k])
-            coef_ref[k, m : m + SUB, :] = value
-            if k % 2:
-                odd = odd + tables.south[k] * value
+    for m in range(0, levels, 2 * SUB):
+        both = from_left(y_ref[...], pair_of(spec, m, north * SUB))
+        for i in range(2):
+            at = m + i * SUB
+            base = base_ref[at : at + SUB, :]
+            tile = both[:, i * east : (i + 1) * east]
+            for k in range(north):
+                coef_ref[k, at : at + SUB, :] = tile[k * SUB : (k + 1) * SUB] / (
+                    base + tables.ly[k]
+                )
+
+
+def block_edges(tables, coef_ref, take_ref, edge_ref):
+    north, east, levels = tables.north, tables.east, tables.levels
+    zero = jnp.zeros((levels, east), jnp.float32)
+    even = odd = total = rest = zero
+    lane = lax.broadcasted_iota(jnp.int32, (levels, east), 1)
+    place = lane % north
+    for k in range(0, north, 4):
+        group = coef_ref[k : k + 4]
+        high, low = parts(group.reshape(4 * levels, east))
+        high, low = mul(high, take_ref[...]), mul(low, take_ref[...])
+        for i in range(4):
+            value = tables.south[k + i] * group[i]
+            if i % 2:
+                odd = odd + value
             else:
-                even = even + tables.south[k] * value
-        edge_ref[pl.ds(PARTS * m + 1, SUB, stride=PARTS), :] = even + odd
-        edge_ref[pl.ds(PARTS * m + 2, SUB, stride=PARTS), :] = even - odd
-    total = jnp.zeros((levels, east), jnp.float32)
-    rest = total
-    for k in range(north):
-        high, low = parts(coef_ref[k])
-        factor = take_ref[k * east : (k + 1) * east, :]
-        total = total + mul(high, factor)
-        rest = rest + mul(low, factor)
-    lane = lax.broadcasted_iota(jnp.int32, total.shape, 1)
+                even = even + value
+            mine = place == k + i
+            total = total + jnp.where(mine, high[i * levels : (i + 1) * levels], 0.0)
+            rest = rest + jnp.where(mine, low[i * levels : (i + 1) * levels], 0.0)
     total = total + pltpu.roll(total, east // 2, 1) + rest
-    edge_ref[pl.ds(0, levels, stride=PARTS), :] = jnp.where(lane < 2 * north, total, 0.0)
-    edge_ref[pl.ds(PARTS - 1, levels, stride=PARTS), :] = jnp.zeros_like(total)
+    sides = (jnp.where(lane < 2 * north, total, 0.0), even + odd, even - odd, zero)
+    for part in range(PARTS):
+        edge_ref[pl.ds(part, levels, stride=PARTS), :] = sides[part]
     if edge_ref.shape[0] > levels * PARTS:
         edge_ref[levels * PARTS :, :] = jnp.zeros_like(edge_ref[levels * PARTS :, :])
 
@@ -460,18 +483,23 @@
     side, ahead, behind = (
         jump_ref[pl.ds(part, levels, stride=PARTS), :] for part in range(PARTS - 1)
     )
-    both = side + pltpu.roll(side, east // 2, 1)
-    side_high, side_low = parts(side)
-    both = both.astype(jnp.bfloat16)
-    half = 2 * north
-    for k in range(north):
-        lanes = slice(k * east, (k + 1) * east)
-        change = mul(both, give_ref[:, lanes]) + mul(side_low[:, :half], give_ref[:half, lanes])
-        change = change + (tables.south[k] * behind - tables.north_edge[k] * ahead)
-        spec[k] = coef_ref[k] + change / (base_ref[...] + tables.ly[k])
-    for m in range(0, levels, SUB):
-        tile = from_left(y_ref[...], spec[:, m : m + SUB, :].reshape(north * SUB, east))
-        spec[:, m : m + SUB, :] = tile.reshape(north, SUB, east)
+    high, low = (half.astype(jnp.float32) for half in parts(side))
+    sides = jnp.concatenate([high + pltpu.roll(high, east // 2, 1), low], 1)
+    place = lax.broadcasted_iota(jnp.int32, sides.shape, 1) % north
+    for k in range(0, north, 4):
+        picked = [jnp.where(place == k + i, sides, 0.0).astype(jnp.bfloat16) for i in range(4)]
+        change = mul(jnp.concatenate(picked, 0), give_ref[...])
+        for i in range(4):
+            value = change[i * levels : (i + 1) * levels] + (
+                tables.south[k + i] * behind - tables.north_edge[k + i] * ahead
+            )
+            spec[k + i] = coef_ref[k + i] + value / (base_ref[...] + tables.ly[k + i])
+    for m in range(0, levels, 2 * SUB):
+        both = from_left(y_ref[...], pair_of(spec, m, north * SUB))
+        for i in range(2):
+            at = m + i * SUB
+            tile = both[:, i * east : (i + 1) * east]
+            spec[:, at : at + SUB, :] = tile.reshape(north, SUB, east)
     for y in range(0, north, 4):
         tile = from_right(spec[y : y + 4].reshape(4 * levels, east), x_ref[...])
         tile = jnp.concatenate([tile[k * levels : (k + 1) * levels] for k in range(4)], 1)
@@ -485,9 +513,10 @@
     strip_ref, column_ref, lines_ref, *rest,
 ):
     del device_ref
-    extra_ref, jump_ref = rest
+    extra_ref, jump_ref = rest[0], rest[-1]
     rows, cols, east, north = tables.rows, tables.cols, tables.east, tables.north
     each = jump_ref.shape[0] // tables.count
+    every_in = edge_ref.shape[0] // tables.count
     if each > tables.share * PARTS:
         more = extra_ref.shape[0] // tables.count
         for d in range(tables.count):
@@ -513,7 +542,7 @@
     for m in range(share):
         west, south, top = (
             [
-                edge_ref[pl.ds((a * cols * share + m) * PARTS + part, cols, stride=share * PARTS), :]
+                edge_ref[pl.ds(a * cols * every_in + m * PARTS + part, cols, stride=every_in), :]
                 for a in range(rows)
             ]
             for part in range(PARTS - 1)
@@ -576,15 +605,15 @@
     return pl.BlockSpec(shape, lambda *_: (0,) * len(shape))
 
 
-def call_params():
-    return pltpu.CompilerParams(vmem_limit_bytes=VMEM_LIMIT)
+def call_params(limit=VMEM_LIMIT):
+    return pltpu.CompilerParams(vmem_limit_bytes=limit)
 
 
 def exchange(block):
     return lax.all_to_all(block, AXES, split_axis=0, concat_axis=0, tiled=True)
 
 
-def interface(tables, received, extra, travels):
+def interface(tables, received, extra, travels, limit, *after):
     device = lax.axis_index("rows") * lax.axis_size("cols") + lax.axis_index("cols")
     operands = (
         received, tables.cross, tables.along, tables.sines, tables.wide_forward, tables.wide_back,
@@ -604,18 +633,18 @@
             in_specs=[
                 *specs,
                 whole_spec(extra) if travels else pl.BlockSpec(memory_space=pl.ANY),
+                *(pl.BlockSpec(memory_space=pl.ANY) for _ in after),
             ],
             out_specs=whole_spec(shape),
         ),
         out_shape=shape,
-        compiler_params=call_params(),
-    )(device.astype(jnp.int32).reshape(1), *operands, extra)
+        compiler_params=call_params(limit),
+    )(device.astype(jnp.int32).reshape(1), *operands, extra, *after)
 
 
 def adjoint_kernel(
-    tables, dep_ref, cot_ref, z_ref, base_ref, x_ref, y_ref, take_ref, *rest,
+    tables, dep_ref, cot_ref, z_ref, base_ref, x_ref, y_ref, coef_ref, spec
 ):
-    coef_ref, edge_ref, spec = rest[-3:]
     north, east, levels = tables.north, tables.east, tables.levels
     level = lax.broadcasted_iota(jnp.int32, (levels, east), 0)
     for y in range(0, north, 4):
@@ -627,7 +656,7 @@
         tile = from_left(z_ref[...], jnp.concatenate(tiles, 1))
         for k in range(4):
             spec[y + k] = tile[:, k * east : (k + 1) * east]
-    local_solve(tables, spec, base_ref, x_ref, y_ref, take_ref, coef_ref, edge_ref)
+    block_solve(tables, spec, base_ref, x_ref, y_ref, coef_ref)
 
 
 def solve_shapes(tables):
@@ -636,10 +665,10 @@
     return [coef, edge]
 
 
-def adjoint_local(tables, cotangent, dep, *after):
+def adjoint_local(tables, cotangent, dep):
     levels, north, east = tables.levels, tables.north, tables.east
-    consts = (tables.z_forward, tables.base, tables.x_forward, tables.y_forward, tables.take)
-    shapes = solve_shapes(tables)
+    consts = (tables.z_forward, tables.base, tables.x_forward, tables.y_forward)
+    coef = solve_shapes(tables)[0]
     return pl.pallas_call(
         functools.partial(adjoint_kernel, tables),
         grid=(1,),
@@ -647,13 +676,32 @@
             whole_spec(dep),
             pl.BlockSpec((1, levels * north, east), lambda k: (2, 0, 0)),
             *(whole_spec(a) for a in consts),
+        ],
+        out_specs=whole_spec(coef),
+        out_shape=coef,
+        scratch_shapes=[pltpu.VMEM(coef.shape, jnp.float32)],
+        compiler_params=call_params(52 << 20),
+    )(dep, cotangent.reshape(FIELDS, levels * north, east), *consts)
+
+
+def edges_kernel(tables, coef_ref, take_ref, *rest):
+    block_edges(tables, coef_ref, take_ref, rest[-1])
+
+
+def adjoint_edges(tables, coef, *after):
+    edge = solve_shapes(tables)[1]
+    return pl.pallas_call(
+        functools.partial(edges_kernel, tables),
+        grid=(1,),
+        in_specs=[
+            whole_spec(coef),
+            whole_spec(tables.take),
             *(pl.BlockSpec(memory_space=pl.ANY) for _ in after),
         ],
-        out_specs=[whole_spec(a) for a in shapes],
-        out_shape=shapes,
-        scratch_shapes=[pltpu.VMEM(shapes[0].shape, jnp.float32)],
+        out_specs=whole_spec(edge),
+        out_shape=edge,
         compiler_params=call_params(),
-    )(dep, cotangent.reshape(FIELDS, levels * north, east), *consts, *after)
+    )(coef, tables.take, *after)
 
 
 def set_weights(w_in_ref, bias_ref, w_ref, w_in, bias, w, w_out, levels):
@@ -687,20 +735,35 @@
 
 
 def column_kernel(
-    tables, dep_ref, adv_ref, spread_ref, w_field_ref, w_in_ref, bias_ref, w_ref,
-    z_ref, base_ref, x_ref, y_ref, take_ref,
-    mixed_ref, coef_ref, edge_ref,
-    spec, feats, hidden, flat, w_in, bias, w, w_out,
+    tables, dep_ref, adv_ref, spread_ref, w_field_ref, heat_ref, salt_ref,
+    w_in_ref, bias_ref, w_ref, back_coef_ref, back_jump_ref,
+    z_ref, base_ref, x_ref, y_ref, take_ref, y_back_ref, x_back_ref, z_back_ref, give_ref,
+    mixed_ref, coef_ref, sides, total_ref,
+    spec, back, feats, activity, hidden, grads, flat,
+    w_in, bias, w, w_out, g_in_ref, g_bias_ref, g_out_ref,
 ):
     step = pl.program_id(0)
     north, east, levels = tables.north, tables.east, tables.levels
+    f32, bf16 = jnp.float32, jnp.bfloat16
 
     @pl.when(step == 0)
     def _():
         set_weights(w_in_ref, bias_ref, w_ref, w_in, bias, w, w_out, levels)
-
-    rates = closure(adv_ref, w_in, bias, w_out, feats, None, hidden)
-    flat[...] = w_field_ref[0].reshape(levels * SUB, east)
+        g_in_ref[...] = jnp.zeros_like(g_in_ref)
+        g_out_ref[...] = jnp.zeros_like(g_out_ref)
+        g_bias_ref[...] = jnp.zeros_like(g_bias_ref)
+
+        def use(y, tile):
+            back[y] = tile
+
+        finish_solve(
+            tables, spec, back_coef_ref, back_jump_ref, base_ref, y_back_ref, x_back_ref,
+            z_back_ref, give_ref, use,
+        )
+
+    rates = closure(adv_ref, w_in, bias, w_out, feats, activity, hidden)
+    for i, ref in enumerate((heat_ref, salt_ref, w_field_ref)):
+        flat[i] = ref[0].reshape(levels * SUB, east)
     level = lax.broadcasted_iota(jnp.int32, (levels, east), 0)
     depths = dep_ref[pl.ds(pl.multiple_of(step * SUB, SUB), SUB), :]
     sources = []
@@ -708,15 +771,23 @@
         lanes = slice(k * east, (k + 1) * east)
         depth = depths[k : k + 1]
         wet = level < depth
-        flow = jnp.where(level + 1 < depth, TIME_STEP, 0.0) * rates[:, lanes]
+        rate = rates[:, lanes]
+        flow = jnp.where(level + 1 < depth, TIME_STEP, 0.0) * rate
+        slope = -vertical_change(jnp.where(wet, back[step * SUB + k], 0.0))
         mixed = []
-        for i in range(2):
+        total = jnp.zeros((levels, east), f32)
+        for i, share in ((0, THERMAL), (1, -HALINE)):
             value = adv_ref[2 + i, k]
-            flux = flow * (pltpu.roll(value, levels - 1, 0) - value)
+            drop = pltpu.roll(value, levels - 1, 0) - value
+            grad = flat[i, pl.ds(k, levels, stride=SUB), :] + share * slope
+            grad = jnp.where(wet, grad, 0.0)
+            total = total + (grad - pltpu.roll(grad, levels - 1, 0)) * drop
+            flux = flow * drop
             value = jnp.where(wet, value + (flux - pltpu.roll(flux, 1, 0)), 0.0)
             mixed.append(value)
             mixed_ref[i, k] = value
-        rise = jnp.where(wet, flat[pl.ds(k, levels, stride=SUB), :], 0.0)
+        grads[:, lanes] = (total * flow * (1.0 - rate * (1.0 / RATE_MAX))).astype(bf16)
+        rise = jnp.where(wet, flat[2, pl.ds(k, levels, stride=SUB), :], 0.0)
         density = THERMAL * mixed[0] - HALINE * mixed[1] - rise * (1.0 / TIME_STEP)
         source = vertical_change(density) - spread_ref[k] * (1.0 / TIME_STEP)
         sources.append(jnp.where(wet, source, 0.0))
@@ -724,104 +795,6 @@
     for k in range(SUB):
         spec[step * SUB + k] = tile[:, k * east : (k + 1) * east]
 
-    @pl.when(step == north // SUB - 1)
-    def _():
-        local_solve(tables, spec, base_ref, x_ref, y_ref, take_ref, coef_ref, edge_ref)
-
-
-def closure_scratch(levels, east, inputs, hidden):
-    f32, bf16 = jnp.float32, jnp.bfloat16
-    return [
-        pltpu.VMEM((hidden, inputs), bf16),
-        pltpu.VMEM((hidden, east), f32),
-        pltpu.VMEM((hidden, east), f32),
-        pltpu.VMEM((levels, hidden), bf16),
-    ]
-
-
-def column(tables, dep, adv, spread, fields, in_weight, in_bias, out_weight):
-    levels, north, east = tables.levels, tables.north, tables.east
-    inputs, hidden = in_weight.shape
-    f32, bf16 = jnp.float32, jnp.bfloat16
-    consts = (
-        in_weight, in_bias, out_weight,
-        tables.z_forward, tables.base, tables.x_forward, tables.y_forward, tables.take,
-    )
-    mixed = jax.ShapeDtypeStruct((2, north, levels, east), f32)
-    shapes = solve_shapes(tables)
-    lanes = SUB * east
-    return pl.pallas_call(
-        functools.partial(column_kernel, tables),
-        grid=(north // SUB,),
-        in_specs=[
-            whole_spec(dep),
-            pl.BlockSpec((len(TRACERS), SUB, levels, east), lambda k: (0, k, 0, 0)),
-            pl.BlockSpec((SUB, levels, east), lambda k: (k, 0, 0)),
-            pl.BlockSpec((1, levels, SUB, east), lambda k: (2, 0, k, 0)),
-            *(whole_spec(a) for a in consts),
-        ],
-        out_specs=[
-            pl.BlockSpec((2, SUB, levels, east), lambda k: (0, k, 0, 0)),
-            *(whole_spec(a) for a in shapes),
-        ],
-        out_shape=[mixed, *shapes],
-        scratch_shapes=[
-            pltpu.VMEM(shapes[0].shape, f32),
-            pltpu.VMEM((inputs, lanes), bf16),
-            pltpu.VMEM((hidden, lanes), bf16),
-            pltpu.VMEM((levels * SUB, east), f32),
-            *closure_scratch(levels, east, inputs, hidden),
-        ],
-        compiler_params=call_params(),
-    )(dep, adv, spread, fields, *consts)
-
-
-def gradient_kernel(
-    tables, dep_ref, adv_ref, heat_ref, salt_ref, w_in_ref, bias_ref, w_ref,
-    coef_ref, jump_ref, base_ref, y_ref, x_ref, z_ref, give_ref, after_ref,
-    total_ref,
-    spec, back, feats, activity, hidden, grads, cots, w_in, bias, w, w_out,
-    g_in_ref, g_bias_ref, g_out_ref,
-):
-    del after_ref
-    step = pl.program_id(0)
-    north, east, levels = tables.north, tables.east, tables.levels
-    f32, bf16 = jnp.float32, jnp.bfloat16
-
-    @pl.when(step == 0)
-    def _():
-        set_weights(w_in_ref, bias_ref, w_ref, w_in, bias, w, w_out, levels)
-        g_in_ref[...] = jnp.zeros_like(g_in_ref)
-        g_out_ref[...] = jnp.zeros_like(g_out_ref)
-        g_bias_ref[...] = jnp.zeros_like(g_bias_ref)
-
-        def use(y, tile):
-            back[y] = tile
-
-        finish_solve(
-            tables, spec, coef_ref, jump_ref, base_ref, y_ref, x_ref, z_ref, give_ref, use
-        )
-
-    rates = closure(adv_ref, w_in, bias, w_out, feats, activity, hidden)
-    cots[0] = heat_ref[0].reshape(levels * SUB, east)
-    cots[1] = salt_ref[0].reshape(levels * SUB, east)
-    level = lax.broadcasted_iota(jnp.int32, (levels, east), 0)
-    depths = dep_ref[pl.ds(pl.multiple_of(step * SUB, SUB), SUB), :]
-    for k in range(SUB):
-        lanes = slice(k * east, (k + 1) * east)
-        depth = depths[k : k + 1]
-        wet = level < depth
-        rate = rates[:, lanes]
-        flow = jnp.where(level + 1 < depth, TIME_STEP, 0.0) * rate
-        slope = -vertical_change(jnp.where(wet, back[step * SUB + k], 0.0))
-        total = jnp.zeros((levels, east), f32)
-        for i, share in ((0, THERMAL), (1, -HALINE)):
-            value = adv_ref[2 + i, k]
-            drop = pltpu.roll(value, levels - 1, 0) - value
-            grad = cots[i, pl.ds(k, levels, stride=SUB), :] + share * slope
-            grad = jnp.where(wet, grad, 0.0)
-            total = total + (grad - pltpu.roll(grad, levels - 1, 0)) * drop
-        grads[:, lanes] = (total * flow * (1.0 - rate * (1.0 / RATE_MAX))).astype(bf16)
     over = (((1,), (1,)), ((), ()))
     grad = grads[...]
     g_out_ref[...] += lax.dot_general(hidden[...], grad, over, preferred_element_type=f32)
@@ -836,6 +809,8 @@
 
     @pl.when(step == north // SUB - 1)
     def _():
+        block_solve(tables, spec, base_ref, x_ref, y_ref, coef_ref)
+        block_edges(tables, coef_ref, take_ref, sides)
         inputs, width = g_in_ref.shape
         for k in range(width // east):
             total_ref[k * inputs : (k + 1) * inputs, :] = g_in_ref[:, k * east : (k + 1) * east]
@@ -844,31 +819,48 @@
         at = inputs * width // east
         for k in range(0, width, east):
             total_ref[at + k : at + k + east, :] = last[k : k + east].T
-
-
-def gradients(tables, dep, adv, cotangent, in_weight, in_bias, out_weight, coef, jumps, after):
+        if total_ref.shape[0] > at + width:
+            total_ref[at + width :, :] = jnp.zeros_like(total_ref[at + width :, :])
+
+
+def column(
+    tables, dep, adv, spread, fields, cotangent, in_weight, in_bias, out_weight, coef, jumps
+):
     levels, north, east = tables.levels, tables.north, tables.east
     inputs, hidden = in_weight.shape
     f32, bf16 = jnp.float32, jnp.bfloat16
-    field = lambda f: pl.BlockSpec((1, levels, SUB, east), lambda k: (f, 0, k, 0))
-    consts = (in_weight, in_bias, out_weight, coef, jumps, *solve_consts(tables))
+    consts = (
+        in_weight, in_bias, out_weight, coef, jumps,
+        tables.z_forward, tables.base, tables.x_forward, tables.y_forward, tables.take,
+        tables.y_back, tables.x_back, tables.z_back, tables.give,
+    )
+    mixed = jax.ShapeDtypeStruct((2, north, levels, east), f32)
+    coef, edge = solve_shapes(tables)
     rows = inputs * hidden // east + hidden
     assert 2 * levels == east
-    total = jax.ShapeDtypeStruct((-(-rows // tables.count) * tables.count, east), f32)
+    rows = -(-rows // tables.count) * tables.count
+    total = jax.ShapeDtypeStruct((rows, east), f32)
     lanes = SUB * east
+    field = lambda f: pl.BlockSpec((1, levels, SUB, east), lambda k: (f, 0, k, 0))
     return pl.pallas_call(
-        functools.partial(gradient_kernel, tables),
+        functools.partial(column_kernel, tables),
         grid=(north // SUB,),
         in_specs=[
             whole_spec(dep),
             pl.BlockSpec((len(TRACERS), SUB, levels, east), lambda k: (0, k, 0, 0)),
+            pl.BlockSpec((SUB, levels, east), lambda k: (k, 0, 0)),
+            field(2),
             field(3),
             field(4),
             *(whole_spec(a) for a in consts),
-            pl.BlockSpec(memory_space=pl.ANY),
         ],
-        out_specs=whole_spec(total),
-        out_shape=total,
+        out_specs=[
+            pl.BlockSpec((2, SUB, levels, east), lambda k: (0, k, 0, 0)),
+            whole_spec(coef),
+            whole_spec(edge),
+            whole_spec(total),
+        ],
+        out_shape=[mixed, coef, edge, total],
         scratch_shapes=[
             pltpu.VMEM(coef.shape, f32),
             pltpu.VMEM(coef.shape, f32),
@@ -876,14 +868,17 @@
             pltpu.VMEM((hidden, lanes), f32),
             pltpu.VMEM((hidden, lanes), bf16),
             pltpu.VMEM((levels, lanes), bf16),
-            pltpu.VMEM((2, levels * SUB, east), f32),
-            *closure_scratch(levels, east, inputs, hidden),
+            pltpu.VMEM((3, levels * SUB, east), f32),
+            pltpu.VMEM((hidden, inputs), bf16),
+            pltpu.VMEM((hidden, east), f32),
+            pltpu.VMEM((hidden, east), f32),
+            pltpu.VMEM((levels, hidden), bf16),
             pltpu.VMEM((inputs, hidden), f32),
             pltpu.VMEM((hidden, east), f32),
             pltpu.VMEM((hidden, levels), f32),
         ],
         compiler_params=call_params(),
-    )(dep, adv, cotangent, cotangent, *consts, after)
+    )(dep, adv, spread, fields, cotangent, cotangent, *consts)
 
 
 def gather_kernel(adv_ref, mixed_ref, after_ref, new_ref, flat):
@@ -1023,25 +1018,27 @@
 def per_device(fields, cotangent, ocean_mask, depth_levels, in_weight, in_bias, out_weight):
     _, levels, north, east = fields.shape
     tables = Tables(levels, north, east, lax.axis_size("rows"), lax.axis_size("cols"))
-    dep = jnp.where(ocean_mask == 1, depth_levels, 0)
     inputs, hidden = in_weight.shape
     outputs = out_weight.shape[1]
     in_bias = in_bias.reshape(1, hidden)
     out_weight = out_weight.T
-    edges = advance_edges(fields, dep)
-    back_coef, back_edges = adjoint_local(tables, cotangent, dep, edges[0], edges[1])
-    adv, spread = advect(fields, dep, TRACERS, edges, edges[0])
-    back_jumps = exchange(interface(tables, exchange(back_edges), adv, False))
-    mixed, coef, sides = column(tables, dep, adv, spread, fields, in_weight, in_bias, out_weight)
+    steps = levels // SUB
+    dep, *edges = advance_edges(fields, ocean_mask, depth_levels)
+    back_coef = adjoint_local(tables, cotangent, dep)
+    back_edges = adjoint_edges(tables, back_coef, edges[0], edges[1])
+    half = advect(fields, dep, TRACERS, edges, (0, steps // 2), back_edges)
+    back_jumps = interface(tables, exchange(back_edges), half[1], False, 52 << 20)
+    adv, spread = advect(fields, dep, TRACERS, edges, (steps // 2, steps), back_jumps, half)
+    mixed, coef, sides, grads = column(
+        tables, dep, adv, spread, fields, cotangent, in_weight, in_bias, out_weight,
+        back_coef, exchange(back_jumps),
+    )
     received = exchange(sides)
-    grads = gradients(
-        tables, dep, adv, cotangent, in_weight, in_bias, out_weight, back_coef, back_jumps, coef
-    )
-    jumps_out = interface(tables, received, grads, True)
+    new = gather_fields(adv, mixed, coef)
+    jumps_out = interface(tables, received, grads, True, VMEM_LIMIT, new)
+    w = advect(fields, dep, (2,), edges, (0, steps), jumps_out)[0]
     jumps = exchange(jumps_out)
-    w = advect(fields, dep, (2,), edges, jumps_out)[0]
-    new = gather_fields(adv, mixed, jumps_out)
-    sums = exchange(sum_pieces(tables, jumps, w, new))
+    sums = exchange(sum_pieces(tables, jumps, w))
     pressure, new_fields = pressure_finish(tables, dep, w, new, coef, jumps)
     return (new_fields, pressure, *split_sums(sums, inputs, hidden, outputs))
 

time: 158 us -> 147 us (0.930)
  Pallas kernels: 98.3 us -> 86.3 us
  waiting for transfers between devices: 11.8 us -> 16.3 us
  starting transfers between devices: 39.6 us -> 35.7 us
    pallas_call x4 -> x5, Pallas kernels: 57.9 us -> 46.6 us  [the longest x3 39.4 us: advect(): pl.pallas_call(functools.partial(advect_kernel, tracers, staged, span[0],...]
    all_to_all x5, waiting for transfers between devices: 5.64 us -> 13.8 us  [exchange(): return lax.all_to_all(block, AXES, split_axis=0, concat_axis=0, tiled=True)]
    pallas_call x1, Pallas kernels: 10.5 us -> 15.6 us  [column(): pl.pallas_call(functools.partial(column_kernel, tables), grid=(north // S...]
    all_to_all x5, starting transfers between devices: 30.4 us -> 26.4 us  [exchange(): return lax.all_to_all(block, AXES, split_axis=0, concat_axis=0, tiled=True)]
    pallas_call x1, Pallas kernels: 5.53 us -> 3.35 us  [adjoint_local(): pl.pallas_call(functools.partial(adjoint_kernel, tables), grid=(1,), in_s...]
    ppermute x2, waiting for transfers between devices: 4.57 us -> 2.5 us  [shift_both(): lax.ppermute(first, axis, backward)]
    unnamed x18 -> x62, local copies, waits for them, and re-layouts: 5.11 us -> 6.64 us
  transfers between devices with their start and end apart: 9 -> 9, of which waited for: 3 -> 4; matrix products, arithmetic and copies ran while one was open for 0% -> 0% of each run, Pallas kernels for 51% -> 38%
where the time goes in v2:
time: 147 us; the launch traced here: 146 us
  Pallas kernels  86.3 us (59%)
  starting transfers between devices  35.7 us (24%)
  waiting for transfers between devices  16.3 us (11%)
  local copies, waits for them, and re-layouts  6.64 us (5%)
    pallas_call x3, Pallas kernels, advect(): pl.pallas_call(functools.partial(advect_kernel, tracers, staged, span[0],...  39.4 us
    all_to_all x5, starting transfers between devices, exchange(): return lax.all_to_all(block, AXES, split_axis=0, concat_axis=0, tiled=True)  26.4 us
    pallas_call x1, Pallas kernels, column(): pl.pallas_call(functools.partial(column_kernel, tables), grid=(north // S...  15.6 us
    all_to_all x5, waiting for transfers between devices, exchange(): return lax.all_to_all(block, AXES, split_axis=0, concat_axis=0, tiled=True)  13.8 us
    pallas_call x2, Pallas kernels, interface(): pl.pallas_call(functools.partial(interface_kernel, tables), grid_spec=plt...  7.49 us
    ppermute x2, starting transfers between devices, shift_both(): lax.ppermute(last, axis, forward)  6.69 us
    unnamed x62, local copies, waits for them, and re-layouts  6.64 us
    pallas_call x1, Pallas kernels, pressure_finish(): pl.pallas_call(functools.partial(pressure_kernel, tables), grid=(1,), in_...  6.31 us
  transfers between devices with their start and end apart: 9, of which 4 were waited for; matrix products, arithmetic and copies ran while one was open for 0% of the time, Pallas kernels for 38%

profile of v2, /device:TPU:0, one launch (start us, length us, event | category | flops | bytes accessed | tf_op | source)
XLA Modules:
  0.0 146.0 jit_solution(2979666134306900704)
XLA Ops:
  0.6 0.0 copy-start.15
  0.6 0.0 copy-start.7
  0.7 0.0 copy-start.11
  0.7 0.0 copy-start.21
  0.7 0.8 copy-done.27
  1.4 0.7 copy-done.28
  2.2 6.0 %shard_map.263 = (s32[32,128]{1,0:T(8,128)S(1)}, f32[3,88,128]{2,1,0:T(8,128)S(1)}, f32[3,88,128]{2,1,0:T(8,128)S(1)}, f32[968,128]{1,0:T(8,128)}, f32[968,128]{1,0:T(8,128)}) custom-call(s32[32,128]{1,0:T(8,128)S(1)} %copy-done.27, s32[32,128]{1,0:T(8,128)S(1)} %copy-done.28, f32[5,2048,128]{2,1,0:T(8,128)} %bitcast.27), custom_call_target="tpu_custom_call" | custom-call | tf_op jit(solution)/shard_map/pallas_call | solution.py:70
  8.2 2.4 %collective-permute-start.2 = (f32[968,128]{1,0:T(8,128)}, f32[968,128]{1,0:T(8,128)S(1)}, u32[]{:S(2)}, u32[]{:S(2)}) collective-permute-start(f32[968,128]{1,0:T(8,128)} %get-tuple-element.26), channel_id=1, source_target_pairs={{0,1},{1,2},{2,3},{3,4},{4,5},{5,6},{6,7},{8,9},{9,10},{10,11},{11... | collective-permute-start | bytes 1486856 | tf_op jit(solution)/shard_map/ppermute | solution.py:276
  10.6 1.3 collective-permute-start.3
  11.8 4.3 %collective-permute-start = (f32[3,88,128]{2,1,0:T(8,128)S(1)}, f32[3,88,128]{2,1,0:T(8,128)S(1)}, u32[]{:S(2)}, u32[]{:S(2)}) collective-permute-start(f32[3,88,128]{2,1,0:T(8,128)S(1)} %get-tuple-element.24), channel_id=1, source_target_pairs={{0,8},{8,16},{16,24},{1,9},{9,17},{17,25},{2,10},{10,18},{18,26},{... | collective-permute-start | bytes 405512 | tf_op jit(solution)/shard_map/ppermute | solution.py:276
  16.2 1.3 collective-permute-start.1
  17.5 3.3 %shard_map.264.coef_ref.back_coef_ref = f32[32,64,128]{2,1,0:T(8,128)S(1)} custom-call(s32[32,128]{1,0:T(8,128)S(1)} %get-tuple-element.23.dep_ref, f32[5,2048,128]{2,1,0:T(8,128)} %bitcast.39, bf16[128,64]{1,0:T(8,128)(2,1)S(1)} %copy-done.21, f32[64,128]{1,0:T(8,128)S(1)} %copy-done.15, bf16[256,256]{1,0:T(8,128)(2,1)S(1)} %copy-done.11, ...), custom_call_target="tpu_custom_call" | custom-call | tf_op jit(solution)/shard_map/pallas_call | solution.py:672
  20.9 0.0 copy-start
  20.9 0.0 collective-permute-done.rest_0_.refs_4_.refs_3_
  20.9 2.5 %collective-permute-done.1.rest_1_.refs_5_.refs_4_ = f32[3,88,128]{2,1,0:T(8,128)S(1)} collective-permute-done((f32[3,88,128]{2,1,0:T(8,128)S(1)}, f32[3,88,128]{2,1,0:T(8,128)S(1)}, u32[]{:S(2)}, u32[]{:S(2)}) %collective-permute-start.1) | collective-permute-done | bytes 135200 | tf_op jit(solution)/shard_map/ppermute | solution.py:276
  23.4 0.0 copy-done.23
  23.4 1.2 shard_map.265.refs_8_
  24.6 7.2 %all-to-all-start = ((f32[32,8,128]{2,1,0:T(8,128)}), f32[32,8,128]{2,1,0:T(8,128)}, u32[]{:S(2)}, u32[]{:S(2)}) async-start(f32[32,8,128]{2,1,0:T(8,128)} %bitcast.3), calls=%async_computation | async-start | bytes 262144 | tf_op jit(solution)/shard_map/all_to_all | solution.py:613
  31.7 0.0 copy-start.3
  31.7 0.0 copy-start.10
  31.8 0.0 copy-start.26
  31.8 0.0 copy-start.29
  31.8 0.0 collective-permute-done.2.refs_6_.refs_5_
  31.8 0.0 collective-permute-done.3.refs_7_.refs_6_
  31.8 14.7 %shard_map.266 = (f32[4,32,64,128]{3,2,1,0:T(8,128)}, f32[32,64,128]{2,1,0:T(8,128)}) custom-call(s32[32,128]{1,0:T(8,128)S(1)} %get-tuple-element.23.dep_ref, f32[5,2048,128]{2,1,0:T(8,128)} %bitcast.28, f32[5,2048,128]{2,1,0:T(8,128)} %bitcast.29, f32[5,2048,128]{2,1,0:T(8,128)} %bitcast.30, f32[5,2048,128]{2,1,0:T(8,128)} %bitcast.31, ...), custom_call_target="tpu_custom_call" | custom-call | tf_op jit(solution)/shard_map/pallas_call | solution.py:241
  46.5 0.0 copy-done
  46.5 0.0 all-to-all-done
  46.5 0.0 copy-done.3
  46.5 0.0 copy-done.10
  46.5 0.0 copy-done.26
  46.6 0.0 copy-start.4
  46.6 1.0 copy-done.4
  47.6 0.8 copy-done.17
  48.4 3.7 %shard_map.267.refs_8_ = f32[256,128]{1,0:T(8,128)} custom-call(s32[1]{0:T(128)} %bitcast.1.device_ref, f32[256,128]{1,0:T(8,128)} %bitcast.4.edge_ref, f32[64,10,128]{2,1,0:T(8,128)S(1)} %copy-done.4, f32[64,8,512]{2,1,0:T(8,128)S(1)} %copy-done.3, f32[16,16]{1,0:T(8,128)S(1)} %copy-done.26, bf16[2,512,512]{2,1,0:T(8,128)(2,1)} %constant.52.clone.forward_ref, ...), custom_call_target="tpu_custom_call" | custom-call | tf_op jit(solution)/shard_map/pallas_call | solution.py:628
  52.1 5.9 %all-to-all-start.1 = ((f32[32,8,128]{2,1,0:T(8,128)}), f32[32,8,128]{2,1,0:T(8,128)S(1)}, u32[]{:S(2)}, u32[]{:S(2)}) async-start(f32[32,8,128]{2,1,0:T(8,128)} %bitcast.7), calls=%async_computation.1 | async-start | bytes 262144 | tf_op jit(solution)/shard_map/all_to_all | solution.py:613
  58.0 0.0 copy-start.6
  58.0 0.0 copy-start.8
  58.0 0.0 copy-start.9
  58.1 0.0 copy-start.12
  58.1 0.0 copy-start.16
  58.1 0.0 copy-start.19
  58.1 0.0 copy-start.20
  58.1 0.0 copy-start.22
  58.1 0.0 copy-start.24
  58.1 0.0 copy-start.25
  58.1 0.0 copy-start.30
  58.2 14.7 %shard_map.268 = (f32[4,32,64,128]{3,2,1,0:T(8,128)}, f32[32,64,128]{2,1,0:T(8,128)}) custom-call(s32[32,128]{1,0:T(8,128)S(1)} %get-tuple-element.23.dep_ref, f32[5,2048,128]{2,1,0:T(8,128)} %bitcast.32, f32[5,2048,128]{2,1,0:T(8,128)} %bitcast.33, f32[5,2048,128]{2,1,0:T(8,128)} %bitcast.34, ...), custom_call_target="tpu_custom_call", output_to_operand_aliasing={{0}: (10, {}), {1}: (11, {})} | custom-call | tf_op jit(solution)/shard_map/pallas_call | solution.py:241
  72.9 0.0 all-to-all-done.1
  73.0 15.6 %shard_map.269 = (f32[2,32,64,128]{3,2,1,0:T(8,128)}, f32[32,64,128]{2,1,0:T(8,128)}, f32[256,128]{1,0:T(8,128)}, f32[768,128]{1,0:T(8,128)S(1)}) custom-call(s32[32,128]{1,0:T(8,128)S(1)} %get-tuple-element.23.dep_ref, f32[4,32,64,128]{3,2,1,0:T(8,128)} %get-tuple-element.30.adv_ref, f32[32,64,128]{2,1,0:T(8,128)} %get-tuple-element.31.spread_ref, ...), custom_call_target="tpu_custom_call" | custom-call | tf_op jit(solution)/shard_map/pallas_call | solution.py:845
  88.6 0.7 copy-done.13
  89.3 5.7 %all-to-all-start.2 = ((f32[32,8,128]{2,1,0:T(8,128)}), f32[32,8,128]{2,1,0:T(8,128)S(1)}, u32[]{:S(2)}, u32[]{:S(2)}) async-start(f32[32,8,128]{2,1,0:T(8,128)} %bitcast.9), calls=%async_computation.2 | async-start | bytes 262144 | tf_op jit(solution)/shard_map/all_to_all | solution.py:613
  95.0 1.2 copy-done.2
  96.2 5.5 %shard_map.270.rest_1_ = f32[5,64,32,128]{3,2,1,0:T(8,128)} custom-call(f32[4,32,64,128]{3,2,1,0:T(8,128)} %get-tuple-element.30.adv_ref, f32[2,32,64,128]{3,2,1,0:T(8,128)} %get-tuple-element.34.mixed_ref, f32[32,64,128]{2,1,0:T(8,128)S(1)} %copy-done.2), custom_call_target="tpu_custom_call" | custom-call | tf_op jit(solution)/shard_map/pallas_call | solution.py:896
  101.7 1.5 %all-to-all-done.2 = f32[32,8,128]{2,1,0:T(8,128)S(1)} async-done(((f32[32,8,128]{2,1,0:T(8,128)}), f32[32,8,128]{2,1,0:T(8,128)S(1)}, u32[]{:S(2)}, u32[]{:S(2)}) %all-to-all-start.2) | async-done | bytes 131104 | tf_op jit(solution)/shard_map/all_to_all | solution.py:613
  103.2 3.8 %shard_map.271.refs_7_ = f32[1024,128]{1,0:T(8,128)} custom-call(s32[1]{0:T(128)} %bitcast.1.device_ref, f32[256,128]{1,0:T(8,128)S(1)} %bitcast.24, f32[64,10,128]{2,1,0:T(8,128)S(1)} %copy-done.5, f32[64,8,512]{2,1,0:T(8,128)} %constant.50.clone.along_ref, f32[16,16]{1,0:T(8,128)S(1)} %copy-done.26, bf16[2,512,512]{2,1,0:T(8,128)(2,1)} %constant.52.clone.forward_ref, ...), custom_call_target="tpu_custom_call" | custom-call | tf_op jit(solution)/shard_map/pallas_call | solution.py:628
  107.1 4.4 %all-to-all-start.3 = ((f32[32,32,128]{2,1,0:T(8,128)}), f32[32,32,128]{2,1,0:T(8,128)S(1)}, u32[]{:S(2)}, u32[]{:S(2)}) async-start(f32[32,32,128]{2,1,0:T(8,128)} %bitcast.12), calls=%async_computation.3 | async-start | bytes 1048576 | tf_op jit(solution)/shard_map/all_to_all | solution.py:613
  111.4 9.9 %shard_map.272.w_ref.rest_0_ = f32[1,32,64,128]{3,2,1,0:T(8,128)} custom-call(s32[32,128]{1,0:T(8,128)S(1)} %get-tuple-element.23.dep_ref, f32[5,2048,128]{2,1,0:T(8,128)} %bitcast.36, f32[5,2048,128]{2,1,0:T(8,128)} %bitcast.37, f32[5,2048,128]{2,1,0:T(8,128)} %bitcast.38, f32[3,88,128]{2,1,0:T(8,128)S(1)} %collective-permute-done.rest_0_.refs_4_.refs_3_, ...), custom_call_target="tpu_custom_call" | custom-call | tf_op jit(solution)/shard_map/pallas_call | solution.py:241
  121.4 5.6 %all-to-all-done.3 = f32[32,32,128]{2,1,0:T(8,128)S(1)} async-done(((f32[32,32,128]{2,1,0:T(8,128)}), f32[32,32,128]{2,1,0:T(8,128)S(1)}, u32[]{:S(2)}, u32[]{:S(2)}) %all-to-all-start.3) | async-done | bytes 524320 | tf_op jit(solution)/shard_map/all_to_all | solution.py:613
  127.0 1.2 copy-done.1
  128.2 0.8 shard_map.274
  129.0 3.3 %all-to-all-start.4 = ((f32[32,24,128]{2,1,0:T(8,128)}), f32[32,24,128]{2,1,0:T(8,128)S(1)}, u32[]{:S(2)}, u32[]{:S(2)}) async-start(f32[32,24,128]{2,1,0:T(8,128)} %bitcast.16), calls=%async_computation.4 | async-start | bytes 786432 | tf_op jit(solution)/shard_map/all_to_all | solution.py:613
  132.3 6.3 %shard_map.273 = (f32[2048,128]{1,0:T(8,128)}, f32[5,2048,128]{2,1,0:T(8,128)}) custom-call(s32[32,128]{1,0:T(8,128)S(1)} %get-tuple-element.23.dep_ref, f32[1,32,64,128]{3,2,1,0:T(8,128)} %shard_map.272.w_ref.rest_0_, f32[5,2048,128]{2,1,0:T(8,128)} %bitcast.40, ...), custom_call_target="tpu_custom_call", output_to_operand_aliasing={{1}: (2, {})} | custom-call | tf_op jit(solution)/shard_map/pallas_call | solution.py:939
  138.6 6.6 %all-to-all-done.4 = f32[32,24,128]{2,1,0:T(8,128)S(1)} async-done(((f32[32,24,128]{2,1,0:T(8,128)}), f32[32,24,128]{2,1,0:T(8,128)S(1)}, u32[]{:S(2)}, u32[]{:S(2)}) %all-to-all-start.4) | async-done | bytes 393248 | tf_op jit(solution)/shard_map/all_to_all | solution.py:613
  145.3 0.7 shard_map.275
  (29 shorter events, 0.1 us)
Async XLA Ops:
  0.6 16.8 %copy-start.15 = (f32[64,128]{1,0:T(8,128)S(1)}, f32[64,128]{1,0:T(8,128)}, u32[]{:S(2)}) copy-start(f32[64,128]{1,0:T(8,128)} %constant.45.clone.base_ref) | copy-start | bytes 98308
  0.6 16.8 %copy-start.7 = (bf16[512,256]{1,0:T(8,128)(2,1)S(1)}, bf16[512,256]{1,0:T(8,128)(2,1)}, u32[]{:S(2)}) copy-start(bf16[512,256]{1,0:T(8,128)(2,1)} %constant.47.clone.y_ref) | copy-start | bytes 786436
  0.7 16.8 %copy-start.11 = (bf16[256,256]{1,0:T(8,128)(2,1)S(1)}, bf16[256,256]{1,0:T(8,128)(2,1)}, u32[]{:S(2)}) copy-start(bf16[256,256]{1,0:T(8,128)(2,1)} %constant.46.clone.x_ref) | copy-start | bytes 393220
  0.7 16.8 %copy-start.21 = (bf16[128,64]{1,0:T(8,128)(2,1)S(1)}, bf16[128,64]{1,0:T(8,128)(2,1)}, u32[]{:S(2)}) copy-start(bf16[128,64]{1,0:T(8,128)(2,1)} %constant.44.clone.z_ref) | copy-start | bytes 49156
  0.7 0.8 copy-start.27
  1.4 0.7 copy-start.28
  2.2 21.2 %copy-start.23 = (bf16[128,128]{1,0:T(8,128)(2,1)S(1)}, bf16[128,128]{1,0:T(8,128)(2,1)}, u32[]{:S(2)}) copy-start(bf16[128,128]{1,0:T(8,128)(2,1)} %constant.48.clone.take_ref) | copy-start | bytes 98308
  8.2 23.6 %collective-permute-start.2 = (f32[968,128]{1,0:T(8,128)}, f32[968,128]{1,0:T(8,128)S(1)}, u32[]{:S(2)}, u32[]{:S(2)}) collective-permute-start(f32[968,128]{1,0:T(8,128)} %get-tuple-element.26), channel_id=1, source_target_pairs={{0,1},{1,2},{2,3},{3,4},{4,5},{5,6},{6,7},{8,9},{9,10},{10,11},{11... | collective-permute-start | bytes 1486856 | tf_op jit(solution)/shard_map/ppermute | solution.py:276
  10.6 21.2 %collective-permute-start.3 = (f32[968,128]{1,0:T(8,128)}, f32[968,128]{1,0:T(8,128)S(1)}, u32[]{:S(2)}, u32[]{:S(2)}) collective-permute-start(f32[968,128]{1,0:T(8,128)} %get-tuple-element.27), channel_id=1, source_target_pairs={{1,0},{2,1},{3,2},{4,3},{5,4},{6,5},{7,6},{9,8},{10,9},{11,10},{12... | collective-permute-start | bytes 1486856 | tf_op jit(solution)/shard_map/ppermute | solution.py:276
  11.8 9.0 %collective-permute-start = (f32[3,88,128]{2,1,0:T(8,128)S(1)}, f32[3,88,128]{2,1,0:T(8,128)S(1)}, u32[]{:S(2)}, u32[]{:S(2)}) collective-permute-start(f32[3,88,128]{2,1,0:T(8,128)S(1)} %get-tuple-element.24), channel_id=1, source_target_pairs={{0,8},{8,16},{16,24},{1,9},{9,17},{17,25},{2,10},{10,18},{18,26},{... | collective-permute-start | bytes 405512 | tf_op jit(solution)/shard_map/ppermute | solution.py:276
  16.2 7.2 %collective-permute-start.1 = (f32[3,88,128]{2,1,0:T(8,128)S(1)}, f32[3,88,128]{2,1,0:T(8,128)S(1)}, u32[]{:S(2)}, u32[]{:S(2)}) collective-permute-start(f32[3,88,128]{2,1,0:T(8,128)S(1)} %get-tuple-element.25), channel_id=1, source_target_pairs={{8,0},{16,8},{24,16},{9,1},{17,9},{25,17},{10,2},{18,10},{26,18},{... | collective-permute-start | bytes 405512 | tf_op jit(solution)/shard_map/ppermute | solution.py:276
  20.9 25.7 %copy-start = (f32[32,64,128]{2,1,0:T(8,128)}, f32[32,64,128]{2,1,0:T(8,128)S(1)}, u32[]{:S(2)}) copy-start(f32[32,64,128]{2,1,0:T(8,128)S(1)} %shard_map.264.coef_ref.back_coef_ref) | copy-start | bytes 3145732
  24.6 22.0 %all-to-all-start = ((f32[32,8,128]{2,1,0:T(8,128)}), f32[32,8,128]{2,1,0:T(8,128)}, u32[]{:S(2)}, u32[]{:S(2)}) async-start(f32[32,8,128]{2,1,0:T(8,128)} %bitcast.3), calls=%async_computation | async-start | bytes 262144 | tf_op jit(solution)/shard_map/all_to_all | solution.py:613
  31.7 14.8 %copy-start.3 = (f32[64,8,512]{2,1,0:T(8,128)S(1)}, f32[64,8,512]{2,1,0:T(8,128)}, u32[]{:S(2)}) copy-start(f32[64,8,512]{2,1,0:T(8,128)} %constant.50.clone.along_ref) | copy-start | bytes 3145732
  31.7 14.8 %copy-start.10 = (f32[2,128,128]{2,1,0:T(8,128)S(1)}, f32[2,128,128]{2,1,0:T(8,128)}, u32[]{:S(2)}) copy-start(f32[2,128,128]{2,1,0:T(8,128)} %constant.55.clone.column_ref) | copy-start | bytes 393220
  31.8 14.8 %copy-start.26 = (f32[16,16]{1,0:T(8,128)S(1)}, f32[16,16]{1,0:T(8,128)}, u32[]{:S(2)}) copy-start(f32[16,16]{1,0:T(8,128)} %constant.51.clone.sines_ref) | copy-start | bytes 3076
  31.8 14.8 %copy-start.29 = (f32[8,128]{1,0:T(8,128)S(1)}, f32[8,128]{1,0:T(8,128)}, u32[]{:S(2)}) copy-start(f32[8,128]{1,0:T(8,128)} %constant.56.clone.lines_ref) | copy-start | bytes 12292
  46.6 1.0 copy-start.4
  47.6 0.8 copy-start.17
  52.1 20.8 %all-to-all-start.1 = ((f32[32,8,128]{2,1,0:T(8,128)}), f32[32,8,128]{2,1,0:T(8,128)S(1)}, u32[]{:S(2)}, u32[]{:S(2)}) async-start(f32[32,8,128]{2,1,0:T(8,128)} %bitcast.7), calls=%async_computation.1 | async-start | bytes 262144 | tf_op jit(solution)/shard_map/all_to_all | solution.py:613
  58.0 14.9 %copy-start.6 = (bf16[512,256]{1,0:T(8,128)(2,1)S(1)}, bf16[512,256]{1,0:T(8,128)(2,1)}, u32[]{:S(2)}) copy-start(bf16[512,256]{1,0:T(8,128)(2,1)} %constant.57.clone.y_back_ref.y_ref) | copy-start | bytes 786436
  58.0 14.9 %copy-start.8 = (bf16[512,256]{1,0:T(8,128)(2,1)S(1)}, bf16[512,256]{1,0:T(8,128)(2,1)}, u32[]{:S(2)}) copy-start(bf16[512,256]{1,0:T(8,128)(2,1)} %constant.47.clone.y_ref) | copy-start | bytes 786436
  58.0 14.9 %copy-start.9 = (bf16[256,256]{1,0:T(8,128)(2,1)S(1)}, bf16[256,256]{1,0:T(8,128)(2,1)}, u32[]{:S(2)}) copy-start(bf16[256,256]{1,0:T(8,128)(2,1)} %constant.58.clone.x_back_ref.x_ref) | copy-start | bytes 393220
  58.1 14.9 %copy-start.12 = (bf16[256,256]{1,0:T(8,128)(2,1)S(1)}, bf16[256,256]{1,0:T(8,128)(2,1)}, u32[]{:S(2)}) copy-start(bf16[256,256]{1,0:T(8,128)(2,1)} %constant.46.clone.x_ref) | copy-start | bytes 393220
  58.1 14.9 %copy-start.16 = (bf16[256,128]{1,0:T(8,128)(2,1)S(1)}, bf16[256,128]{1,0:T(8,128)(2,1)}, u32[]{:S(2)}) copy-start(bf16[256,128]{1,0:T(8,128)(2,1)} %constant.60.clone.give_ref) | copy-start | bytes 196612
  58.1 14.9 %copy-start.19 = (bf16[256,256]{1,0:T(8,128)(2,1)S(1)}, bf16[256,256]{1,0:T(8,128)(2,1)}, u32[]{:S(2)}) copy-start(bf16[256,256]{1,0:T(8,128)(2,1)} %w_in_ref.1) | copy-start | bytes 393220
  58.1 14.9 %copy-start.20 = (bf16[128,64]{1,0:T(8,128)(2,1)S(1)}, bf16[128,64]{1,0:T(8,128)(2,1)}, u32[]{:S(2)}) copy-start(bf16[128,64]{1,0:T(8,128)(2,1)} %constant.59.clone.z_back_ref.z_ref) | copy-start | bytes 49156
  58.1 14.9 %copy-start.22 = (bf16[128,64]{1,0:T(8,128)(2,1)S(1)}, bf16[128,64]{1,0:T(8,128)(2,1)}, u32[]{:S(2)}) copy-start(bf16[128,64]{1,0:T(8,128)(2,1)} %constant.44.clone.z_ref) | copy-start | bytes 49156
  58.1 14.9 %copy-start.24 = (bf16[128,128]{1,0:T(8,128)(2,1)S(1)}, bf16[128,128]{1,0:T(8,128)(2,1)}, u32[]{:S(2)}) copy-start(bf16[128,128]{1,0:T(8,128)(2,1)} %constant.48.clone.take_ref) | copy-start | bytes 98308
  58.1 14.9 %copy-start.25 = (bf16[256,63]{0,1:T(8,128)(2,1)S(1)}, bf16[256,63]{0,1:T(8,128)(2,1)}, u32[]{:S(2)}) copy-start(bf16[256,63]{0,1:T(8,128)(2,1)} %param.30) | copy-start | bytes 96772
  58.1 14.9 %copy-start.30 = (f32[256]{0:T(256)S(1)}, f32[256]{0:T(256)}, u32[]{:S(2)}) copy-start(f32[256]{0:T(256)} %param.29) | copy-start | bytes 3076
  88.6 0.7 copy-start.13
  89.3 13.9 %all-to-all-start.2 = ((f32[32,8,128]{2,1,0:T(8,128)}), f32[32,8,128]{2,1,0:T(8,128)S(1)}, u32[]{:S(2)}, u32[]{:S(2)}) async-start(f32[32,8,128]{2,1,0:T(8,128)} %bitcast.9), calls=%async_computation.2 | async-start | bytes 262144 | tf_op jit(solution)/shard_map/all_to_all | solution.py:613
  95.0 1.2 copy-start.2
  96.2 7.0 %copy-start.5 = (f32[64,10,128]{2,1,0:T(8,128)S(1)}, f32[64,10,128]{2,1,0:T(8,128)}, u32[]{:S(2)}) copy-start(f32[64,10,128]{2,1,0:T(8,128)} %constant.49.clone.cross_ref) | copy-start | bytes 983044
  96.2 7.0 %copy-start.14 = (f32[768,128]{1,0:T(8,128)S(1)}, f32[768,128]{1,0:T(8,128)}, u32[]{:S(2)}) copy-start(f32[768,128]{1,0:T(8,128)} %copy-done.13) | copy-start | bytes 1179652
  96.2 7.0 %copy-start.18 = (f32[3,32,128]{2,1,0:T(8,128)S(1)}, f32[3,32,128]{2,1,0:T(8,128)}, u32[]{:S(2)}) copy-start(f32[3,32,128]{2,1,0:T(8,128)} %constant.54.clone.strip_ref) | copy-start | bytes 147460
  107.1 19.9 %all-to-all-start.3 = ((f32[32,32,128]{2,1,0:T(8,128)}), f32[32,32,128]{2,1,0:T(8,128)S(1)}, u32[]{:S(2)}, u32[]{:S(2)}) async-start(f32[32,32,128]{2,1,0:T(8,128)} %bitcast.12), calls=%async_computation.3 | async-start | bytes 1048576 | tf_op jit(solution)/shard_map/all_to_all | solution.py:613
  127.0 1.2 copy-start.1
  129.0 16.3 %all-to-all-start.4 = ((f32[32,24,128]{2,1,0:T(8,128)}), f32[32,24,128]{2,1,0:T(8,128)S(1)}, u32[]{:S(2)}, u32[]{:S(2)}) async-start(f32[32,24,128]{2,1,0:T(8,128)} %bitcast.16), calls=%async_computation.4 | async-start | bytes 786432 | tf_op jit(solution)/shard_map/all_to_all | solution.py:613

commit v3 on v2

--- a/solution.py
+++ b/solution.py
@@ -17,12 +17,16 @@
 HALO = 3
 FIELDS = 5
 SUB = 8
-
-
-def pack_kernel(mask_ref, depth_ref, fields_ref, dep_ref, xfirst_ref, xlast_ref, yfirst_ref, ylast_ref):
+PIECES = 4
+
+
+def pack_kernel(mask_ref, depth_ref, *refs):
+    field_refs, refs = refs[:PIECES], refs[PIECES:]
+    dep_ref, xfirst_ref, xlast_ref, yfirst_ref, ylast_ref = refs
     field = pl.program_id(0)
     north, east = dep_ref.shape
-    levels = fields_ref.shape[1] // north
+    some = field_refs[0].shape[1] // north
+    levels = PIECES * some
     per = east // north
     blocks = levels // per
     dep = jnp.where(mask_ref[...] == 1, depth_ref[...], 0)
@@ -30,21 +34,22 @@
     tiled = jnp.concatenate([dep] * per, 0)
     level_in_block = lax.broadcasted_iota(jnp.int32, (east, east), 0) // north
     for t in range(blocks):
-        block = fields_ref[0, t * east : (t + 1) * east, :]
+        piece, at = divmod(t * east, some * north)
+        block = field_refs[piece][0, at : at + east, :]
         masked = jnp.where(level_in_block + t * per < tiled, block, 0.0)
         turned = masked.T
         row = field * blocks + t
         for s in range(HALO):
             xfirst_ref[s, pl.ds(row, 1), :] = turned[s : s + 1]
             xlast_ref[s, pl.ds(row, 1), :] = turned[east - HALO + s : east - HALO + s + 1]
-    level = lax.broadcasted_iota(jnp.int32, (levels, east), 0)
-    for s in range(HALO):
-        at = pl.multiple_of((field * HALO + s) * levels, SUB)
+    for s, piece in [(s, piece) for s in range(HALO) for piece in range(PIECES)]:
+        level = lax.broadcasted_iota(jnp.int32, (some, east), 0) + piece * some
+        at = pl.multiple_of((field * HALO + s) * levels + piece * some, SUB)
         low, high = s, north - HALO + s
-        first = fields_ref[0, pl.ds(low, levels, stride=north), :]
-        last = fields_ref[0, pl.ds(high, levels, stride=north), :]
-        yfirst_ref[pl.ds(at, levels), :] = jnp.where(level < dep[low : low + 1], first, 0.0)
-        ylast_ref[pl.ds(at, levels), :] = jnp.where(level < dep[high : high + 1], last, 0.0)
+        first = field_refs[piece][0, pl.ds(low, some, stride=north), :]
+        last = field_refs[piece][0, pl.ds(high, some, stride=north), :]
+        yfirst_ref[pl.ds(at, some), :] = jnp.where(level < dep[low : low + 1], first, 0.0)
+        ylast_ref[pl.ds(at, some), :] = jnp.where(level < dep[high : high + 1], last, 0.0)
 
     @pl.when(field == 0)
     def _():
@@ -73,12 +78,15 @@
         in_specs=[
             whole(mask),
             whole(depth),
-            pl.BlockSpec((1, levels * north, east), lambda f: (f, 0, 0)),
+            *(
+                pl.BlockSpec((1, levels * north // PIECES, east), lambda f, p=p: (f, p, 0))
+                for p in range(PIECES)
+            ),
         ],
         out_specs=[whole(mask), whole(x_shape), whole(x_shape), whole(y_shape), whole(y_shape)],
         out_shape=[jax.ShapeDtypeStruct(mask.shape, jnp.int32), x_shape, x_shape, y_shape, y_shape],
-        compiler_params=pltpu.CompilerParams(vmem_limit_bytes=52 << 20),
-    )(mask, depth, fields.reshape(FIELDS, levels * north, east))
+        compiler_params=pltpu.CompilerParams(vmem_limit_bytes=61 << 20),
+    )(mask, depth, *(fields.reshape(FIELDS, levels * north, east) for _ in range(PIECES)))
 
 
 def face_flux(slopes, left, right, speed, share):
@@ -513,15 +521,16 @@
     strip_ref, column_ref, lines_ref, *rest,
 ):
     del device_ref
-    extra_ref, jump_ref = rest[0], rest[-1]
+    jump_ref = rest[-1]
     rows, cols, east, north = tables.rows, tables.cols, tables.east, tables.north
-    each = jump_ref.shape[0] // tables.count
-    every_in = edge_ref.shape[0] // tables.count
-    if each > tables.share * PARTS:
-        more = extra_ref.shape[0] // tables.count
+    each = edge_ref.shape[0] // tables.count
+    mine = tables.share * PARTS
+    if each > mine:
+        total = edge_ref[mine:each, :]
+        for d in range(1, tables.count):
+            total = total + edge_ref[d * each + mine : (d + 1) * each, :]
         for d in range(tables.count):
-            at = d * each + tables.share * PARTS
-            jump_ref[at : at + more, :] = extra_ref[d * more : (d + 1) * more, :]
+            jump_ref[d * each + mine : (d + 1) * each, :] = total
     share, inner = tables.share, tables.rows - 1
     f32 = jnp.float32
     east_last, east_first = lines_ref[0:1, :], lines_ref[1:2, :]
@@ -542,7 +551,7 @@
     for m in range(share):
         west, south, top = (
             [
-                edge_ref[pl.ds(a * cols * every_in + m * PARTS + part, cols, stride=every_in), :]
+                edge_ref[pl.ds(a * cols * each + m * PARTS + part, cols, stride=each), :]
                 for a in range(rows)
             ]
             for part in range(PARTS - 1)
@@ -613,7 +622,7 @@
     return lax.all_to_all(block, AXES, split_axis=0, concat_axis=0, tiled=True)
 
 
-def interface(tables, received, extra, travels, limit, *after):
+def interface(tables, received, *after):
     device = lax.axis_index("rows") * lax.axis_size("cols") + lax.axis_index("cols")
     operands = (
         received, tables.cross, tables.along, tables.sines, tables.wide_forward, tables.wide_back,
@@ -623,23 +632,17 @@
     for at in (1, 2):
         shape = (tables.share, *operands[at].shape[1:])
         specs[at] = pl.BlockSpec(shape, lambda k, mine: (mine[0], 0, 0))
-    rows = received.shape[0] + (extra.shape[0] if travels else 0)
-    shape = jax.ShapeDtypeStruct((rows, tables.east), jnp.float32)
     return pl.pallas_call(
         functools.partial(interface_kernel, tables),
         grid_spec=pltpu.PrefetchScalarGridSpec(
             num_scalar_prefetch=1,
             grid=(1,),
-            in_specs=[
-                *specs,
-                whole_spec(extra) if travels else pl.BlockSpec(memory_space=pl.ANY),
-                *(pl.BlockSpec(memory_space=pl.ANY) for _ in after),
-            ],
-            out_specs=whole_spec(shape),
+            in_specs=[*specs, *(pl.BlockSpec(memory_space=pl.ANY) for _ in after)],
+            out_specs=whole_spec(received),
         ),
-        out_shape=shape,
-        compiler_params=call_params(limit),
-    )(device.astype(jnp.int32).reshape(1), *operands, extra, *after)
+        out_shape=jax.ShapeDtypeStruct(received.shape, jnp.float32),
+        compiler_params=call_params(56 << 20),
+    )(device.astype(jnp.int32).reshape(1), *operands, *after)
 
 
 def adjoint_kernel(
@@ -738,8 +741,8 @@
     tables, dep_ref, adv_ref, spread_ref, w_field_ref, heat_ref, salt_ref,
     w_in_ref, bias_ref, w_ref, back_coef_ref, back_jump_ref,
     z_ref, base_ref, x_ref, y_ref, take_ref, y_back_ref, x_back_ref, z_back_ref, give_ref,
-    mixed_ref, coef_ref, sides, total_ref,
-    spec, back, feats, activity, hidden, grads, flat,
+    mixed_ref, coef_ref, send_ref,
+    spec, back, feats, activity, hidden, grads, flat, sides, total_ref,
     w_in, bias, w, w_out, g_in_ref, g_bias_ref, g_out_ref,
 ):
     step = pl.program_id(0)
@@ -821,6 +824,15 @@
             total_ref[at + k : at + k + east, :] = last[k : k + east].T
         if total_ref.shape[0] > at + width:
             total_ref[at + width :, :] = jnp.zeros_like(total_ref[at + width :, :])
+        mine = tables.share * PARTS
+        each = send_ref.shape[0] // tables.count
+        for part in range(mine):
+            send_ref[pl.ds(part, tables.count, stride=each), :] = sides[
+                pl.ds(part, tables.count, stride=mine), :
+            ]
+        more = each - mine
+        for d in range(tables.count):
+            send_ref[d * each + mine : (d + 1) * each, :] = total_ref[d * more : (d + 1) * more, :]
 
 
 def column(
@@ -839,7 +851,7 @@
     rows = inputs * hidden // east + hidden
     assert 2 * levels == east
     rows = -(-rows // tables.count) * tables.count
-    total = jax.ShapeDtypeStruct((rows, east), f32)
+    send = jax.ShapeDtypeStruct((edge.shape[0] + rows, east), f32)
     lanes = SUB * east
     field = lambda f: pl.BlockSpec((1, levels, SUB, east), lambda k: (f, 0, k, 0))
     return pl.pallas_call(
@@ -857,10 +869,9 @@
         out_specs=[
             pl.BlockSpec((2, SUB, levels, east), lambda k: (0, k, 0, 0)),
             whole_spec(coef),
-            whole_spec(edge),
-            whole_spec(total),
+            whole_spec(send),
         ],
-        out_shape=[mixed, coef, edge, total],
+        out_shape=[mixed, coef, send],
         scratch_shapes=[
             pltpu.VMEM(coef.shape, f32),
             pltpu.VMEM(coef.shape, f32),
@@ -869,6 +880,8 @@
             pltpu.VMEM((hidden, lanes), bf16),
             pltpu.VMEM((levels, lanes), bf16),
             pltpu.VMEM((3, levels * SUB, east), f32),
+            pltpu.VMEM(edge.shape, f32),
+            pltpu.VMEM((rows, east), f32),
             pltpu.VMEM((hidden, inputs), bf16),
             pltpu.VMEM((hidden, east), f32),
             pltpu.VMEM((hidden, east), f32),
@@ -900,7 +913,7 @@
         out_specs=pl.BlockSpec((FIELDS, levels, SUB, east), lambda k: (0, 0, k, 0)),
         out_shape=jax.ShapeDtypeStruct((FIELDS, levels, north, east), jnp.float32),
         scratch_shapes=[pltpu.VMEM((FIELDS, levels * SUB, east), jnp.float32)],
-        compiler_params=call_params(),
+        compiler_params=call_params(61 << 20),
     )(adv, mixed, after)
 
 
@@ -962,54 +975,36 @@
     return pressure.reshape(levels, north, east), new.reshape(FIELDS, levels, north, east)
 
 
-def sum_kernel(count, skip, pieces_ref, *rest):
-    out_ref = rest[-1]
-    each = pieces_ref.shape[0] // count
-    more = each - skip
-    total = pieces_ref[skip:each, :]
-    for d in range(1, count):
-        total = total + pieces_ref[d * each + skip : (d + 1) * each, :]
-    for d in range(count):
-        out_ref[d * more : (d + 1) * more, :] = total
-
-
-def sum_pieces(tables, received, *after):
-    skip = tables.share * PARTS
-    rows = received.shape[0] - skip * tables.count
-    shape = jax.ShapeDtypeStruct((rows, tables.east), jnp.float32)
-    return pl.pallas_call(
-        functools.partial(sum_kernel, tables.count, skip),
-        grid=(1,),
-        in_specs=[whole_spec(received), *(pl.BlockSpec(memory_space=pl.ANY) for _ in after)],
-        out_specs=whole_spec(shape),
-        out_shape=shape,
-        compiler_params=call_params(),
-    )(received, *after)
-
-
-def split_kernel(sums_ref, in_ref, bias_ref, out_ref):
+def split_kernel(skip, count, sums_ref, in_ref, bias_ref, out_ref, flat):
     inputs, width = in_ref.shape
     east = sums_ref.shape[1]
+    each = sums_ref.shape[0] // count
+    more = each - skip
+    for d in range(count):
+        flat[d * more : (d + 1) * more, :] = sums_ref[d * each + skip : (d + 1) * each, :]
     wide = inputs * width // east
     for k in range(width // east):
         lanes = slice(k * east, (k + 1) * east)
-        in_ref[:, lanes] = sums_ref[k * inputs : (k + 1) * inputs, :]
+        in_ref[:, lanes] = flat[k * inputs : (k + 1) * inputs, :]
         at = wide + k * east
-        out_ref[:, lanes] = sums_ref[at : at + out_ref.shape[0], :]
-        bias_ref[:, lanes] = sums_ref[at + east // 2 : at + east // 2 + 1, :]
-
-
-def split_sums(sums, inputs, hidden, outputs):
+        out_ref[:, lanes] = flat[at : at + out_ref.shape[0], :]
+        bias_ref[:, lanes] = flat[at + east // 2 : at + east // 2 + 1, :]
+
+
+def split_sums(tables, sums, inputs, hidden, outputs):
+    skip = tables.share * PARTS
+    rows = sums.shape[0] - skip * tables.count
     shapes = [
         jax.ShapeDtypeStruct(shape, jnp.float32)
         for shape in ((inputs, hidden), (1, hidden), (outputs, hidden))
     ]
     g_in, g_bias, g_out = pl.pallas_call(
-        split_kernel,
+        functools.partial(split_kernel, skip, tables.count),
         grid=(1,),
         in_specs=[whole_spec(sums)],
         out_specs=[whole_spec(a) for a in shapes],
         out_shape=shapes,
+        scratch_shapes=[pltpu.VMEM((rows, tables.east), jnp.float32)],
         compiler_params=call_params(),
     )(sums)
     return g_in, g_bias.reshape(hidden), g_out.T
@@ -1027,20 +1022,18 @@
     back_coef = adjoint_local(tables, cotangent, dep)
     back_edges = adjoint_edges(tables, back_coef, edges[0], edges[1])
     half = advect(fields, dep, TRACERS, edges, (0, steps // 2), back_edges)
-    back_jumps = interface(tables, exchange(back_edges), half[1], False, 52 << 20)
+    back_jumps = interface(tables, exchange(back_edges), half[1])
     adv, spread = advect(fields, dep, TRACERS, edges, (steps // 2, steps), back_jumps, half)
-    mixed, coef, sides, grads = column(
+    mixed, coef, send = column(
         tables, dep, adv, spread, fields, cotangent, in_weight, in_bias, out_weight,
         back_coef, exchange(back_jumps),
     )
-    received = exchange(sides)
+    received = exchange(send)
+    w = advect(fields, dep, (2,), edges, (0, steps), coef)[0]
     new = gather_fields(adv, mixed, coef)
-    jumps_out = interface(tables, received, grads, True, VMEM_LIMIT, new)
-    w = advect(fields, dep, (2,), edges, (0, steps), jumps_out)[0]
-    jumps = exchange(jumps_out)
-    sums = exchange(sum_pieces(tables, jumps, w))
+    jumps = exchange(interface(tables, received, w, new))
     pressure, new_fields = pressure_finish(tables, dep, w, new, coef, jumps)
-    return (new_fields, pressure, *split_sums(sums, inputs, hidden, outputs))
+    return (new_fields, pressure, *split_sums(tables, jumps, inputs, hidden, outputs))
 
 
 def solution(mesh):

time: 147 us -> 143 us (0.973)
  blocking collectives: 0 us -> 21.2 us
  waiting for transfers between devices: 16.3 us -> 2.2 us
  starting transfers between devices: 35.7 us -> 28.4 us
  local copies, waits for them, and re-layouts: 6.64 us -> 3.16 us
    all_to_all x0 -> x1, blocking collectives: none -> 21.2 us  [exchange(): return lax.all_to_all(block, AXES, split_axis=0, concat_axis=0, tiled=True)]
    all_to_all x5 -> x3, waiting for transfers between devices: 13.8 us -> 0.21 us  [exchange(): return lax.all_to_all(block, AXES, split_axis=0, concat_axis=0, tiled=True)]
    all_to_all x5 -> x3, starting transfers between devices: 26.4 us -> 19.1 us  [exchange(): return lax.all_to_all(block, AXES, split_axis=0, concat_axis=0, tiled=True)]
    unnamed x62 -> x36, local copies, waits for them, and re-layouts: 6.64 us -> 3.16 us
  transfers between devices with their start and end apart: 9 -> 7, of which waited for: 4 -> 2; matrix products, arithmetic and copies ran while one was open for 0% -> 0% of each run, Pallas kernels for 38% -> 35%
where the time goes in v3:
time: 143 us; the launch traced here: 142 us
  Pallas kernels  85.9 us (60%)
  starting transfers between devices  28.4 us (20%)
  blocking collectives  21.2 us (15%)
  local copies, waits for them, and re-layouts  3.16 us (2%)
  waiting for transfers between devices  2.2 us (2%)
    pallas_call x3, Pallas kernels, advect(): pl.pallas_call(functools.partial(advect_kernel, tracers, staged, span[0],...  39.3 us
    all_to_all x1, blocking collectives, exchange(): return lax.all_to_all(block, AXES, split_axis=0, concat_axis=0, tiled=True)  21.2 us
    all_to_all x3, starting transfers between devices, exchange(): return lax.all_to_all(block, AXES, split_axis=0, concat_axis=0, tiled=True)  19.1 us
    pallas_call x1, Pallas kernels, column(): pl.pallas_call(functools.partial(column_kernel, tables), grid=(north // S...  15.7 us
    pallas_call x2, Pallas kernels, interface(): pl.pallas_call(functools.partial(interface_kernel, tables), grid_spec=plt...  7.83 us
    ppermute x2, starting transfers between devices, shift_both(): lax.ppermute(last, axis, forward)  6.69 us
    pallas_call x1, Pallas kernels, pressure_finish(): pl.pallas_call(functools.partial(pressure_kernel, tables), grid=(1,), in_...  6.29 us
    pallas_call x1, Pallas kernels, pack_edges(): pl.pallas_call(pack_kernel, grid=(FIELDS,), in_specs=[whole(mask), whole(...  6.08 us
  transfers between devices with their start and end apart: 7, of which 2 were waited for; matrix products, arithmetic and copies ran while one was open for 0% of the time, Pallas kernels for 35%

profile of v3, /device:TPU:0, one launch (start us, length us, event | category | flops | bytes accessed | tf_op | source)
XLA Modules:
  0.0 141.8 jit_solution(15450072879892869969)
XLA Ops:
  0.6 0.0 copy-start.3
  0.6 0.0 copy-start.7
  0.7 0.0 copy-start.8
  0.7 0.0 copy-start.12
  0.7 0.0 copy-start.13
  0.7 6.1 %shard_map.263 = (s32[32,128]{1,0:T(8,128)}, f32[3,88,128]{2,1,0:T(8,128)}, f32[3,88,128]{2,1,0:T(8,128)}, f32[968,128]{1,0:T(8,128)}, f32[968,128]{1,0:T(8,128)}) custom-call(s32[32,128]{1,0:T(8,128)} %mask_ref.1, s32[32,128]{1,0:T(8,128)} %depth_ref.1, f32[5,2048,128]{2,1,0:T(8,128)} %bitcast.24, f32[5,2048,128]{2,1,0:T(8,128)} %bitcast.25, ...), custom_call_target="tpu_custom_call" | custom-call | tf_op jit(solution)/shard_map/pallas_call | solution.py:75
  6.8 2.4 %collective-permute-start.2 = (f32[968,128]{1,0:T(8,128)}, f32[968,128]{1,0:T(8,128)S(1)}, u32[]{:S(2)}, u32[]{:S(2)}) collective-permute-start(f32[968,128]{1,0:T(8,128)} %get-tuple-element.25), channel_id=1, source_target_pairs={{0,1},{1,2},{2,3},{3,4},{4,5},{5,6},{6,7},{8,9},{9,10},{10,11},{11... | collective-permute-start | bytes 1486856 | tf_op jit(solution)/shard_map/ppermute | solution.py:284
  9.2 1.3 collective-permute-start.3
  10.5 4.3 %collective-permute-start = (f32[3,88,128]{2,1,0:T(8,128)}, f32[3,88,128]{2,1,0:T(8,128)S(1)}, u32[]{:S(2)}, u32[]{:S(2)}) collective-permute-start(f32[3,88,128]{2,1,0:T(8,128)} %get-tuple-element.23), channel_id=1, source_target_pairs={{0,8},{8,16},{16,24},{1,9},{9,17},{17,25},{2,10},{10,18},{18,26},{... | collective-permute-start | bytes 405512 | tf_op jit(solution)/shard_map/ppermute | solution.py:284
  14.8 1.3 collective-permute-start.1
  16.1 0.0 copy-done.3
  16.1 0.0 copy-done.7
  16.1 0.0 copy-done.8
  16.1 0.0 copy-done.12
  16.1 0.0 copy-start.4
  16.1 0.7 copy-done.4
  16.8 0.0 copy-start.5
  16.8 3.3 %shard_map.264.coef_ref.back_coef_ref = f32[32,64,128]{2,1,0:T(8,128)S(1)} custom-call(s32[32,128]{1,0:T(8,128)S(1)} %copy-done.4, f32[5,2048,128]{2,1,0:T(8,128)} %bitcast.39, bf16[128,64]{1,0:T(8,128)(2,1)S(1)} %copy-done.12, f32[64,128]{1,0:T(8,128)S(1)} %copy-done.8, bf16[256,256]{1,0:T(8,128)(2,1)S(1)} %copy-done.7, bf16[512,256]{1,0:T(8,128)(2,1)S(1)} %copy-done.3), custom_call_target="tpu_custom_call" | custom-call | tf_op jit(solution)/shard_map/pallas_call | solution.py:675
  20.2 0.0 copy-start
  20.2 0.0 collective-permute-done.rest_0_.refs_4_.refs_3_
  20.2 2.0 %collective-permute-done.1.rest_1_.refs_5_.refs_4_ = f32[3,88,128]{2,1,0:T(8,128)S(1)} collective-permute-done((f32[3,88,128]{2,1,0:T(8,128)}, f32[3,88,128]{2,1,0:T(8,128)S(1)}, u32[]{:S(2)}, u32[]{:S(2)}) %collective-permute-start.1) | collective-permute-done | bytes 135200 | tf_op jit(solution)/shard_map/ppermute | solution.py:284
  22.2 0.0 copy-done.13
  22.2 1.2 shard_map.265.refs_8_
  23.4 7.4 %all-to-all-start = ((f32[32,8,128]{2,1,0:T(8,128)}), f32[32,8,128]{2,1,0:T(8,128)S(1)}, u32[]{:S(2)}, u32[]{:S(2)}) async-start(f32[32,8,128]{2,1,0:T(8,128)} %bitcast.3), calls=%async_computation | async-start | bytes 262144 | tf_op jit(solution)/shard_map/all_to_all | solution.py:622
  30.8 0.0 collective-permute-done.2.refs_6_.refs_5_
  30.8 0.0 collective-permute-done.3.refs_7_.refs_6_
  30.9 0.0 copy-done.5
  30.9 14.7 %shard_map.266 = (f32[4,32,64,128]{3,2,1,0:T(8,128)}, f32[32,64,128]{2,1,0:T(8,128)}) custom-call(s32[32,128]{1,0:T(8,128)S(1)} %copy-done.5, f32[5,2048,128]{2,1,0:T(8,128)} %bitcast.28, f32[5,2048,128]{2,1,0:T(8,128)} %bitcast.29, f32[5,2048,128]{2,1,0:T(8,128)} %bitcast.30, f32[5,2048,128]{2,1,0:T(8,128)} %bitcast.31, ...), custom_call_target="tpu_custom_call" | custom-call | tf_op jit(solution)/shard_map/pallas_call | solution.py:249
  45.5 0.0 copy-done
  45.5 0.0 all-to-all-done
  45.5 0.0 copy-start.17
  45.5 0.6 copy-done.17
  46.2 3.8 %shard_map.267.refs_8_ = f32[256,128]{1,0:T(8,128)} custom-call(s32[1]{0:T(128)} %bitcast.1.device_ref, f32[256,128]{1,0:T(8,128)} %bitcast.44, f32[64,10,128]{2,1,0:T(8,128)} %constant.49.clone.cross_ref, f32[64,8,512]{2,1,0:T(8,128)} %constant.50.clone.along_ref, f32[16,16]{1,0:T(8,128)} %constant.51.clone.sines_ref, ...), custom_call_target="tpu_custom_call" | custom-call | tf_op jit(solution)/shard_map/pallas_call | solution.py:635
  49.9 6.0 %all-to-all-start.1 = ((f32[32,8,128]{2,1,0:T(8,128)}), f32[32,8,128]{2,1,0:T(8,128)S(1)}, u32[]{:S(2)}, u32[]{:S(2)}) async-start(f32[32,8,128]{2,1,0:T(8,128)} %bitcast.20), calls=%async_computation.1 | async-start | bytes 262144 | tf_op jit(solution)/shard_map/all_to_all | solution.py:622
  56.0 0.0 copy-start.1
  56.0 0.9 copy-done.1
  56.9 0.0 copy-start.2
  56.9 0.0 copy-start.6
  56.9 0.0 copy-start.9
  56.9 0.0 copy-start.10
  56.9 0.0 copy-start.11
  56.9 0.0 copy-start.14
  56.9 0.0 copy-start.15
  57.0 14.7 %shard_map.268 = (f32[4,32,64,128]{3,2,1,0:T(8,128)}, f32[32,64,128]{2,1,0:T(8,128)}) custom-call(s32[32,128]{1,0:T(8,128)S(1)} %copy-done.5, f32[5,2048,128]{2,1,0:T(8,128)} %bitcast.32, f32[5,2048,128]{2,1,0:T(8,128)} %bitcast.33, f32[5,2048,128]{2,1,0:T(8,128)} %bitcast.34, ...), custom_call_target="tpu_custom_call", output_to_operand_aliasing={{0}: (10, {}), {1}: (11, {})} | custom-call | tf_op jit(solution)/shard_map/pallas_call | solution.py:249
  71.7 0.0 all-to-all-done.1
  71.7 0.0 copy-done.2
  71.7 0.0 copy-done.6
  71.7 0.0 copy-done.9
  71.7 0.0 copy-done.10
  71.7 0.0 copy-done.11
  71.7 0.0 copy-done.14
  71.7 0.0 copy-done.15
  71.7 15.7 %shard_map.269 = (f32[2,32,64,128]{3,2,1,0:T(8,128)}, f32[32,64,128]{2,1,0:T(8,128)}, f32[1024,128]{1,0:T(8,128)}) custom-call(s32[32,128]{1,0:T(8,128)S(1)} %copy-done.5, f32[4,32,64,128]{3,2,1,0:T(8,128)} %get-tuple-element.29.adv_ref, f32[32,64,128]{2,1,0:T(8,128)} %get-tuple-element.30.spread_ref, f32[5,64,32,128]{3,2,1,0:T(8,128)} %w_field_ref.1, ...), custom_call_target="tpu_custom_call" | custom-call | tf_op jit(solution)/shard_map/pallas_call | solution.py:857
  87.5 5.7 %all-to-all-start.2 = ((f32[32,32,128]{2,1,0:T(8,128)}), f32[32,32,128]{2,1,0:T(8,128)S(1)}, u32[]{:S(2)}, u32[]{:S(2)}) async-start(f32[32,32,128]{2,1,0:T(8,128)} %bitcast.10), calls=%async_computation.2 | async-start | bytes 1048576 | tf_op jit(solution)/shard_map/all_to_all | solution.py:622
  93.1 5.4 %shard_map.271.rest_1_ = f32[5,64,32,128]{3,2,1,0:T(8,128)} custom-call(f32[4,32,64,128]{3,2,1,0:T(8,128)} %get-tuple-element.29.adv_ref, f32[2,32,64,128]{3,2,1,0:T(8,128)} %get-tuple-element.32.mixed_ref, f32[32,64,128]{2,1,0:T(8,128)} %get-tuple-element.31.refs_7_.after_ref.coef_ref), custom_call_target="tpu_custom_call" | custom-call | tf_op jit(solution)/shard_map/pallas_call | solution.py:909
  98.6 9.9 %shard_map.270.rest_0_.w_ref = f32[1,32,64,128]{3,2,1,0:T(8,128)} custom-call(s32[32,128]{1,0:T(8,128)S(1)} %copy-done.5, f32[5,2048,128]{2,1,0:T(8,128)} %bitcast.36, f32[5,2048,128]{2,1,0:T(8,128)} %bitcast.37, f32[5,2048,128]{2,1,0:T(8,128)} %bitcast.38, f32[3,88,128]{2,1,0:T(8,128)S(1)} %collective-permute-done.rest_0_.refs_4_.refs_3_, ...), custom_call_target="tpu_custom_call" | custom-call | tf_op jit(solution)/shard_map/pallas_call | solution.py:249
  108.5 0.2 all-to-all-done.2
  108.7 0.0 copy-start.16
  108.7 0.8 copy-done.16
  109.5 4.1 %shard_map.272 = f32[1024,128]{1,0:T(8,128)} custom-call(s32[1]{0:T(128)} %bitcast.1.device_ref, f32[1024,128]{1,0:T(8,128)} %bitcast.42, f32[64,10,128]{2,1,0:T(8,128)} %constant.49.clone.cross_ref, f32[64,8,512]{2,1,0:T(8,128)} %constant.50.clone.along_ref, f32[16,16]{1,0:T(8,128)} %constant.51.clone.sines_ref, ...), custom_call_target="tpu_custom_call" | custom-call | tf_op jit(solution)/shard_map/pallas_call | solution.py:635
  113.6 21.2 %all_to_all.44 = f32[32,32,128]{2,1,0:T(8,128)S(1)} all-to-all(f32[32,32,128]{2,1,0:T(8,128)} %bitcast.43), channel_id=1, replica_groups=mesh['rows'=4,'cols'=8] {'rows','cols'}, dimensions={0} | all-to-all | bytes 1048576 | tf_op jit(solution)/shard_map/all_to_all | solution.py:622
  134.7 0.7 shard_map.274
  135.5 6.3 %shard_map.273 = (f32[2048,128]{1,0:T(8,128)}, f32[5,2048,128]{2,1,0:T(8,128)}) custom-call(s32[32,128]{1,0:T(8,128)S(1)} %copy-done.5, f32[1,32,64,128]{3,2,1,0:T(8,128)} %shard_map.270.rest_0_.w_ref, f32[5,2048,128]{2,1,0:T(8,128)} %bitcast.40, f32[32,64,128]{2,1,0:T(8,128)} %get-tuple-element.31.refs_7_.after_ref.coef_ref, ...), custom_call_target="tpu_custom_call", output_to_operand_aliasing={{1}: (2, {})} | custom-call | tf_op jit(solution)/shard_map/pallas_call | solution.py:952
Async XLA Ops:
  0.6 15.5 %copy-start.3 = (bf16[512,256]{1,0:T(8,128)(2,1)S(1)}, bf16[512,256]{1,0:T(8,128)(2,1)}, u32[]{:S(2)}) copy-start(bf16[512,256]{1,0:T(8,128)(2,1)} %constant.47.clone.y_ref) | copy-start | bytes 786436
  0.6 15.5 %copy-start.7 = (bf16[256,256]{1,0:T(8,128)(2,1)S(1)}, bf16[256,256]{1,0:T(8,128)(2,1)}, u32[]{:S(2)}) copy-start(bf16[256,256]{1,0:T(8,128)(2,1)} %constant.46.clone.x_ref) | copy-start | bytes 393220
  0.7 15.5 %copy-start.8 = (f32[64,128]{1,0:T(8,128)S(1)}, f32[64,128]{1,0:T(8,128)}, u32[]{:S(2)}) copy-start(f32[64,128]{1,0:T(8,128)} %constant.45.clone.base_ref) | copy-start | bytes 98308
  0.7 15.4 %copy-start.12 = (bf16[128,64]{1,0:T(8,128)(2,1)S(1)}, bf16[128,64]{1,0:T(8,128)(2,1)}, u32[]{:S(2)}) copy-start(bf16[128,64]{1,0:T(8,128)(2,1)} %constant.44.clone.z_ref) | copy-start | bytes 49156
  0.7 21.5 %copy-start.13 = (bf16[128,128]{1,0:T(8,128)(2,1)S(1)}, bf16[128,128]{1,0:T(8,128)(2,1)}, u32[]{:S(2)}) copy-start(bf16[128,128]{1,0:T(8,128)(2,1)} %constant.48.clone.take_ref) | copy-start | bytes 98308
  6.8 24.1 %collective-permute-start.2 = (f32[968,128]{1,0:T(8,128)}, f32[968,128]{1,0:T(8,128)S(1)}, u32[]{:S(2)}, u32[]{:S(2)}) collective-permute-start(f32[968,128]{1,0:T(8,128)} %get-tuple-element.25), channel_id=1, source_target_pairs={{0,1},{1,2},{2,3},{3,4},{4,5},{5,6},{6,7},{8,9},{9,10},{10,11},{11... | collective-permute-start | bytes 1486856 | tf_op jit(solution)/shard_map/ppermute | solution.py:284
  9.2 21.7 %collective-permute-start.3 = (f32[968,128]{1,0:T(8,128)}, f32[968,128]{1,0:T(8,128)S(1)}, u32[]{:S(2)}, u32[]{:S(2)}) collective-permute-start(f32[968,128]{1,0:T(8,128)} %get-tuple-element.26), channel_id=1, source_target_pairs={{1,0},{2,1},{3,2},{4,3},{5,4},{6,5},{7,6},{9,8},{10,9},{11,10},{12... | collective-permute-start | bytes 1486856 | tf_op jit(solution)/shard_map/ppermute | solution.py:284
  10.5 9.8 %collective-permute-start = (f32[3,88,128]{2,1,0:T(8,128)}, f32[3,88,128]{2,1,0:T(8,128)S(1)}, u32[]{:S(2)}, u32[]{:S(2)}) collective-permute-start(f32[3,88,128]{2,1,0:T(8,128)} %get-tuple-element.23), channel_id=1, source_target_pairs={{0,8},{8,16},{16,24},{1,9},{9,17},{17,25},{2,10},{10,18},{18,26},{... | collective-permute-start | bytes 405512 | tf_op jit(solution)/shard_map/ppermute | solution.py:284
  14.8 7.4 %collective-permute-start.1 = (f32[3,88,128]{2,1,0:T(8,128)}, f32[3,88,128]{2,1,0:T(8,128)S(1)}, u32[]{:S(2)}, u32[]{:S(2)}) collective-permute-start(f32[3,88,128]{2,1,0:T(8,128)} %get-tuple-element.24), channel_id=1, source_target_pairs={{8,0},{16,8},{24,16},{9,1},{17,9},{25,17},{10,2},{18,10},{26,18},{... | collective-permute-start | bytes 405512 | tf_op jit(solution)/shard_map/ppermute | solution.py:284
  16.1 0.7 copy-start.4
  16.8 14.0 %copy-start.5 = (s32[32,128]{1,0:T(8,128)S(1)}, s32[32,128]{1,0:T(8,128)}, u32[]{:S(2)}) copy-start(s32[32,128]{1,0:T(8,128)} %get-tuple-element.22.dep_ref) | copy-start | bytes 49156
  20.2 25.3 %copy-start = (f32[32,64,128]{2,1,0:T(8,128)}, f32[32,64,128]{2,1,0:T(8,128)S(1)}, u32[]{:S(2)}) copy-start(f32[32,64,128]{2,1,0:T(8,128)S(1)} %shard_map.264.coef_ref.back_coef_ref) | copy-start | bytes 3145732
  23.4 22.1 %all-to-all-start = ((f32[32,8,128]{2,1,0:T(8,128)}), f32[32,8,128]{2,1,0:T(8,128)S(1)}, u32[]{:S(2)}, u32[]{:S(2)}) async-start(f32[32,8,128]{2,1,0:T(8,128)} %bitcast.3), calls=%async_computation | async-start | bytes 262144 | tf_op jit(solution)/shard_map/all_to_all | solution.py:622
  45.5 0.7 copy-start.17
  49.9 21.7 %all-to-all-start.1 = ((f32[32,8,128]{2,1,0:T(8,128)}), f32[32,8,128]{2,1,0:T(8,128)S(1)}, u32[]{:S(2)}, u32[]{:S(2)}) async-start(f32[32,8,128]{2,1,0:T(8,128)} %bitcast.20), calls=%async_computation.1 | async-start | bytes 262144 | tf_op jit(solution)/shard_map/all_to_all | solution.py:622
  56.0 0.9 copy-start.1
  56.9 14.8 %copy-start.2 = (bf16[512,256]{1,0:T(8,128)(2,1)S(1)}, bf16[512,256]{1,0:T(8,128)(2,1)}, u32[]{:S(2)}) copy-start(bf16[512,256]{1,0:T(8,128)(2,1)} %constant.57.clone.y_back_ref.y_ref) | copy-start | bytes 786436
  56.9 14.8 %copy-start.6 = (bf16[256,256]{1,0:T(8,128)(2,1)S(1)}, bf16[256,256]{1,0:T(8,128)(2,1)}, u32[]{:S(2)}) copy-start(bf16[256,256]{1,0:T(8,128)(2,1)} %constant.58.clone.x_back_ref.x_ref) | copy-start | bytes 393220
  56.9 14.8 %copy-start.9 = (bf16[256,128]{1,0:T(8,128)(2,1)S(1)}, bf16[256,128]{1,0:T(8,128)(2,1)}, u32[]{:S(2)}) copy-start(bf16[256,128]{1,0:T(8,128)(2,1)} %constant.60.clone.give_ref) | copy-start | bytes 196612
  56.9 14.8 %copy-start.10 = (bf16[256,256]{1,0:T(8,128)(2,1)S(1)}, bf16[256,256]{1,0:T(8,128)(2,1)}, u32[]{:S(2)}) copy-start(bf16[256,256]{1,0:T(8,128)(2,1)} %w_in_ref.1) | copy-start | bytes 393220
  56.9 14.8 %copy-start.11 = (bf16[128,64]{1,0:T(8,128)(2,1)S(1)}, bf16[128,64]{1,0:T(8,128)(2,1)}, u32[]{:S(2)}) copy-start(bf16[128,64]{1,0:T(8,128)(2,1)} %constant.59.clone.z_back_ref.z_ref) | copy-start | bytes 49156
  56.9 14.8 %copy-start.14 = (bf16[256,63]{0,1:T(8,128)(2,1)S(1)}, bf16[256,63]{0,1:T(8,128)(2,1)}, u32[]{:S(2)}) copy-start(bf16[256,63]{0,1:T(8,128)(2,1)} %param.30) | copy-start | bytes 96772
  56.9 14.8 %copy-start.15 = (f32[256]{0:T(256)S(1)}, f32[256]{0:T(256)}, u32[]{:S(2)}) copy-start(f32[256]{0:T(256)} %param.29) | copy-start | bytes 3076
  87.5 21.2 %all-to-all-start.2 = ((f32[32,32,128]{2,1,0:T(8,128)}), f32[32,32,128]{2,1,0:T(8,128)S(1)}, u32[]{:S(2)}, u32[]{:S(2)}) async-start(f32[32,32,128]{2,1,0:T(8,128)} %bitcast.10), calls=%async_computation.2 | async-start | bytes 1048576 | tf_op jit(solution)/shard_map/all_to_all | solution.py:622
  108.7 0.8 copy-start.16

commit v4 on v3

--- a/solution.py
+++ b/solution.py
@@ -20,6 +20,14 @@
 PIECES = 4
 
 
+def spread_rows(rows, b):
+    east = rows.shape[1]
+    ys = east // SUB
+    return jnp.concatenate(
+        [jnp.broadcast_to(rows[y : y + 1], (SUB, east)) for y in range(b * ys, (b + 1) * ys)], 0
+    )
+
+
 def pack_kernel(mask_ref, depth_ref, *refs):
     field_refs, refs = refs[:PIECES], refs[PIECES:]
     dep_ref, xfirst_ref, xlast_ref, yfirst_ref, ylast_ref = refs
@@ -27,17 +35,20 @@
     north, east = dep_ref.shape
     some = field_refs[0].shape[1] // north
     levels = PIECES * some
-    per = east // north
-    blocks = levels // per
+    ys = east // SUB
+    halves = north // ys
+    blocks = levels // SUB * halves
     dep = jnp.where(mask_ref[...] == 1, depth_ref[...], 0)
     dep_ref[...] = dep
-    tiled = jnp.concatenate([dep] * per, 0)
-    level_in_block = lax.broadcasted_iota(jnp.int32, (east, east), 0) // north
+    first_levels = lax.broadcasted_iota(jnp.int32, (SUB, east), 0)
     for t in range(blocks):
-        piece, at = divmod(t * east, some * north)
-        block = field_refs[piece][0, at : at + east, :]
-        masked = jnp.where(level_in_block + t * per < tiled, block, 0.0)
-        turned = masked.T
+        low, start = t // halves * SUB, t % halves * ys
+        piece, at = divmod(low, some)
+        tiles = []
+        for y in range(start, start + ys):
+            value = field_refs[piece][0, pl.ds(at * north + y, SUB, stride=north), :]
+            tiles.append(jnp.where(first_levels + low < dep[y : y + 1], value, 0.0))
+        turned = jnp.concatenate(tiles, 0).T
         row = field * blocks + t
         for s in range(HALO):
             xfirst_ref[s, pl.ds(row, 1), :] = turned[s : s + 1]
@@ -57,13 +68,15 @@
         end = FIELDS * HALO * levels
         yfirst_ref[end:, :] = jnp.broadcast_to(depths[:1], (SUB, east))
         ylast_ref[end:, :] = jnp.broadcast_to(depths[north - 1 :], (SUB, east))
-        turned = tiled.astype(jnp.float32).T
         for s in range(HALO):
-            high = east - HALO + s
-            xfirst_ref[s, FIELDS * blocks :, :] = jnp.broadcast_to(turned[s : s + 1], (SUB, east))
-            xlast_ref[s, FIELDS * blocks :, :] = jnp.broadcast_to(
-                turned[high : high + 1], (SUB, east)
-            )
+            xfirst_ref[s, FIELDS * blocks :, :] = jnp.zeros((SUB, east), jnp.float32)
+            xlast_ref[s, FIELDS * blocks :, :] = jnp.zeros((SUB, east), jnp.float32)
+        for b in range(halves):
+            turned = spread_rows(depths, b).T
+            row = FIELDS * blocks + b
+            for s in range(HALO):
+                xfirst_ref[s, row : row + 1, :] = turned[s : s + 1]
+                xlast_ref[s, row : row + 1, :] = turned[east - HALO + s : east - HALO + s + 1]
 
 
 def pack_edges(fields, mask, depth):
@@ -120,10 +133,10 @@
     ) = refs[-12:]
     step = pl.program_id(0) + begin
     north, east = dep_ref.shape
-    per = east // north
-    blocks = SUB // per
+    ys = east // SUB
+    blocks = north // ys
     all_blocks = (xlo_ref.shape[1] - SUB) // FIELDS
-    levels = all_blocks * per
+    levels = all_blocks // blocks * SUB
     depth_row = FIELDS * all_blocks
     depth_end = FIELDS * HALO * levels
     faces = range(0, east + SUB, SUB)
@@ -132,16 +145,21 @@
     @pl.when(step == begin)
     def _():
         depths = dep_ref[...].astype(jnp.float32)
-        deep[SUB : SUB + east, :] = jnp.concatenate([depths] * per, 0).T
-        deep[SUB - 1 : SUB, :] = xlo_ref[HALO - 1, depth_row : depth_row + 1, :]
-        deep[SUB + east : SUB + east + 1, :] = xhi_ref[0, depth_row : depth_row + 1, :]
-        both[:east, :] = jnp.minimum(deep[SUB - 1 : SUB - 1 + east, :], deep[SUB : SUB + east, :])
-        both[east : east + 1, :] = jnp.minimum(
-            deep[SUB + east - 1 : SUB + east, :], deep[SUB + east : SUB + east + 1, :]
-        )
+        for b in range(blocks):
+            row = depth_row + b
+            deep[SUB : SUB + east, :] = spread_rows(depths, b).T
+            deep[SUB - 1 : SUB, :] = xlo_ref[HALO - 1, row : row + 1, :]
+            deep[SUB + east : SUB + east + 1, :] = xhi_ref[0, row : row + 1, :]
+            both[b, :east, :] = jnp.minimum(
+                deep[SUB - 1 : SUB - 1 + east, :], deep[SUB : SUB + east, :]
+            )
+            both[b, east : east + 1, :] = jnp.minimum(
+                deep[SUB + east - 1 : SUB + east, :], deep[SUB + east : SUB + east + 1, :]
+            )
 
     level = (lax.broadcasted_iota(jnp.int32, (SUB, east), 0) + first_level).astype(jnp.float32)
-    side_level = lax.broadcasted_iota(jnp.int32, (SUB, east), 1) // north + first_level
+    height = lax.broadcasted_iota(jnp.int32, (SUB, east), 1) % SUB + first_level
+    height = height.astype(jnp.float32)
     depths = dep_ref[...].astype(jnp.float32)
     wets[0] = (level < ylo_ref[depth_end : depth_end + 1, :]).astype(jnp.float32)
     wets[north + 1] = (level < yhi_ref[depth_end : depth_end + 1, :]).astype(jnp.float32)
@@ -165,21 +183,15 @@
                 lines[slot, b, SUB + east + s : SUB + east + s + 1, :] = xhi_ref[
                     s, pl.ds(row, 1), :
                 ]
-            turned = field[0, b * east : (b + 1) * east, :].T
-            height = (side_level + b * per).astype(jnp.float32)
-            for r in range(0, east, SUB):
-                wet = height < deep[SUB + r : 2 * SUB + r, :]
-                lines[slot, b, SUB + r : 2 * SUB + r, :] = jnp.where(
-                    wet, turned[r : r + SUB], 0.0
-                )
+            tile = cells[slot, HALO + b * ys : HALO + (b + 1) * ys].reshape(east, east)
+            lines[slot, b, SUB : SUB + east, :] = tile.T
 
     for b in range(blocks):
-        height = (side_level + b * per).astype(jnp.float32)
         for r in faces:
             speed = (0.5 * TIME_STEP) * (
                 lines[0, b, SUB + r - 1 : 2 * SUB + r - 1, :] + lines[0, b, SUB + r : 2 * SUB + r, :]
             )
-            speed = jnp.where(height < both[r : r + SUB, :], speed, 0.0)
+            speed = jnp.where(height < both[b, r : r + SUB, :], speed, 0.0)
             su[b, r : r + SUB, :] = speed
             su6[b, r : r + SUB, :] = jnp.abs(speed) * (1.0 / 6.0)
         if spread_ref is not None:
@@ -189,7 +201,7 @@
             sides[b * east : (b + 1) * east, :] = change.T
     if spread_ref is not None:
         for y in range(north):
-            spread_ref[y] = sides[pl.ds(y, SUB, stride=north), :] + 0.5 * (
+            spread_ref[y] = sides[y * SUB : (y + 1) * SUB, :] + 0.5 * (
                 cells[1, y + HALO + 1] - cells[1, y + HALO - 1]
             )
     for y in range(north + 1):
@@ -225,7 +237,7 @@
             inclines.append(line[-1] - line[-2])
             north_face = face_flux(inclines[-5:], line[-4], line[-3], sv[y], sv6[y])
             if y > 0:
-                change = sides[pl.ds(y - 1, SUB, stride=north), :] + (south - north_face)
+                change = sides[(y - 1) * SUB : y * SUB, :] + (south - north_face)
                 adv_ref[f - first, y - 1] = wets[y] * (line[-4] + change)
             south = north_face
         return carry
@@ -261,7 +273,7 @@
         input_output_aliases={len(staged) + 6 + i: i for i in range(len(filled))},
         scratch_shapes=[
             pltpu.VMEM((east + 2 * SUB, east), f32),
-            pltpu.VMEM((east + SUB, east), f32),
+            pltpu.VMEM((blocks, east + SUB, east), f32),
             pltpu.VMEM((len(staged), blocks, east + 3 * SUB, east), f32),
             pltpu.VMEM((blocks, east + 3 * SUB, east), f32),
             pltpu.VMEM((blocks, east + SUB, east), f32),
@@ -622,7 +634,7 @@
     return lax.all_to_all(block, AXES, split_axis=0, concat_axis=0, tiled=True)
 
 
-def interface(tables, received, *after):
+def interface(tables, received, limit, *after):
     device = lax.axis_index("rows") * lax.axis_size("cols") + lax.axis_index("cols")
     operands = (
         received, tables.cross, tables.along, tables.sines, tables.wide_forward, tables.wide_back,
@@ -641,7 +653,7 @@
             out_specs=whole_spec(received),
         ),
         out_shape=jax.ShapeDtypeStruct(received.shape, jnp.float32),
-        compiler_params=call_params(56 << 20),
+        compiler_params=call_params(limit),
     )(device.astype(jnp.int32).reshape(1), *operands, *after)
 
 
@@ -970,7 +982,7 @@
             pltpu.VMEM(coef.shape, jnp.float32),
             pltpu.VMEM((tables.share * tables.count * PARTS, east), jnp.float32),
         ],
-        compiler_params=call_params(),
+        compiler_params=call_params(44 << 20),
     )(dep, w, new.reshape(FIELDS, levels * north, east), coef, jumps, *consts)
     return pressure.reshape(levels, north, east), new.reshape(FIELDS, levels, north, east)
 
@@ -1022,7 +1034,7 @@
     back_coef = adjoint_local(tables, cotangent, dep)
     back_edges = adjoint_edges(tables, back_coef, edges[0], edges[1])
     half = advect(fields, dep, TRACERS, edges, (0, steps // 2), back_edges)
-    back_jumps = interface(tables, exchange(back_edges), half[1])
+    back_jumps = interface(tables, exchange(back_edges), 56 << 20, half[1])
     adv, spread = advect(fields, dep, TRACERS, edges, (steps // 2, steps), back_jumps, half)
     mixed, coef, send = column(
         tables, dep, adv, spread, fields, cotangent, in_weight, in_bias, out_weight,
@@ -1031,7 +1043,7 @@
     received = exchange(send)
     w = advect(fields, dep, (2,), edges, (0, steps), coef)[0]
     new = gather_fields(adv, mixed, coef)
-    jumps = exchange(interface(tables, received, w, new))
+    jumps = exchange(interface(tables, received, VMEM_LIMIT, w, new))
     pressure, new_fields = pressure_finish(tables, dep, w, new, coef, jumps)
     return (new_fields, pressure, *split_sums(tables, jumps, inputs, hidden, outputs))
 

time: 143 us -> 138 us (0.965)
  Pallas kernels: 85.9 us -> 81.5 us
    pallas_call x3, Pallas kernels: 39.3 us -> 36.6 us  [advect(): pl.pallas_call(functools.partial(advect_kernel, tracers, staged, span[0],...]
    pallas_call x1, Pallas kernels: 6.29 us -> 4.73 us  [pressure_finish(): pl.pallas_call(functools.partial(pressure_kernel, tables), grid=(1,), in_...]
    unnamed x36 -> x50, local copies, waits for them, and re-layouts: 3.16 us -> 3.25 us
  transfers between devices with their start and end apart: 7 -> 7, of which waited for: 2 -> 2; matrix products, arithmetic and copies ran while one was open for 0% -> 0% of each run, Pallas kernels for 35% -> 34%
where the time goes in v4:
time: 138 us; the launch traced here: 137 us
  Pallas kernels  81.5 us (59%)
  starting transfers between devices  28.4 us (21%)
  blocking collectives  20.7 us (15%)
  local copies, waits for them, and re-layouts  3.25 us (2%)
  waiting for transfers between devices  2.53 us (2%)
    pallas_call x3, Pallas kernels, advect(): pl.pallas_call(functools.partial(advect_kernel, tracers, staged, span[0],...  36.6 us
    all_to_all x1, blocking collectives, exchange(): return lax.all_to_all(block, AXES, split_axis=0, concat_axis=0, tiled=True)  20.7 us
    all_to_all x3, starting transfers between devices, exchange(): return lax.all_to_all(block, AXES, split_axis=0, concat_axis=0, tiled=True)  19.1 us
    pallas_call x1, Pallas kernels, column(): pl.pallas_call(functools.partial(column_kernel, tables), grid=(north // S...  15.5 us
    pallas_call x1, Pallas kernels, pack_edges(): pl.pallas_call(pack_kernel, grid=(FIELDS,), in_specs=[whole(mask), whole(...  7.05 us
    pallas_call x2, Pallas kernels, interface(): pl.pallas_call(functools.partial(interface_kernel, tables), grid_spec=plt...  6.98 us
    ppermute x2, starting transfers between devices, shift_both(): lax.ppermute(last, axis, forward)  6.69 us
    pallas_call x1, Pallas kernels, gather_fields(): pl.pallas_call(gather_kernel, grid=(north // SUB,), in_specs=[block, bloc...  5.43 us
  transfers between devices with their start and end apart: 7, of which 2 were waited for; matrix products, arithmetic and copies ran while one was open for 0% of the time, Pallas kernels for 34%

profile of v4, /device:TPU:0, one launch (start us, length us, event | category | flops | bytes accessed | tf_op | source)
XLA Modules:
  0.0 137.4 jit_solution(9074096148059503888)
XLA Ops:
  0.6 0.0 copy-start.6
  0.6 0.0 copy-start.11
  0.7 0.0 copy-start.13
  0.7 0.0 copy-start.18
  0.7 0.0 copy-start.19
  0.7 7.0 %shard_map.263 = (s32[32,128]{1,0:T(8,128)}, f32[3,88,128]{2,1,0:T(8,128)}, f32[3,88,128]{2,1,0:T(8,128)}, f32[968,128]{1,0:T(8,128)}, f32[968,128]{1,0:T(8,128)}) custom-call(s32[32,128]{1,0:T(8,128)} %mask_ref.1, s32[32,128]{1,0:T(8,128)} %depth_ref.1, f32[5,2048,128]{2,1,0:T(8,128)} %bitcast.27, f32[5,2048,128]{2,1,0:T(8,128)} %bitcast.28, ...), custom_call_target="tpu_custom_call" | custom-call | tf_op jit(solution)/shard_map/pallas_call | solution.py:88
  7.7 2.4 %collective-permute-start.2 = (f32[968,128]{1,0:T(8,128)}, f32[968,128]{1,0:T(8,128)S(1)}, u32[]{:S(2)}, u32[]{:S(2)}) collective-permute-start(f32[968,128]{1,0:T(8,128)} %get-tuple-element.25), channel_id=1, source_target_pairs={{0,1},{1,2},{2,3},{3,4},{4,5},{5,6},{6,7},{8,9},{9,10},{10,11},{11... | collective-permute-start | bytes 1486856 | tf_op jit(solution)/shard_map/ppermute | solution.py:296
  10.1 1.3 collective-permute-start.3
  11.4 4.3 %collective-permute-start = (f32[3,88,128]{2,1,0:T(8,128)}, f32[3,88,128]{2,1,0:T(8,128)S(1)}, u32[]{:S(2)}, u32[]{:S(2)}) collective-permute-start(f32[3,88,128]{2,1,0:T(8,128)} %get-tuple-element.23), channel_id=1, source_target_pairs={{0,8},{8,16},{16,24},{1,9},{9,17},{17,25},{2,10},{10,18},{18,26},{... | collective-permute-start | bytes 405512 | tf_op jit(solution)/shard_map/ppermute | solution.py:296
  15.8 1.3 collective-permute-start.1
  17.1 0.0 copy-done.6
  17.1 0.0 copy-done.11
  17.1 0.0 copy-done.13
  17.1 0.0 copy-done.18
  17.1 0.0 copy-start.7
  17.1 0.7 copy-done.7
  17.8 3.3 %shard_map.264.coef_ref.back_coef_ref = f32[32,64,128]{2,1,0:T(8,128)S(1)} custom-call(s32[32,128]{1,0:T(8,128)S(1)} %copy-done.7, f32[5,2048,128]{2,1,0:T(8,128)} %bitcast.42, bf16[128,64]{1,0:T(8,128)(2,1)S(1)} %copy-done.18, f32[64,128]{1,0:T(8,128)S(1)} %copy-done.13, bf16[256,256]{1,0:T(8,128)(2,1)S(1)} %copy-done.11, bf16[512,256]{1,0:T(8,128)(2,1)S(1)} %copy-done.6), custom_call_target="tpu_custom_call" | custom-call | tf_op jit(solution)/shard_map/pallas_call | solution.py:687
  21.2 0.0 copy-start
  21.2 0.0 collective-permute-done.rest_0_.refs_4_.refs_3_
  21.2 2.0 %collective-permute-done.1.rest_1_.refs_5_.refs_4_ = f32[3,88,128]{2,1,0:T(8,128)S(1)} collective-permute-done((f32[3,88,128]{2,1,0:T(8,128)}, f32[3,88,128]{2,1,0:T(8,128)S(1)}, u32[]{:S(2)}, u32[]{:S(2)}) %collective-permute-start.1) | collective-permute-done | bytes 135200 | tf_op jit(solution)/shard_map/ppermute | solution.py:296
  23.2 0.0 copy-done.19
  23.2 1.2 shard_map.265.refs_8_
  24.4 7.4 %all-to-all-start = ((f32[32,8,128]{2,1,0:T(8,128)}), f32[32,8,128]{2,1,0:T(8,128)S(1)}, u32[]{:S(2)}, u32[]{:S(2)}) async-start(f32[32,8,128]{2,1,0:T(8,128)} %bitcast.3), calls=%async_computation | async-start | bytes 262144 | tf_op jit(solution)/shard_map/all_to_all | solution.py:634
  31.8 0.0 collective-permute-done.2.refs_6_.refs_5_
  31.8 0.0 collective-permute-done.3.refs_7_.refs_6_
  31.8 0.0 copy-done.8
  31.8 13.5 %shard_map.266 = (f32[4,32,64,128]{3,2,1,0:T(8,128)}, f32[32,64,128]{2,1,0:T(8,128)}) custom-call(s32[32,128]{1,0:T(8,128)S(1)} %copy-done.8, f32[5,2048,128]{2,1,0:T(8,128)} %bitcast.31, f32[5,2048,128]{2,1,0:T(8,128)} %bitcast.32, f32[5,2048,128]{2,1,0:T(8,128)} %bitcast.33, f32[5,2048,128]{2,1,0:T(8,128)} %bitcast.34, ...), custom_call_target="tpu_custom_call" | custom-call | tf_op jit(solution)/shard_map/pallas_call | solution.py:261
  45.3 0.0 copy-done
  45.3 0.0 all-to-all-done
  45.3 0.0 copy-start.24
  45.4 0.6 copy-done.24
  46.0 3.8 %shard_map.267.refs_8_ = f32[256,128]{1,0:T(8,128)} custom-call(s32[1]{0:T(128)} %bitcast.1.device_ref, f32[256,128]{1,0:T(8,128)} %bitcast.45, f32[64,10,128]{2,1,0:T(8,128)} %constant.49.clone.cross_ref, f32[64,8,512]{2,1,0:T(8,128)} %constant.50.clone.along_ref, f32[16,16]{1,0:T(8,128)} %constant.51.clone.sines_ref, ...), custom_call_target="tpu_custom_call" | custom-call | tf_op jit(solution)/shard_map/pallas_call | solution.py:647
  49.8 6.0 %all-to-all-start.1 = ((f32[32,8,128]{2,1,0:T(8,128)}), f32[32,8,128]{2,1,0:T(8,128)S(1)}, u32[]{:S(2)}, u32[]{:S(2)}) async-start(f32[32,8,128]{2,1,0:T(8,128)} %bitcast.22), calls=%async_computation.1 | async-start | bytes 262144 | tf_op jit(solution)/shard_map/all_to_all | solution.py:634
  55.8 0.0 copy-start.4
  55.8 0.9 copy-done.4
  56.7 0.0 copy-start.17
  56.7 0.0 copy-start.20
  56.8 0.0 copy-start.23
  56.8 13.5 %shard_map.268 = (f32[4,32,64,128]{3,2,1,0:T(8,128)}, f32[32,64,128]{2,1,0:T(8,128)}) custom-call(s32[32,128]{1,0:T(8,128)S(1)} %copy-done.8, f32[5,2048,128]{2,1,0:T(8,128)} %bitcast.35, f32[5,2048,128]{2,1,0:T(8,128)} %bitcast.36, f32[5,2048,128]{2,1,0:T(8,128)} %bitcast.37, ...), custom_call_target="tpu_custom_call", output_to_operand_aliasing={{0}: (10, {}), {1}: (11, {})} | custom-call | tf_op jit(solution)/shard_map/pallas_call | solution.py:261
  70.3 0.0 all-to-all-done.1
  70.3 0.0 copy-done.5
  70.3 0.0 copy-done.9
  70.3 0.0 copy-done.14
  70.3 0.0 copy-done.16
  70.4 0.0 copy-done.17
  70.4 0.0 copy-done.20
  70.4 0.0 copy-done.23
  70.4 15.5 %shard_map.269 = (f32[2,32,64,128]{3,2,1,0:T(8,128)}, f32[32,64,128]{2,1,0:T(8,128)}, f32[1024,128]{1,0:T(8,128)S(1)}) custom-call(s32[32,128]{1,0:T(8,128)S(1)} %copy-done.8, f32[4,32,64,128]{3,2,1,0:T(8,128)} %get-tuple-element.29.adv_ref, f32[32,64,128]{2,1,0:T(8,128)} %get-tuple-element.30.spread_ref, f32[5,64,32,128]{3,2,1,0:T(8,128)} %w_field_ref.1, ...), custom_call_target="tpu_custom_call" | custom-call | tf_op jit(solution)/shard_map/pallas_call | solution.py:869
  85.9 0.8 copy-done.12
  86.7 5.7 %all-to-all-start.2 = ((f32[32,32,128]{2,1,0:T(8,128)}), f32[32,32,128]{2,1,0:T(8,128)S(1)}, u32[]{:S(2)}, u32[]{:S(2)}) async-start(f32[32,32,128]{2,1,0:T(8,128)} %bitcast.24), calls=%async_computation.2 | async-start | bytes 1048576 | tf_op jit(solution)/shard_map/all_to_all | solution.py:634
  92.4 5.4 %shard_map.271.rest_1_ = f32[5,64,32,128]{3,2,1,0:T(8,128)} custom-call(f32[4,32,64,128]{3,2,1,0:T(8,128)} %get-tuple-element.29.adv_ref, f32[2,32,64,128]{3,2,1,0:T(8,128)} %get-tuple-element.32.mixed_ref, f32[32,64,128]{2,1,0:T(8,128)} %get-tuple-element.31.refs_7_.after_ref.coef_ref), custom_call_target="tpu_custom_call" | custom-call | tf_op jit(solution)/shard_map/pallas_call | solution.py:921
  97.8 0.0 copy-start.21
  97.9 0.0 copy-start.22
  97.9 9.6 %shard_map.270.rest_0_.w_ref = f32[1,32,64,128]{3,2,1,0:T(8,128)} custom-call(s32[32,128]{1,0:T(8,128)S(1)} %copy-done.8, f32[5,2048,128]{2,1,0:T(8,128)} %bitcast.39, f32[5,2048,128]{2,1,0:T(8,128)} %bitcast.40, f32[5,2048,128]{2,1,0:T(8,128)} %bitcast.41, f32[3,88,128]{2,1,0:T(8,128)S(1)} %collective-permute-done.rest_0_.refs_4_.refs_3_, ...), custom_call_target="tpu_custom_call" | custom-call | tf_op jit(solution)/shard_map/pallas_call | solution.py:261
  107.4 0.5 all-to-all-done.2
  108.0 0.0 copy-done.3
  108.0 0.0 copy-done.10
  108.0 0.0 copy-done.15
  108.0 0.0 copy-start.2
  108.0 3.2 %shard_map.272 = f32[1024,128]{1,0:T(8,128)S(1)} custom-call(s32[1]{0:T(128)} %bitcast.1.device_ref, f32[1024,128]{1,0:T(8,128)S(1)} %bitcast.20, f32[64,10,128]{2,1,0:T(8,128)S(1)} %copy-done.3, f32[64,8,512]{2,1,0:T(8,128)} %constant.50.clone.along_ref, f32[16,16]{1,0:T(8,128)S(1)} %copy-done.21, bf16[2,512,512]{2,1,0:T(8,128)(2,1)} %constant.52.clone.forward_ref, ...), custom_call_target="tpu_custom_call" | custom-call | tf_op jit(solution)/shard_map/pallas_call | solution.py:647
  111.2 20.7 %all_to_all.44 = f32[32,32,128]{2,1,0:T(8,128)S(1)} all-to-all(f32[32,32,128]{2,1,0:T(8,128)S(1)} %bitcast.21), channel_id=1, replica_groups=mesh['rows'=4,'cols'=8] {'rows','cols'}, dimensions={0} | all-to-all | bytes 1048576 | tf_op jit(solution)/shard_map/all_to_all | solution.py:634
  131.9 0.7 shard_map.274
  132.7 0.0 copy-done.1
  132.7 4.7 %shard_map.273 = (f32[2048,128]{1,0:T(8,128)}, f32[5,2048,128]{2,1,0:T(8,128)}) custom-call(s32[32,128]{1,0:T(8,128)S(1)} %copy-done.8, f32[1,32,64,128]{3,2,1,0:T(8,128)S(1)} %copy-done.2, f32[5,2048,128]{2,1,0:T(8,128)} %bitcast.43, f32[32,64,128]{2,1,0:T(8,128)S(1)} %copy-done.1, f32[1024,128]{1,0:T(8,128)S(1)} %bitcast.19, ...), custom_call_target="tpu_custom_call", output_to_operand_aliasing={{1}: (2, {})} | custom-call | tf_op jit(solution)/shard_map/pallas_call | solution.py:964
  (13 shorter events, 0.0 us)
Async XLA Ops:
  0.6 16.4 %copy-start.6 = (bf16[512,256]{1,0:T(8,128)(2,1)S(1)}, bf16[512,256]{1,0:T(8,128)(2,1)}, u32[]{:S(2)}) copy-start(bf16[512,256]{1,0:T(8,128)(2,1)} %constant.47.clone.y_ref) | copy-start | bytes 786436
  0.6 16.4 %copy-start.11 = (bf16[256,256]{1,0:T(8,128)(2,1)S(1)}, bf16[256,256]{1,0:T(8,128)(2,1)}, u32[]{:S(2)}) copy-start(bf16[256,256]{1,0:T(8,128)(2,1)} %constant.46.clone.x_ref) | copy-start | bytes 393220
  0.7 16.4 %copy-start.13 = (f32[64,128]{1,0:T(8,128)S(1)}, f32[64,128]{1,0:T(8,128)}, u32[]{:S(2)}) copy-start(f32[64,128]{1,0:T(8,128)} %constant.45.clone.base_ref) | copy-start | bytes 98308
  0.7 16.4 %copy-start.18 = (bf16[128,64]{1,0:T(8,128)(2,1)S(1)}, bf16[128,64]{1,0:T(8,128)(2,1)}, u32[]{:S(2)}) copy-start(bf16[128,64]{1,0:T(8,128)(2,1)} %constant.44.clone.z_ref) | copy-start | bytes 49156
  0.7 22.5 %copy-start.19 = (bf16[128,128]{1,0:T(8,128)(2,1)S(1)}, bf16[128,128]{1,0:T(8,128)(2,1)}, u32[]{:S(2)}) copy-start(bf16[128,128]{1,0:T(8,128)(2,1)} %constant.48.clone.take_ref) | copy-start | bytes 98308
  7.7 24.1 %collective-permute-start.2 = (f32[968,128]{1,0:T(8,128)}, f32[968,128]{1,0:T(8,128)S(1)}, u32[]{:S(2)}, u32[]{:S(2)}) collective-permute-start(f32[968,128]{1,0:T(8,128)} %get-tuple-element.25), channel_id=1, source_target_pairs={{0,1},{1,2},{2,3},{3,4},{4,5},{5,6},{6,7},{8,9},{9,10},{10,11},{11... | collective-permute-start | bytes 1486856 | tf_op jit(solution)/shard_map/ppermute | solution.py:296
  10.1 21.7 %collective-permute-start.3 = (f32[968,128]{1,0:T(8,128)}, f32[968,128]{1,0:T(8,128)S(1)}, u32[]{:S(2)}, u32[]{:S(2)}) collective-permute-start(f32[968,128]{1,0:T(8,128)} %get-tuple-element.26), channel_id=1, source_target_pairs={{1,0},{2,1},{3,2},{4,3},{5,4},{6,5},{7,6},{9,8},{10,9},{11,10},{12... | collective-permute-start | bytes 1486856 | tf_op jit(solution)/shard_map/ppermute | solution.py:296
  11.4 9.7 %collective-permute-start = (f32[3,88,128]{2,1,0:T(8,128)}, f32[3,88,128]{2,1,0:T(8,128)S(1)}, u32[]{:S(2)}, u32[]{:S(2)}) collective-permute-start(f32[3,88,128]{2,1,0:T(8,128)} %get-tuple-element.23), channel_id=1, source_target_pairs={{0,8},{8,16},{16,24},{1,9},{9,17},{17,25},{2,10},{10,18},{18,26},{... | collective-permute-start | bytes 405512 | tf_op jit(solution)/shard_map/ppermute | solution.py:296
  15.8 7.4 %collective-permute-start.1 = (f32[3,88,128]{2,1,0:T(8,128)}, f32[3,88,128]{2,1,0:T(8,128)S(1)}, u32[]{:S(2)}, u32[]{:S(2)}) collective-permute-start(f32[3,88,128]{2,1,0:T(8,128)} %get-tuple-element.24), channel_id=1, source_target_pairs={{8,0},{16,8},{24,16},{9,1},{17,9},{25,17},{10,2},{18,10},{26,18},{... | collective-permute-start | bytes 405512 | tf_op jit(solution)/shard_map/ppermute | solution.py:296
  17.1 0.7 copy-start.7
  17.8 14.0 %copy-start.8 = (s32[32,128]{1,0:T(8,128)S(1)}, s32[32,128]{1,0:T(8,128)}, u32[]{:S(2)}) copy-start(s32[32,128]{1,0:T(8,128)} %get-tuple-element.22.dep_ref) | copy-start | bytes 49156
  21.2 24.2 %copy-start = (f32[32,64,128]{2,1,0:T(8,128)}, f32[32,64,128]{2,1,0:T(8,128)S(1)}, u32[]{:S(2)}) copy-start(f32[32,64,128]{2,1,0:T(8,128)S(1)} %shard_map.264.coef_ref.back_coef_ref) | copy-start | bytes 3145732
  24.4 21.0 %all-to-all-start = ((f32[32,8,128]{2,1,0:T(8,128)}), f32[32,8,128]{2,1,0:T(8,128)S(1)}, u32[]{:S(2)}, u32[]{:S(2)}) async-start(f32[32,8,128]{2,1,0:T(8,128)} %bitcast.3), calls=%async_computation | async-start | bytes 262144 | tf_op jit(solution)/shard_map/all_to_all | solution.py:634
  45.3 0.7 copy-start.24
  49.8 20.6 %all-to-all-start.1 = ((f32[32,8,128]{2,1,0:T(8,128)}), f32[32,8,128]{2,1,0:T(8,128)S(1)}, u32[]{:S(2)}, u32[]{:S(2)}) async-start(f32[32,8,128]{2,1,0:T(8,128)} %bitcast.22), calls=%async_computation.1 | async-start | bytes 262144 | tf_op jit(solution)/shard_map/all_to_all | solution.py:634
  55.8 0.9 copy-start.4
  56.7 13.6 %copy-start.5 = (bf16[512,256]{1,0:T(8,128)(2,1)S(1)}, bf16[512,256]{1,0:T(8,128)(2,1)}, u32[]{:S(2)}) copy-start(bf16[512,256]{1,0:T(8,128)(2,1)} %constant.57.clone.y_back_ref.y_ref) | copy-start | bytes 786436
  56.7 13.6 %copy-start.9 = (bf16[256,256]{1,0:T(8,128)(2,1)S(1)}, bf16[256,256]{1,0:T(8,128)(2,1)}, u32[]{:S(2)}) copy-start(bf16[256,256]{1,0:T(8,128)(2,1)} %constant.58.clone.x_back_ref.x_ref) | copy-start | bytes 393220
  56.7 13.6 %copy-start.14 = (bf16[256,128]{1,0:T(8,128)(2,1)S(1)}, bf16[256,128]{1,0:T(8,128)(2,1)}, u32[]{:S(2)}) copy-start(bf16[256,128]{1,0:T(8,128)(2,1)} %constant.60.clone.give_ref) | copy-start | bytes 196612
  56.7 13.6 %copy-start.16 = (bf16[256,256]{1,0:T(8,128)(2,1)S(1)}, bf16[256,256]{1,0:T(8,128)(2,1)}, u32[]{:S(2)}) copy-start(bf16[256,256]{1,0:T(8,128)(2,1)} %w_in_ref.1) | copy-start | bytes 393220
  56.7 13.6 %copy-start.17 = (bf16[128,64]{1,0:T(8,128)(2,1)S(1)}, bf16[128,64]{1,0:T(8,128)(2,1)}, u32[]{:S(2)}) copy-start(bf16[128,64]{1,0:T(8,128)(2,1)} %constant.59.clone.z_back_ref.z_ref) | copy-start | bytes 49156
  56.7 13.6 %copy-start.20 = (bf16[256,63]{0,1:T(8,128)(2,1)S(1)}, bf16[256,63]{0,1:T(8,128)(2,1)}, u32[]{:S(2)}) copy-start(bf16[256,63]{0,1:T(8,128)(2,1)} %param.30) | copy-start | bytes 96772
  56.8 13.6 %copy-start.23 = (f32[256]{0:T(256)S(1)}, f32[256]{0:T(256)}, u32[]{:S(2)}) copy-start(f32[256]{0:T(256)} %param.29) | copy-start | bytes 3076
  85.9 0.9 copy-start.12
  86.7 21.2 %all-to-all-start.2 = ((f32[32,32,128]{2,1,0:T(8,128)}), f32[32,32,128]{2,1,0:T(8,128)S(1)}, u32[]{:S(2)}, u32[]{:S(2)}) async-start(f32[32,32,128]{2,1,0:T(8,128)} %bitcast.24), calls=%async_computation.2 | async-start | bytes 1048576 | tf_op jit(solution)/shard_map/all_to_all | solution.py:634
  97.8 10.1 %copy-start.3 = (f32[64,10,128]{2,1,0:T(8,128)S(1)}, f32[64,10,128]{2,1,0:T(8,128)}, u32[]{:S(2)}) copy-start(f32[64,10,128]{2,1,0:T(8,128)} %constant.49.clone.cross_ref) | copy-start | bytes 983044
  97.8 10.1 %copy-start.10 = (f32[2,128,128]{2,1,0:T(8,128)S(1)}, f32[2,128,128]{2,1,0:T(8,128)}, u32[]{:S(2)}) copy-start(f32[2,128,128]{2,1,0:T(8,128)} %constant.55.clone.column_ref) | copy-start | bytes 393220
  97.8 10.1 %copy-start.15 = (f32[3,32,128]{2,1,0:T(8,128)S(1)}, f32[3,32,128]{2,1,0:T(8,128)}, u32[]{:S(2)}) copy-start(f32[3,32,128]{2,1,0:T(8,128)} %constant.54.clone.strip_ref) | copy-start | bytes 147460
  97.8 10.1 %copy-start.21 = (f32[16,16]{1,0:T(8,128)S(1)}, f32[16,16]{1,0:T(8,128)}, u32[]{:S(2)}) copy-start(f32[16,16]{1,0:T(8,128)} %constant.51.clone.sines_ref) | copy-start | bytes 3076
  97.9 10.1 %copy-start.22 = (f32[8,128]{1,0:T(8,128)S(1)}, f32[8,128]{1,0:T(8,128)}, u32[]{:S(2)}) copy-start(f32[8,128]{1,0:T(8,128)} %constant.56.clone.lines_ref) | copy-start | bytes 12292
  108.0 24.7 %copy-start.1 = (f32[32,64,128]{2,1,0:T(8,128)S(1)}, f32[32,64,128]{2,1,0:T(8,128)}, u32[]{:S(2)}) copy-start(f32[32,64,128]{2,1,0:T(8,128)} %get-tuple-element.31.refs_7_.after_ref.coef_ref) | copy-start | bytes 3145732
  108.0 24.7 %copy-start.2 = (f32[1,32,64,128]{3,2,1,0:T(8,128)S(1)}, f32[1,32,64,128]{3,2,1,0:T(8,128)}, u32[]{:S(2)}) copy-start(f32[1,32,64,128]{3,2,1,0:T(8,128)} %shard_map.270.rest_0_.w_ref) | copy-start | bytes 3145732

commit v5 on v4

--- a/solution.py
+++ b/solution.py
@@ -212,7 +212,7 @@
 
     first = len(staged) - len(tracers)
 
-    def advance_field(f, carry):
+    def advance_field(f):
         for b in range(blocks):
             for r in range(0, east + 2 * SUB, SUB):
                 ahead = lines[f, b, r + 1 : r + 1 + SUB, :]
@@ -240,9 +240,9 @@
                 change = sides[(y - 1) * SUB : y * SUB, :] + (south - north_face)
                 adv_ref[f - first, y - 1] = wets[y] * (line[-4] + change)
             south = north_face
-        return carry
-
-    lax.fori_loop(first, len(staged), advance_field, 0)
+
+    for f in range(first, len(staged)):
+        advance_field(f)
 
 
 def advect(fields, dep, tracers, edges, span, after, filled=()):

time: 138 us -> 136 us (0.986)
  Pallas kernels: 81.5 us -> 79.1 us
    pallas_call x3, Pallas kernels: 36.6 us -> 34.1 us  [advect(): pl.pallas_call(functools.partial(advect_kernel, tracers, staged, span[0],...]
  transfers between devices with their start and end apart: 7 -> 7, of which waited for: 2 -> 2; matrix products, arithmetic and copies ran while one was open for 0% -> 0% of each run, Pallas kernels for 34% -> 33%
where the time goes in v5:
time: 136 us; the launch traced here: 135 us
  Pallas kernels  79.1 us (58%)
  starting transfers between devices  28.4 us (21%)
  blocking collectives  20.7 us (15%)
  local copies, waits for them, and re-layouts  3.25 us (2%)
  waiting for transfers between devices  2.53 us (2%)
    pallas_call x3, Pallas kernels, advect(): pl.pallas_call(functools.partial(advect_kernel, tracers, staged, span[0],...  34.1 us
    all_to_all x1, blocking collectives, exchange(): return lax.all_to_all(block, AXES, split_axis=0, concat_axis=0, tiled=True)  20.7 us
    all_to_all x3, starting transfers between devices, exchange(): return lax.all_to_all(block, AXES, split_axis=0, concat_axis=0, tiled=True)  19.1 us
    pallas_call x1, Pallas kernels, column(): pl.pallas_call(functools.partial(column_kernel, tables), grid=(north // S...  15.5 us
    pallas_call x1, Pallas kernels, pack_edges(): pl.pallas_call(pack_kernel, grid=(FIELDS,), in_specs=[whole(mask), whole(...  7.05 us
    pallas_call x2, Pallas kernels, interface(): pl.pallas_call(functools.partial(interface_kernel, tables), grid_spec=plt...  6.98 us
    ppermute x2, starting transfers between devices, shift_both(): lax.ppermute(last, axis, forward)  6.69 us
    pallas_call x1, Pallas kernels, gather_fields(): pl.pallas_call(gather_kernel, grid=(north // SUB,), in_specs=[block, bloc...  5.43 us
  transfers between devices with their start and end apart: 7, of which 2 were waited for; matrix products, arithmetic and copies ran while one was open for 0% of the time, Pallas kernels for 33%

profile of v5, /device:TPU:0, one launch (start us, length us, event | category | flops | bytes accessed | tf_op | source)
XLA Modules:
  0.0 134.9 jit_solution(15348993514554274019)
XLA Ops:
  0.6 0.0 copy-start.6
  0.6 0.0 copy-start.11
  0.7 0.0 copy-start.13
  0.7 0.0 copy-start.18
  0.7 0.0 copy-start.19
  0.7 7.0 %shard_map.263 = (s32[32,128]{1,0:T(8,128)}, f32[3,88,128]{2,1,0:T(8,128)}, f32[3,88,128]{2,1,0:T(8,128)}, f32[968,128]{1,0:T(8,128)}, f32[968,128]{1,0:T(8,128)}) custom-call(s32[32,128]{1,0:T(8,128)} %mask_ref.1, s32[32,128]{1,0:T(8,128)} %depth_ref.1, f32[5,2048,128]{2,1,0:T(8,128)} %bitcast.27, f32[5,2048,128]{2,1,0:T(8,128)} %bitcast.28, ...), custom_call_target="tpu_custom_call" | custom-call | tf_op jit(solution)/shard_map/pallas_call | solution.py:88
  7.7 2.4 %collective-permute-start.2 = (f32[968,128]{1,0:T(8,128)}, f32[968,128]{1,0:T(8,128)S(1)}, u32[]{:S(2)}, u32[]{:S(2)}) collective-permute-start(f32[968,128]{1,0:T(8,128)} %get-tuple-element.25), channel_id=1, source_target_pairs={{0,1},{1,2},{2,3},{3,4},{4,5},{5,6},{6,7},{8,9},{9,10},{10,11},{11... | collective-permute-start | bytes 1486856 | tf_op jit(solution)/shard_map/ppermute | solution.py:296
  10.1 1.3 collective-permute-start.3
  11.4 4.3 %collective-permute-start = (f32[3,88,128]{2,1,0:T(8,128)}, f32[3,88,128]{2,1,0:T(8,128)S(1)}, u32[]{:S(2)}, u32[]{:S(2)}) collective-permute-start(f32[3,88,128]{2,1,0:T(8,128)} %get-tuple-element.23), channel_id=1, source_target_pairs={{0,8},{8,16},{16,24},{1,9},{9,17},{17,25},{2,10},{10,18},{18,26},{... | collective-permute-start | bytes 405512 | tf_op jit(solution)/shard_map/ppermute | solution.py:296
  15.8 1.3 collective-permute-start.1
  17.1 0.0 copy-done.6
  17.1 0.0 copy-done.11
  17.1 0.0 copy-done.13
  17.1 0.0 copy-done.18
  17.1 0.0 copy-start.7
  17.1 0.7 copy-done.7
  17.8 3.3 %shard_map.264.coef_ref.back_coef_ref = f32[32,64,128]{2,1,0:T(8,128)S(1)} custom-call(s32[32,128]{1,0:T(8,128)S(1)} %copy-done.7, f32[5,2048,128]{2,1,0:T(8,128)} %bitcast.42, bf16[128,64]{1,0:T(8,128)(2,1)S(1)} %copy-done.18, f32[64,128]{1,0:T(8,128)S(1)} %copy-done.13, bf16[256,256]{1,0:T(8,128)(2,1)S(1)} %copy-done.11, bf16[512,256]{1,0:T(8,128)(2,1)S(1)} %copy-done.6), custom_call_target="tpu_custom_call" | custom-call | tf_op jit(solution)/shard_map/pallas_call | solution.py:687
  21.2 0.0 copy-start
  21.2 0.0 collective-permute-done.rest_0_.refs_4_.refs_3_
  21.2 2.0 %collective-permute-done.1.rest_1_.refs_5_.refs_4_ = f32[3,88,128]{2,1,0:T(8,128)S(1)} collective-permute-done((f32[3,88,128]{2,1,0:T(8,128)}, f32[3,88,128]{2,1,0:T(8,128)S(1)}, u32[]{:S(2)}, u32[]{:S(2)}) %collective-permute-start.1) | collective-permute-done | bytes 135200 | tf_op jit(solution)/shard_map/ppermute | solution.py:296
  23.2 0.0 copy-done.19
  23.2 1.2 shard_map.265.refs_8_
  24.4 7.4 %all-to-all-start = ((f32[32,8,128]{2,1,0:T(8,128)}), f32[32,8,128]{2,1,0:T(8,128)S(1)}, u32[]{:S(2)}, u32[]{:S(2)}) async-start(f32[32,8,128]{2,1,0:T(8,128)} %bitcast.3), calls=%async_computation | async-start | bytes 262144 | tf_op jit(solution)/shard_map/all_to_all | solution.py:634
  31.8 0.0 collective-permute-done.2.refs_6_.refs_5_
  31.8 0.0 collective-permute-done.3.refs_7_.refs_6_
  31.8 0.0 copy-done.8
  31.8 12.2 %shard_map.266 = (f32[4,32,64,128]{3,2,1,0:T(8,128)}, f32[32,64,128]{2,1,0:T(8,128)}) custom-call(s32[32,128]{1,0:T(8,128)S(1)} %copy-done.8, f32[5,2048,128]{2,1,0:T(8,128)} %bitcast.31, f32[5,2048,128]{2,1,0:T(8,128)} %bitcast.32, f32[5,2048,128]{2,1,0:T(8,128)} %bitcast.33, f32[5,2048,128]{2,1,0:T(8,128)} %bitcast.34, ...), custom_call_target="tpu_custom_call" | custom-call | tf_op jit(solution)/shard_map/pallas_call | solution.py:261
  44.1 0.0 copy-done
  44.1 0.0 all-to-all-done
  44.1 0.0 copy-start.24
  44.1 0.6 copy-done.24
  44.8 3.8 %shard_map.267.refs_8_ = f32[256,128]{1,0:T(8,128)} custom-call(s32[1]{0:T(128)} %bitcast.1.device_ref, f32[256,128]{1,0:T(8,128)} %bitcast.45, f32[64,10,128]{2,1,0:T(8,128)} %constant.49.clone.cross_ref, f32[64,8,512]{2,1,0:T(8,128)} %constant.50.clone.along_ref, f32[16,16]{1,0:T(8,128)} %constant.51.clone.sines_ref, ...), custom_call_target="tpu_custom_call" | custom-call | tf_op jit(solution)/shard_map/pallas_call | solution.py:647
  48.5 6.0 %all-to-all-start.1 = ((f32[32,8,128]{2,1,0:T(8,128)}), f32[32,8,128]{2,1,0:T(8,128)S(1)}, u32[]{:S(2)}, u32[]{:S(2)}) async-start(f32[32,8,128]{2,1,0:T(8,128)} %bitcast.22), calls=%async_computation.1 | async-start | bytes 262144 | tf_op jit(solution)/shard_map/all_to_all | solution.py:634
  54.5 0.0 copy-start.4
  54.5 0.9 copy-done.4
  55.5 0.0 copy-start.17
  55.5 0.0 copy-start.20
  55.5 0.0 copy-start.23
  55.5 12.3 %shard_map.268 = (f32[4,32,64,128]{3,2,1,0:T(8,128)}, f32[32,64,128]{2,1,0:T(8,128)}) custom-call(s32[32,128]{1,0:T(8,128)S(1)} %copy-done.8, f32[5,2048,128]{2,1,0:T(8,128)} %bitcast.35, f32[5,2048,128]{2,1,0:T(8,128)} %bitcast.36, f32[5,2048,128]{2,1,0:T(8,128)} %bitcast.37, ...), custom_call_target="tpu_custom_call", output_to_operand_aliasing={{0}: (10, {}), {1}: (11, {})} | custom-call | tf_op jit(solution)/shard_map/pallas_call | solution.py:261
  67.8 0.0 all-to-all-done.1
  67.8 0.0 copy-done.5
  67.8 0.0 copy-done.9
  67.9 0.0 copy-done.14
  67.9 0.0 copy-done.16
  67.9 0.0 copy-done.17
  67.9 0.0 copy-done.20
  67.9 0.0 copy-done.23
  67.9 15.5 %shard_map.269 = (f32[2,32,64,128]{3,2,1,0:T(8,128)}, f32[32,64,128]{2,1,0:T(8,128)}, f32[1024,128]{1,0:T(8,128)S(1)}) custom-call(s32[32,128]{1,0:T(8,128)S(1)} %copy-done.8, f32[4,32,64,128]{3,2,1,0:T(8,128)} %get-tuple-element.29.adv_ref, f32[32,64,128]{2,1,0:T(8,128)} %get-tuple-element.30.spread_ref, f32[5,64,32,128]{3,2,1,0:T(8,128)} %w_field_ref.1, ...), custom_call_target="tpu_custom_call" | custom-call | tf_op jit(solution)/shard_map/pallas_call | solution.py:869
  83.4 0.8 copy-done.12
  84.3 5.7 %all-to-all-start.2 = ((f32[32,32,128]{2,1,0:T(8,128)}), f32[32,32,128]{2,1,0:T(8,128)S(1)}, u32[]{:S(2)}, u32[]{:S(2)}) async-start(f32[32,32,128]{2,1,0:T(8,128)} %bitcast.24), calls=%async_computation.2 | async-start | bytes 1048576 | tf_op jit(solution)/shard_map/all_to_all | solution.py:634
  89.9 5.4 %shard_map.271.rest_1_ = f32[5,64,32,128]{3,2,1,0:T(8,128)} custom-call(f32[4,32,64,128]{3,2,1,0:T(8,128)} %get-tuple-element.29.adv_ref, f32[2,32,64,128]{3,2,1,0:T(8,128)} %get-tuple-element.32.mixed_ref, f32[32,64,128]{2,1,0:T(8,128)} %get-tuple-element.31.refs_7_.after_ref.coef_ref), custom_call_target="tpu_custom_call" | custom-call | tf_op jit(solution)/shard_map/pallas_call | solution.py:921
  95.4 0.0 copy-start.21
  95.4 0.0 copy-start.22
  95.4 9.6 %shard_map.270.rest_0_.w_ref = f32[1,32,64,128]{3,2,1,0:T(8,128)} custom-call(s32[32,128]{1,0:T(8,128)S(1)} %copy-done.8, f32[5,2048,128]{2,1,0:T(8,128)} %bitcast.39, f32[5,2048,128]{2,1,0:T(8,128)} %bitcast.40, f32[5,2048,128]{2,1,0:T(8,128)} %bitcast.41, f32[3,88,128]{2,1,0:T(8,128)S(1)} %collective-permute-done.rest_0_.refs_4_.refs_3_, ...), custom_call_target="tpu_custom_call" | custom-call | tf_op jit(solution)/shard_map/pallas_call | solution.py:261
  105.0 0.5 all-to-all-done.2
  105.5 0.0 copy-done.3
  105.5 0.0 copy-done.10
  105.5 0.0 copy-done.15
  105.5 0.0 copy-done.21
  105.5 0.0 copy-start.2
  105.5 3.2 %shard_map.272 = f32[1024,128]{1,0:T(8,128)S(1)} custom-call(s32[1]{0:T(128)} %bitcast.1.device_ref, f32[1024,128]{1,0:T(8,128)S(1)} %bitcast.20, f32[64,10,128]{2,1,0:T(8,128)S(1)} %copy-done.3, f32[64,8,512]{2,1,0:T(8,128)} %constant.50.clone.along_ref, f32[16,16]{1,0:T(8,128)S(1)} %copy-done.21, bf16[2,512,512]{2,1,0:T(8,128)(2,1)} %constant.52.clone.forward_ref, ...), custom_call_target="tpu_custom_call" | custom-call | tf_op jit(solution)/shard_map/pallas_call | solution.py:647
  108.8 20.7 %all_to_all.44 = f32[32,32,128]{2,1,0:T(8,128)S(1)} all-to-all(f32[32,32,128]{2,1,0:T(8,128)S(1)} %bitcast.21), channel_id=1, replica_groups=mesh['rows'=4,'cols'=8] {'rows','cols'}, dimensions={0} | all-to-all | bytes 1048576 | tf_op jit(solution)/shard_map/all_to_all | solution.py:634
  129.4 0.7 shard_map.274
  130.2 4.7 %shard_map.273 = (f32[2048,128]{1,0:T(8,128)}, f32[5,2048,128]{2,1,0:T(8,128)}) custom-call(s32[32,128]{1,0:T(8,128)S(1)} %copy-done.8, f32[1,32,64,128]{3,2,1,0:T(8,128)S(1)} %copy-done.2, f32[5,2048,128]{2,1,0:T(8,128)} %bitcast.43, f32[32,64,128]{2,1,0:T(8,128)S(1)} %copy-done.1, f32[1024,128]{1,0:T(8,128)S(1)} %bitcast.19, ...), custom_call_target="tpu_custom_call", output_to_operand_aliasing={{1}: (2, {})} | custom-call | tf_op jit(solution)/shard_map/pallas_call | solution.py:964
  (13 shorter events, 0.0 us)
Async XLA Ops:
  0.6 16.4 %copy-start.6 = (bf16[512,256]{1,0:T(8,128)(2,1)S(1)}, bf16[512,256]{1,0:T(8,128)(2,1)}, u32[]{:S(2)}) copy-start(bf16[512,256]{1,0:T(8,128)(2,1)} %constant.47.clone.y_ref) | copy-start | bytes 786436
  0.6 16.4 %copy-start.11 = (bf16[256,256]{1,0:T(8,128)(2,1)S(1)}, bf16[256,256]{1,0:T(8,128)(2,1)}, u32[]{:S(2)}) copy-start(bf16[256,256]{1,0:T(8,128)(2,1)} %constant.46.clone.x_ref) | copy-start | bytes 393220
  0.7 16.4 %copy-start.13 = (f32[64,128]{1,0:T(8,128)S(1)}, f32[64,128]{1,0:T(8,128)}, u32[]{:S(2)}) copy-start(f32[64,128]{1,0:T(8,128)} %constant.45.clone.base_ref) | copy-start | bytes 98308
  0.7 16.4 %copy-start.18 = (bf16[128,64]{1,0:T(8,128)(2,1)S(1)}, bf16[128,64]{1,0:T(8,128)(2,1)}, u32[]{:S(2)}) copy-start(bf16[128,64]{1,0:T(8,128)(2,1)} %constant.44.clone.z_ref) | copy-start | bytes 49156
  0.7 22.5 %copy-start.19 = (bf16[128,128]{1,0:T(8,128)(2,1)S(1)}, bf16[128,128]{1,0:T(8,128)(2,1)}, u32[]{:S(2)}) copy-start(bf16[128,128]{1,0:T(8,128)(2,1)} %constant.48.clone.take_ref) | copy-start | bytes 98308
  7.7 24.1 %collective-permute-start.2 = (f32[968,128]{1,0:T(8,128)}, f32[968,128]{1,0:T(8,128)S(1)}, u32[]{:S(2)}, u32[]{:S(2)}) collective-permute-start(f32[968,128]{1,0:T(8,128)} %get-tuple-element.25), channel_id=1, source_target_pairs={{0,1},{1,2},{2,3},{3,4},{4,5},{5,6},{6,7},{8,9},{9,10},{10,11},{11... | collective-permute-start | bytes 1486856 | tf_op jit(solution)/shard_map/ppermute | solution.py:296
  10.1 21.7 %collective-permute-start.3 = (f32[968,128]{1,0:T(8,128)}, f32[968,128]{1,0:T(8,128)S(1)}, u32[]{:S(2)}, u32[]{:S(2)}) collective-permute-start(f32[968,128]{1,0:T(8,128)} %get-tuple-element.26), channel_id=1, source_target_pairs={{1,0},{2,1},{3,2},{4,3},{5,4},{6,5},{7,6},{9,8},{10,9},{11,10},{12... | collective-permute-start | bytes 1486856 | tf_op jit(solution)/shard_map/ppermute | solution.py:296
  11.4 9.7 %collective-permute-start = (f32[3,88,128]{2,1,0:T(8,128)}, f32[3,88,128]{2,1,0:T(8,128)S(1)}, u32[]{:S(2)}, u32[]{:S(2)}) collective-permute-start(f32[3,88,128]{2,1,0:T(8,128)} %get-tuple-element.23), channel_id=1, source_target_pairs={{0,8},{8,16},{16,24},{1,9},{9,17},{17,25},{2,10},{10,18},{18,26},{... | collective-permute-start | bytes 405512 | tf_op jit(solution)/shard_map/ppermute | solution.py:296
  15.8 7.4 %collective-permute-start.1 = (f32[3,88,128]{2,1,0:T(8,128)}, f32[3,88,128]{2,1,0:T(8,128)S(1)}, u32[]{:S(2)}, u32[]{:S(2)}) collective-permute-start(f32[3,88,128]{2,1,0:T(8,128)} %get-tuple-element.24), channel_id=1, source_target_pairs={{8,0},{16,8},{24,16},{9,1},{17,9},{25,17},{10,2},{18,10},{26,18},{... | collective-permute-start | bytes 405512 | tf_op jit(solution)/shard_map/ppermute | solution.py:296
  17.1 0.7 copy-start.7
  17.8 14.0 %copy-start.8 = (s32[32,128]{1,0:T(8,128)S(1)}, s32[32,128]{1,0:T(8,128)}, u32[]{:S(2)}) copy-start(s32[32,128]{1,0:T(8,128)} %get-tuple-element.22.dep_ref) | copy-start | bytes 49156
  21.2 22.9 %copy-start = (f32[32,64,128]{2,1,0:T(8,128)}, f32[32,64,128]{2,1,0:T(8,128)S(1)}, u32[]{:S(2)}) copy-start(f32[32,64,128]{2,1,0:T(8,128)S(1)} %shard_map.264.coef_ref.back_coef_ref) | copy-start | bytes 3145732
  24.4 19.7 %all-to-all-start = ((f32[32,8,128]{2,1,0:T(8,128)}), f32[32,8,128]{2,1,0:T(8,128)S(1)}, u32[]{:S(2)}, u32[]{:S(2)}) async-start(f32[32,8,128]{2,1,0:T(8,128)} %bitcast.3), calls=%async_computation | async-start | bytes 262144 | tf_op jit(solution)/shard_map/all_to_all | solution.py:634
  44.1 0.7 copy-start.24
  48.5 19.3 %all-to-all-start.1 = ((f32[32,8,128]{2,1,0:T(8,128)}), f32[32,8,128]{2,1,0:T(8,128)S(1)}, u32[]{:S(2)}, u32[]{:S(2)}) async-start(f32[32,8,128]{2,1,0:T(8,128)} %bitcast.22), calls=%async_computation.1 | async-start | bytes 262144 | tf_op jit(solution)/shard_map/all_to_all | solution.py:634
  54.5 0.9 copy-start.4
  55.5 12.4 %copy-start.5 = (bf16[512,256]{1,0:T(8,128)(2,1)S(1)}, bf16[512,256]{1,0:T(8,128)(2,1)}, u32[]{:S(2)}) copy-start(bf16[512,256]{1,0:T(8,128)(2,1)} %constant.57.clone.y_back_ref.y_ref) | copy-start | bytes 786436
  55.5 12.4 %copy-start.9 = (bf16[256,256]{1,0:T(8,128)(2,1)S(1)}, bf16[256,256]{1,0:T(8,128)(2,1)}, u32[]{:S(2)}) copy-start(bf16[256,256]{1,0:T(8,128)(2,1)} %constant.58.clone.x_back_ref.x_ref) | copy-start | bytes 393220
  55.5 12.4 %copy-start.14 = (bf16[256,128]{1,0:T(8,128)(2,1)S(1)}, bf16[256,128]{1,0:T(8,128)(2,1)}, u32[]{:S(2)}) copy-start(bf16[256,128]{1,0:T(8,128)(2,1)} %constant.60.clone.give_ref) | copy-start | bytes 196612
  55.5 12.4 %copy-start.16 = (bf16[256,256]{1,0:T(8,128)(2,1)S(1)}, bf16[256,256]{1,0:T(8,128)(2,1)}, u32[]{:S(2)}) copy-start(bf16[256,256]{1,0:T(8,128)(2,1)} %w_in_ref.1) | copy-start | bytes 393220
  55.5 12.4 %copy-start.17 = (bf16[128,64]{1,0:T(8,128)(2,1)S(1)}, bf16[128,64]{1,0:T(8,128)(2,1)}, u32[]{:S(2)}) copy-start(bf16[128,64]{1,0:T(8,128)(2,1)} %constant.59.clone.z_back_ref.z_ref) | copy-start | bytes 49156
  55.5 12.4 %copy-start.20 = (bf16[256,63]{0,1:T(8,128)(2,1)S(1)}, bf16[256,63]{0,1:T(8,128)(2,1)}, u32[]{:S(2)}) copy-start(bf16[256,63]{0,1:T(8,128)(2,1)} %param.30) | copy-start | bytes 96772
  55.5 12.4 %copy-start.23 = (f32[256]{0:T(256)S(1)}, f32[256]{0:T(256)}, u32[]{:S(2)}) copy-start(f32[256]{0:T(256)} %param.29) | copy-start | bytes 3076
  83.4 0.9 copy-start.12
  84.3 21.2 %all-to-all-start.2 = ((f32[32,32,128]{2,1,0:T(8,128)}), f32[32,32,128]{2,1,0:T(8,128)S(1)}, u32[]{:S(2)}, u32[]{:S(2)}) async-start(f32[32,32,128]{2,1,0:T(8,128)} %bitcast.24), calls=%async_computation.2 | async-start | bytes 1048576 | tf_op jit(solution)/shard_map/all_to_all | solution.py:634
  95.4 10.1 %copy-start.3 = (f32[64,10,128]{2,1,0:T(8,128)S(1)}, f32[64,10,128]{2,1,0:T(8,128)}, u32[]{:S(2)}) copy-start(f32[64,10,128]{2,1,0:T(8,128)} %constant.49.clone.cross_ref) | copy-start | bytes 983044
  95.4 10.1 %copy-start.10 = (f32[2,128,128]{2,1,0:T(8,128)S(1)}, f32[2,128,128]{2,1,0:T(8,128)}, u32[]{:S(2)}) copy-start(f32[2,128,128]{2,1,0:T(8,128)} %constant.55.clone.column_ref) | copy-start | bytes 393220
  95.4 10.1 %copy-start.15 = (f32[3,32,128]{2,1,0:T(8,128)S(1)}, f32[3,32,128]{2,1,0:T(8,128)}, u32[]{:S(2)}) copy-start(f32[3,32,128]{2,1,0:T(8,128)} %constant.54.clone.strip_ref) | copy-start | bytes 147460
  95.4 10.1 %copy-start.21 = (f32[16,16]{1,0:T(8,128)S(1)}, f32[16,16]{1,0:T(8,128)}, u32[]{:S(2)}) copy-start(f32[16,16]{1,0:T(8,128)} %constant.51.clone.sines_ref) | copy-start | bytes 3076
  95.4 10.1 %copy-start.22 = (f32[8,128]{1,0:T(8,128)S(1)}, f32[8,128]{1,0:T(8,128)}, u32[]{:S(2)}) copy-start(f32[8,128]{1,0:T(8,128)} %constant.56.clone.lines_ref) | copy-start | bytes 12292
  105.5 24.7 %copy-start.1 = (f32[32,64,128]{2,1,0:T(8,128)S(1)}, f32[32,64,128]{2,1,0:T(8,128)}, u32[]{:S(2)}) copy-start(f32[32,64,128]{2,1,0:T(8,128)} %get-tuple-element.31.refs_7_.after_ref.coef_ref) | copy-start | bytes 3145732
  105.5 24.7 %copy-start.2 = (f32[1,32,64,128]{3,2,1,0:T(8,128)S(1)}, f32[1,32,64,128]{3,2,1,0:T(8,128)}, u32[]{:S(2)}) copy-start(f32[1,32,64,128]{3,2,1,0:T(8,128)} %shard_map.270.rest_0_.w_ref) | copy-start | bytes 3145732

commit v6 on v5

--- a/solution.py
+++ b/solution.py
@@ -935,10 +935,11 @@
 
 def pressure_kernel(
     tables, dep_ref, w_ref, new_ref, coef_ref, jump_ref, base_ref, y_ref, x_ref, z_ref, give_ref,
-    pressure_ref, out_ref, spec, jumps,
+    pressure_ref, out_ref, g_in_ref, g_bias_ref, g_out_ref, spec, jumps, flat,
 ):
     north, east, levels = tables.north, tables.east, tables.levels
     mine = tables.share * PARTS
+    split_kernel(mine, tables.count, jump_ref, g_in_ref, g_bias_ref, g_out_ref, flat)
     each = jump_ref.shape[0] // tables.count
     for part in range(mine):
         jumps[pl.ds(part, tables.count, stride=mine), :] = jump_ref[
@@ -957,11 +958,16 @@
     )
 
 
-def pressure_finish(tables, dep, w, new, coef, jumps):
+def pressure_finish(tables, dep, w, new, coef, jumps, inputs, hidden, outputs):
     levels, north, east = tables.levels, tables.north, tables.east
     consts = solve_consts(tables)
     flat = jax.ShapeDtypeStruct((levels * north, east), jnp.float32)
-    pressure, new = pl.pallas_call(
+    rows = jumps.shape[0] - tables.share * tables.count * PARTS
+    sums = [
+        jax.ShapeDtypeStruct(shape, jnp.float32)
+        for shape in ((inputs, hidden), (1, hidden), (outputs, hidden))
+    ]
+    pressure, new, g_in, g_bias, g_out = pl.pallas_call(
         functools.partial(pressure_kernel, tables),
         grid=(1,),
         in_specs=[
@@ -975,16 +981,22 @@
         out_specs=[
             whole_spec(flat),
             pl.BlockSpec((1, levels * north, east), lambda k: (2, 0, 0)),
-        ],
-        out_shape=[flat, jax.ShapeDtypeStruct((FIELDS, levels * north, east), jnp.float32)],
+            *(whole_spec(a) for a in sums),
+        ],
+        out_shape=[
+            flat, jax.ShapeDtypeStruct((FIELDS, levels * north, east), jnp.float32), *sums
+        ],
         input_output_aliases={2: 1},
         scratch_shapes=[
             pltpu.VMEM(coef.shape, jnp.float32),
             pltpu.VMEM((tables.share * tables.count * PARTS, east), jnp.float32),
+            pltpu.VMEM((rows, east), jnp.float32),
         ],
         compiler_params=call_params(44 << 20),
     )(dep, w, new.reshape(FIELDS, levels * north, east), coef, jumps, *consts)
-    return pressure.reshape(levels, north, east), new.reshape(FIELDS, levels, north, east)
+    pressure = pressure.reshape(levels, north, east)
+    new = new.reshape(FIELDS, levels, north, east)
+    return new, pressure, g_in, g_bias.reshape(hidden), g_out.T
 
 
 def split_kernel(skip, count, sums_ref, in_ref, bias_ref, out_ref, flat):
@@ -1001,25 +1013,6 @@
         at = wide + k * east
         out_ref[:, lanes] = flat[at : at + out_ref.shape[0], :]
         bias_ref[:, lanes] = flat[at + east // 2 : at + east // 2 + 1, :]
-
-
-def split_sums(tables, sums, inputs, hidden, outputs):
-    skip = tables.share * PARTS
-    rows = sums.shape[0] - skip * tables.count
-    shapes = [
-        jax.ShapeDtypeStruct(shape, jnp.float32)
-        for shape in ((inputs, hidden), (1, hidden), (outputs, hidden))
-    ]
-    g_in, g_bias, g_out = pl.pallas_call(
-        functools.partial(split_kernel, skip, tables.count),
-        grid=(1,),
-        in_specs=[whole_spec(sums)],
-        out_specs=[whole_spec(a) for a in shapes],
-        out_shape=shapes,
-        scratch_shapes=[pltpu.VMEM((rows, tables.east), jnp.float32)],
-        compiler_params=call_params(),
-    )(sums)
-    return g_in, g_bias.reshape(hidden), g_out.T
 
 
 def per_device(fields, cotangent, ocean_mask, depth_levels, in_weight, in_bias, out_weight):
@@ -1044,8 +1037,7 @@
     w = advect(fields, dep, (2,), edges, (0, steps), coef)[0]
     new = gather_fields(adv, mixed, coef)
     jumps = exchange(interface(tables, received, VMEM_LIMIT, w, new))
-    pressure, new_fields = pressure_finish(tables, dep, w, new, coef, jumps)
-    return (new_fields, pressure, *split_sums(tables, jumps, inputs, hidden, outputs))
+    return pressure_finish(tables, dep, w, new, coef, jumps, inputs, hidden, outputs)
 
 
 def solution(mesh):

time: 136 us -> 135 us (level)
  no operation moved by 1% of the time
where the time goes in v6:
time: 135 us; the launch traced here: 134 us
  Pallas kernels  78.4 us (58%)
  starting transfers between devices  28.4 us (21%)
  blocking collectives  20.7 us (15%)
  local copies, waits for them, and re-layouts  3.24 us (2%)
  waiting for transfers between devices  2.53 us (2%)
    pallas_call x3, Pallas kernels, advect(): pl.pallas_call(functools.partial(advect_kernel, tracers, staged, span[0],...  34.1 us
    all_to_all x1, blocking collectives, exchange(): return lax.all_to_all(block, AXES, split_axis=0, concat_axis=0, tiled=True)  20.7 us
    all_to_all x3, starting transfers between devices, exchange(): return lax.all_to_all(block, AXES, split_axis=0, concat_axis=0, tiled=True)  19.1 us
    pallas_call x1, Pallas kernels, column(): pl.pallas_call(functools.partial(column_kernel, tables), grid=(north // S...  15.5 us
    pallas_call x1, Pallas kernels, pack_edges(): pl.pallas_call(pack_kernel, grid=(FIELDS,), in_specs=[whole(mask), whole(...  7.05 us
    pallas_call x2, Pallas kernels, interface(): pl.pallas_call(functools.partial(interface_kernel, tables), grid_spec=plt...  6.98 us
    ppermute x2, starting transfers between devices, shift_both(): lax.ppermute(last, axis, forward)  6.69 us
    pallas_call x1, Pallas kernels, gather_fields(): pl.pallas_call(gather_kernel, grid=(north // SUB,), in_specs=[block, bloc...  5.43 us
  transfers between devices with their start and end apart: 7, of which 2 were waited for; matrix products, arithmetic and copies ran while one was open for 0% of the time, Pallas kernels for 33%

profile of v6, /device:TPU:0, one launch (start us, length us, event | category | flops | bytes accessed | tf_op | source)
XLA Modules:
  0.0 134.3 jit_solution(12375203356301371972)
XLA Ops:
  0.6 0.0 copy-start.6
  0.6 0.0 copy-start.11
  0.7 0.0 copy-start.13
  0.7 0.0 copy-start.18
  0.7 0.0 copy-start.19
  0.7 7.1 %shard_map.263 = (s32[32,128]{1,0:T(8,128)}, f32[3,88,128]{2,1,0:T(8,128)}, f32[3,88,128]{2,1,0:T(8,128)}, f32[968,128]{1,0:T(8,128)}, f32[968,128]{1,0:T(8,128)}) custom-call(s32[32,128]{1,0:T(8,128)} %mask_ref.1, s32[32,128]{1,0:T(8,128)} %depth_ref.1, f32[5,2048,128]{2,1,0:T(8,128)} %bitcast.26, f32[5,2048,128]{2,1,0:T(8,128)} %bitcast.27, ...), custom_call_target="tpu_custom_call" | custom-call | tf_op jit(solution)/shard_map/pallas_call | solution.py:88
  7.7 2.4 %collective-permute-start.2 = (f32[968,128]{1,0:T(8,128)}, f32[968,128]{1,0:T(8,128)S(1)}, u32[]{:S(2)}, u32[]{:S(2)}) collective-permute-start(f32[968,128]{1,0:T(8,128)} %get-tuple-element.25), channel_id=1, source_target_pairs={{0,1},{1,2},{2,3},{3,4},{4,5},{5,6},{6,7},{8,9},{9,10},{10,11},{11... | collective-permute-start | bytes 1486856 | tf_op jit(solution)/shard_map/ppermute | solution.py:296
  10.1 1.3 collective-permute-start.3
  11.4 4.3 %collective-permute-start = (f32[3,88,128]{2,1,0:T(8,128)}, f32[3,88,128]{2,1,0:T(8,128)S(1)}, u32[]{:S(2)}, u32[]{:S(2)}) collective-permute-start(f32[3,88,128]{2,1,0:T(8,128)} %get-tuple-element.23), channel_id=1, source_target_pairs={{0,8},{8,16},{16,24},{1,9},{9,17},{17,25},{2,10},{10,18},{18,26},{... | collective-permute-start | bytes 405512 | tf_op jit(solution)/shard_map/ppermute | solution.py:296
  15.8 1.3 collective-permute-start.1
  17.1 0.0 copy-done.6
  17.1 0.0 copy-done.11
  17.1 0.0 copy-done.13
  17.1 0.0 copy-done.18
  17.1 0.0 copy-start.7
  17.1 0.7 copy-done.7
  17.8 3.3 %shard_map.264.coef_ref.back_coef_ref = f32[32,64,128]{2,1,0:T(8,128)S(1)} custom-call(s32[32,128]{1,0:T(8,128)S(1)} %copy-done.7, f32[5,2048,128]{2,1,0:T(8,128)} %bitcast.41, bf16[128,64]{1,0:T(8,128)(2,1)S(1)} %copy-done.18, f32[64,128]{1,0:T(8,128)S(1)} %copy-done.13, bf16[256,256]{1,0:T(8,128)(2,1)S(1)} %copy-done.11, bf16[512,256]{1,0:T(8,128)(2,1)S(1)} %copy-done.6), custom_call_target="tpu_custom_call" | custom-call | tf_op jit(solution)/shard_map/pallas_call | solution.py:687
  21.2 0.0 copy-start
  21.2 0.0 collective-permute-done.rest_0_.refs_4_.refs_3_
  21.2 2.0 %collective-permute-done.1.rest_1_.refs_5_.refs_4_ = f32[3,88,128]{2,1,0:T(8,128)S(1)} collective-permute-done((f32[3,88,128]{2,1,0:T(8,128)}, f32[3,88,128]{2,1,0:T(8,128)S(1)}, u32[]{:S(2)}, u32[]{:S(2)}) %collective-permute-start.1) | collective-permute-done | bytes 135200 | tf_op jit(solution)/shard_map/ppermute | solution.py:296
  23.2 0.0 copy-done.19
  23.2 1.2 shard_map.265.refs_8_
  24.4 7.4 %all-to-all-start = ((f32[32,8,128]{2,1,0:T(8,128)}), f32[32,8,128]{2,1,0:T(8,128)S(1)}, u32[]{:S(2)}, u32[]{:S(2)}) async-start(f32[32,8,128]{2,1,0:T(8,128)} %bitcast.3), calls=%async_computation | async-start | bytes 262144 | tf_op jit(solution)/shard_map/all_to_all | solution.py:634
  31.8 0.0 collective-permute-done.2.refs_6_.refs_5_
  31.8 0.0 collective-permute-done.3.refs_7_.refs_6_
  31.8 0.0 copy-done.8
  31.8 12.2 %shard_map.266 = (f32[4,32,64,128]{3,2,1,0:T(8,128)}, f32[32,64,128]{2,1,0:T(8,128)}) custom-call(s32[32,128]{1,0:T(8,128)S(1)} %copy-done.8, f32[5,2048,128]{2,1,0:T(8,128)} %bitcast.30, f32[5,2048,128]{2,1,0:T(8,128)} %bitcast.31, f32[5,2048,128]{2,1,0:T(8,128)} %bitcast.32, f32[5,2048,128]{2,1,0:T(8,128)} %bitcast.33, ...), custom_call_target="tpu_custom_call" | custom-call | tf_op jit(solution)/shard_map/pallas_call | solution.py:261
  44.1 0.0 copy-done
  44.1 0.0 all-to-all-done
  44.1 0.0 copy-start.24
  44.1 0.6 copy-done.24
  44.8 3.8 %shard_map.267.refs_8_ = f32[256,128]{1,0:T(8,128)} custom-call(s32[1]{0:T(128)} %bitcast.1.device_ref, f32[256,128]{1,0:T(8,128)} %bitcast.44, f32[64,10,128]{2,1,0:T(8,128)} %constant.49.clone.cross_ref, f32[64,8,512]{2,1,0:T(8,128)} %constant.50.clone.along_ref, f32[16,16]{1,0:T(8,128)} %constant.51.clone.sines_ref, ...), custom_call_target="tpu_custom_call" | custom-call | tf_op jit(solution)/shard_map/pallas_call | solution.py:647
  48.5 6.0 %all-to-all-start.1 = ((f32[32,8,128]{2,1,0:T(8,128)}), f32[32,8,128]{2,1,0:T(8,128)S(1)}, u32[]{:S(2)}, u32[]{:S(2)}) async-start(f32[32,8,128]{2,1,0:T(8,128)} %bitcast.21), calls=%async_computation.1 | async-start | bytes 262144 | tf_op jit(solution)/shard_map/all_to_all | solution.py:634
  54.5 0.0 copy-start.4
  54.5 0.9 copy-done.4
  55.5 0.0 copy-start.17
  55.5 0.0 copy-start.20
  55.5 0.0 copy-start.23
  55.5 12.3 %shard_map.268 = (f32[4,32,64,128]{3,2,1,0:T(8,128)}, f32[32,64,128]{2,1,0:T(8,128)}) custom-call(s32[32,128]{1,0:T(8,128)S(1)} %copy-done.8, f32[5,2048,128]{2,1,0:T(8,128)} %bitcast.34, f32[5,2048,128]{2,1,0:T(8,128)} %bitcast.35, f32[5,2048,128]{2,1,0:T(8,128)} %bitcast.36, ...), custom_call_target="tpu_custom_call", output_to_operand_aliasing={{0}: (10, {}), {1}: (11, {})} | custom-call | tf_op jit(solution)/shard_map/pallas_call | solution.py:261
  67.8 0.0 all-to-all-done.1
  67.8 0.0 copy-done.5
  67.8 0.0 copy-done.9
  67.9 0.0 copy-done.14
  67.9 0.0 copy-done.16
  67.9 0.0 copy-done.17
  67.9 0.0 copy-done.20
  67.9 0.0 copy-done.23
  67.9 15.5 %shard_map.269 = (f32[2,32,64,128]{3,2,1,0:T(8,128)}, f32[32,64,128]{2,1,0:T(8,128)}, f32[1024,128]{1,0:T(8,128)S(1)}) custom-call(s32[32,128]{1,0:T(8,128)S(1)} %copy-done.8, f32[4,32,64,128]{3,2,1,0:T(8,128)} %get-tuple-element.29.adv_ref, f32[32,64,128]{2,1,0:T(8,128)} %get-tuple-element.30.spread_ref, f32[5,64,32,128]{3,2,1,0:T(8,128)} %w_field_ref.1, ...), custom_call_target="tpu_custom_call" | custom-call | tf_op jit(solution)/shard_map/pallas_call | solution.py:869
  83.4 0.8 copy-done.12
  84.3 5.7 %all-to-all-start.2 = ((f32[32,32,128]{2,1,0:T(8,128)}), f32[32,32,128]{2,1,0:T(8,128)S(1)}, u32[]{:S(2)}, u32[]{:S(2)}) async-start(f32[32,32,128]{2,1,0:T(8,128)} %bitcast.23), calls=%async_computation.2 | async-start | bytes 1048576 | tf_op jit(solution)/shard_map/all_to_all | solution.py:634
  89.9 5.4 %shard_map.271.rest_1_ = f32[5,64,32,128]{3,2,1,0:T(8,128)} custom-call(f32[4,32,64,128]{3,2,1,0:T(8,128)} %get-tuple-element.29.adv_ref, f32[2,32,64,128]{3,2,1,0:T(8,128)} %get-tuple-element.32.mixed_ref, f32[32,64,128]{2,1,0:T(8,128)} %get-tuple-element.31.refs_7_.after_ref.coef_ref), custom_call_target="tpu_custom_call" | custom-call | tf_op jit(solution)/shard_map/pallas_call | solution.py:921
  95.4 0.0 copy-start.21
  95.4 0.0 copy-start.22
  95.4 9.6 %shard_map.270.rest_0_.w_ref = f32[1,32,64,128]{3,2,1,0:T(8,128)} custom-call(s32[32,128]{1,0:T(8,128)S(1)} %copy-done.8, f32[5,2048,128]{2,1,0:T(8,128)} %bitcast.38, f32[5,2048,128]{2,1,0:T(8,128)} %bitcast.39, f32[5,2048,128]{2,1,0:T(8,128)} %bitcast.40, f32[3,88,128]{2,1,0:T(8,128)S(1)} %collective-permute-done.rest_0_.refs_4_.refs_3_, ...), custom_call_target="tpu_custom_call" | custom-call | tf_op jit(solution)/shard_map/pallas_call | solution.py:261
  104.9 0.5 all-to-all-done.2
  105.5 0.0 copy-done.3
  105.5 0.0 copy-done.10
  105.5 0.0 copy-done.15
  105.5 0.0 copy-done.21
  105.5 0.0 copy-done.22
  105.5 0.0 copy-start.2
  105.5 3.2 %shard_map.272 = f32[1024,128]{1,0:T(8,128)S(1)} custom-call(s32[1]{0:T(128)} %bitcast.1.device_ref, f32[1024,128]{1,0:T(8,128)S(1)} %bitcast.18, f32[64,10,128]{2,1,0:T(8,128)S(1)} %copy-done.3, f32[64,8,512]{2,1,0:T(8,128)} %constant.50.clone.along_ref, f32[16,16]{1,0:T(8,128)S(1)} %copy-done.21, bf16[2,512,512]{2,1,0:T(8,128)(2,1)} %constant.52.clone.forward_ref, ...), custom_call_target="tpu_custom_call" | custom-call | tf_op jit(solution)/shard_map/pallas_call | solution.py:647
  108.8 20.7 %all_to_all.44 = f32[32,32,128]{2,1,0:T(8,128)S(1)} all-to-all(f32[32,32,128]{2,1,0:T(8,128)S(1)} %bitcast.20), channel_id=1, replica_groups=mesh['rows'=4,'cols'=8] {'rows','cols'}, dimensions={0} | all-to-all | bytes 1048576 | tf_op jit(solution)/shard_map/all_to_all | solution.py:634
  129.4 4.8 %shard_map.273 = (f32[2048,128]{1,0:T(8,128)}, f32[5,2048,128]{2,1,0:T(8,128)}, f32[256,256]{1,0:T(8,128)}, f32[1,256]{1,0:T(1,128)}, f32[63,256]{1,0:T(8,128)}) custom-call(s32[32,128]{1,0:T(8,128)S(1)} %copy-done.8, f32[1,32,64,128]{3,2,1,0:T(8,128)S(1)} %copy-done.2, f32[5,2048,128]{2,1,0:T(8,128)} %bitcast.42, ...), custom_call_target="tpu_custom_call", output_to_operand_aliasing={{1}: (2, {})} | custom-call | tf_op jit(solution)/shard_map/pallas_call | solution.py:970
  (12 shorter events, 0.0 us)
Async XLA Ops:
  0.6 16.4 %copy-start.6 = (bf16[512,256]{1,0:T(8,128)(2,1)S(1)}, bf16[512,256]{1,0:T(8,128)(2,1)}, u32[]{:S(2)}) copy-start(bf16[512,256]{1,0:T(8,128)(2,1)} %constant.47.clone.y_ref) | copy-start | bytes 786436
  0.6 16.4 %copy-start.11 = (bf16[256,256]{1,0:T(8,128)(2,1)S(1)}, bf16[256,256]{1,0:T(8,128)(2,1)}, u32[]{:S(2)}) copy-start(bf16[256,256]{1,0:T(8,128)(2,1)} %constant.46.clone.x_ref) | copy-start | bytes 393220
  0.7 16.4 %copy-start.13 = (f32[64,128]{1,0:T(8,128)S(1)}, f32[64,128]{1,0:T(8,128)}, u32[]{:S(2)}) copy-start(f32[64,128]{1,0:T(8,128)} %constant.45.clone.base_ref) | copy-start | bytes 98308
  0.7 16.4 %copy-start.18 = (bf16[128,64]{1,0:T(8,128)(2,1)S(1)}, bf16[128,64]{1,0:T(8,128)(2,1)}, u32[]{:S(2)}) copy-start(bf16[128,64]{1,0:T(8,128)(2,1)} %constant.44.clone.z_ref) | copy-start | bytes 49156
  0.7 22.5 %copy-start.19 = (bf16[128,128]{1,0:T(8,128)(2,1)S(1)}, bf16[128,128]{1,0:T(8,128)(2,1)}, u32[]{:S(2)}) copy-start(bf16[128,128]{1,0:T(8,128)(2,1)} %constant.48.clone.take_ref) | copy-start | bytes 98308
  7.7 24.1 %collective-permute-start.2 = (f32[968,128]{1,0:T(8,128)}, f32[968,128]{1,0:T(8,128)S(1)}, u32[]{:S(2)}, u32[]{:S(2)}) collective-permute-start(f32[968,128]{1,0:T(8,128)} %get-tuple-element.25), channel_id=1, source_target_pairs={{0,1},{1,2},{2,3},{3,4},{4,5},{5,6},{6,7},{8,9},{9,10},{10,11},{11... | collective-permute-start | bytes 1486856 | tf_op jit(solution)/shard_map/ppermute | solution.py:296
  10.1 21.7 %collective-permute-start.3 = (f32[968,128]{1,0:T(8,128)}, f32[968,128]{1,0:T(8,128)S(1)}, u32[]{:S(2)}, u32[]{:S(2)}) collective-permute-start(f32[968,128]{1,0:T(8,128)} %get-tuple-element.26), channel_id=1, source_target_pairs={{1,0},{2,1},{3,2},{4,3},{5,4},{6,5},{7,6},{9,8},{10,9},{11,10},{12... | collective-permute-start | bytes 1486856 | tf_op jit(solution)/shard_map/ppermute | solution.py:296
  11.4 9.7 %collective-permute-start = (f32[3,88,128]{2,1,0:T(8,128)}, f32[3,88,128]{2,1,0:T(8,128)S(1)}, u32[]{:S(2)}, u32[]{:S(2)}) collective-permute-start(f32[3,88,128]{2,1,0:T(8,128)} %get-tuple-element.23), channel_id=1, source_target_pairs={{0,8},{8,16},{16,24},{1,9},{9,17},{17,25},{2,10},{10,18},{18,26},{... | collective-permute-start | bytes 405512 | tf_op jit(solution)/shard_map/ppermute | solution.py:296
  15.8 7.4 %collective-permute-start.1 = (f32[3,88,128]{2,1,0:T(8,128)}, f32[3,88,128]{2,1,0:T(8,128)S(1)}, u32[]{:S(2)}, u32[]{:S(2)}) collective-permute-start(f32[3,88,128]{2,1,0:T(8,128)} %get-tuple-element.24), channel_id=1, source_target_pairs={{8,0},{16,8},{24,16},{9,1},{17,9},{25,17},{10,2},{18,10},{26,18},{... | collective-permute-start | bytes 405512 | tf_op jit(solution)/shard_map/ppermute | solution.py:296
  17.1 0.7 copy-start.7
  17.8 14.0 %copy-start.8 = (s32[32,128]{1,0:T(8,128)S(1)}, s32[32,128]{1,0:T(8,128)}, u32[]{:S(2)}) copy-start(s32[32,128]{1,0:T(8,128)} %get-tuple-element.22.dep_ref) | copy-start | bytes 49156
  21.2 22.9 %copy-start = (f32[32,64,128]{2,1,0:T(8,128)}, f32[32,64,128]{2,1,0:T(8,128)S(1)}, u32[]{:S(2)}) copy-start(f32[32,64,128]{2,1,0:T(8,128)S(1)} %shard_map.264.coef_ref.back_coef_ref) | copy-start | bytes 3145732
  24.4 19.7 %all-to-all-start = ((f32[32,8,128]{2,1,0:T(8,128)}), f32[32,8,128]{2,1,0:T(8,128)S(1)}, u32[]{:S(2)}, u32[]{:S(2)}) async-start(f32[32,8,128]{2,1,0:T(8,128)} %bitcast.3), calls=%async_computation | async-start | bytes 262144 | tf_op jit(solution)/shard_map/all_to_all | solution.py:634
  44.1 0.7 copy-start.24
  48.5 19.3 %all-to-all-start.1 = ((f32[32,8,128]{2,1,0:T(8,128)}), f32[32,8,128]{2,1,0:T(8,128)S(1)}, u32[]{:S(2)}, u32[]{:S(2)}) async-start(f32[32,8,128]{2,1,0:T(8,128)} %bitcast.21), calls=%async_computation.1 | async-start | bytes 262144 | tf_op jit(solution)/shard_map/all_to_all | solution.py:634
  54.5 0.9 copy-start.4
  55.5 12.4 %copy-start.5 = (bf16[512,256]{1,0:T(8,128)(2,1)S(1)}, bf16[512,256]{1,0:T(8,128)(2,1)}, u32[]{:S(2)}) copy-start(bf16[512,256]{1,0:T(8,128)(2,1)} %constant.57.clone.y_back_ref.y_ref) | copy-start | bytes 786436
  55.5 12.4 %copy-start.9 = (bf16[256,256]{1,0:T(8,128)(2,1)S(1)}, bf16[256,256]{1,0:T(8,128)(2,1)}, u32[]{:S(2)}) copy-start(bf16[256,256]{1,0:T(8,128)(2,1)} %constant.58.clone.x_back_ref.x_ref) | copy-start | bytes 393220
  55.5 12.4 %copy-start.14 = (bf16[256,128]{1,0:T(8,128)(2,1)S(1)}, bf16[256,128]{1,0:T(8,128)(2,1)}, u32[]{:S(2)}) copy-start(bf16[256,128]{1,0:T(8,128)(2,1)} %constant.60.clone.give_ref) | copy-start | bytes 196612
  55.5 12.4 %copy-start.16 = (bf16[256,256]{1,0:T(8,128)(2,1)S(1)}, bf16[256,256]{1,0:T(8,128)(2,1)}, u32[]{:S(2)}) copy-start(bf16[256,256]{1,0:T(8,128)(2,1)} %w_in_ref.1) | copy-start | bytes 393220
  55.5 12.4 %copy-start.17 = (bf16[128,64]{1,0:T(8,128)(2,1)S(1)}, bf16[128,64]{1,0:T(8,128)(2,1)}, u32[]{:S(2)}) copy-start(bf16[128,64]{1,0:T(8,128)(2,1)} %constant.59.clone.z_back_ref.z_ref) | copy-start | bytes 49156
  55.5 12.4 %copy-start.20 = (bf16[256,63]{0,1:T(8,128)(2,1)S(1)}, bf16[256,63]{0,1:T(8,128)(2,1)}, u32[]{:S(2)}) copy-start(bf16[256,63]{0,1:T(8,128)(2,1)} %param.30) | copy-start | bytes 96772
  55.5 12.4 %copy-start.23 = (f32[256]{0:T(256)S(1)}, f32[256]{0:T(256)}, u32[]{:S(2)}) copy-start(f32[256]{0:T(256)} %param.29) | copy-start | bytes 3076
  83.4 0.8 copy-start.12
  84.3 21.2 %all-to-all-start.2 = ((f32[32,32,128]{2,1,0:T(8,128)}), f32[32,32,128]{2,1,0:T(8,128)S(1)}, u32[]{:S(2)}, u32[]{:S(2)}) async-start(f32[32,32,128]{2,1,0:T(8,128)} %bitcast.23), calls=%async_computation.2 | async-start | bytes 1048576 | tf_op jit(solution)/shard_map/all_to_all | solution.py:634
  95.4 10.1 %copy-start.3 = (f32[64,10,128]{2,1,0:T(8,128)S(1)}, f32[64,10,128]{2,1,0:T(8,128)}, u32[]{:S(2)}) copy-start(f32[64,10,128]{2,1,0:T(8,128)} %constant.49.clone.cross_ref) | copy-start | bytes 983044
  95.4 10.1 %copy-start.10 = (f32[2,128,128]{2,1,0:T(8,128)S(1)}, f32[2,128,128]{2,1,0:T(8,128)}, u32[]{:S(2)}) copy-start(f32[2,128,128]{2,1,0:T(8,128)} %constant.55.clone.column_ref) | copy-start | bytes 393220
  95.4 10.1 %copy-start.15 = (f32[3,32,128]{2,1,0:T(8,128)S(1)}, f32[3,32,128]{2,1,0:T(8,128)}, u32[]{:S(2)}) copy-start(f32[3,32,128]{2,1,0:T(8,128)} %constant.54.clone.strip_ref) | copy-start | bytes 147460
  95.4 10.1 %copy-start.21 = (f32[16,16]{1,0:T(8,128)S(1)}, f32[16,16]{1,0:T(8,128)}, u32[]{:S(2)}) copy-start(f32[16,16]{1,0:T(8,128)} %constant.51.clone.sines_ref) | copy-start | bytes 3076
  95.4 10.1 %copy-start.22 = (f32[8,128]{1,0:T(8,128)S(1)}, f32[8,128]{1,0:T(8,128)}, u32[]{:S(2)}) copy-start(f32[8,128]{1,0:T(8,128)} %constant.56.clone.lines_ref) | copy-start | bytes 12292
  105.5 23.9 %copy-start.1 = (f32[32,64,128]{2,1,0:T(8,128)S(1)}, f32[32,64,128]{2,1,0:T(8,128)}, u32[]{:S(2)}) copy-start(f32[32,64,128]{2,1,0:T(8,128)} %get-tuple-element.31.refs_7_.after_ref.coef_ref) | copy-start | bytes 3145732
  105.5 23.9 %copy-start.2 = (f32[1,32,64,128]{3,2,1,0:T(8,128)S(1)}, f32[1,32,64,128]{3,2,1,0:T(8,128)}, u32[]{:S(2)}) copy-start(f32[1,32,64,128]{3,2,1,0:T(8,128)} %shard_map.270.rest_0_.w_ref) | copy-start | bytes 3145732
